TPU v7x, 32 devices: a whole 2x2x4 slice. The times are simulated.
32 devices in a mesh: band: 2 (over x), patch: 16 (over z, y, core).
Axes of the slice: x: 2, y: 2, z: 4, core: 2. Of those that a mesh axis runs over, the one named last changes fastest.
Arguments:
- grid_feat: bfloat16 [8192, 474], P(('band', 'patch')), may hold values from -6 to 6
- enc_sender: int32 [12288], P(('band', 'patch')), may hold values from 0 to 255
- enc_patch: int32 [12288, 1], P(('band', 'patch')), may hold values from 0 to 15; in each aligned block of 384 rows (0 to 383, 384 to 767, ...) at most 32 rows name the same one
- enc_node: int32 [12288], P(('band', 'patch')), may hold values from 0 to 319
- enc_geo: bfloat16 [4, 12288], P(None, ('band', 'patch')), may hold values from -6 to 6
- mesh_nodes: bfloat16 [5120, 512], P('patch'), may hold values from -6 to 6
- mesh_edge: bfloat16 [8192, 512], P(('band', 'patch')), may hold values from -6 to 6
- mesh_send: int32 [8192], P(('band', 'patch')), may hold values from 0 to 575
- mesh_recv: int32 [8192], P(('band', 'patch')), may hold values from 0 to 319
- halo_rows: int32 [16, 256], P('patch'), may hold values from 0 to 319
- grid_in: bfloat16 [474, 512], replicated, may hold values from -0.25 to 0.25
- grid_out: bfloat16 [512, 512], replicated, may hold values from -0.25 to 0.25
- geo_weight: bfloat16 [4, 512], replicated, may hold values from -3 to 3
- enc_edge_w: bfloat16 [3, 512, 512], replicated, may hold values from -0.25 to 0.25
- enc_node_w: bfloat16 [3, 512, 512], replicated, may hold values from -0.25 to 0.25
- proc_edge_w: bfloat16 [4, 512, 512], replicated, may hold values from -0.25 to 0.25
- proc_node_w: bfloat16 [3, 512, 512], replicated, may hold values from -0.25 to 0.25
Outputs:
- mesh_two: bfloat16 [5120, 512], P('patch')
- edge_out: bfloat16 [8192, 512], P(('band', 'patch'))
Inputs may be any that keep to these rules, and one draw needn't show every extreme that they name: `enc_sender`: row among the 256 grid rows of the device that holds the edge. `enc_patch`: among the 384 edge rows of one device no patch is named more than 32 times; some patch exactly 32 times. `halo_rows`: row q holds, in blocks of 16, the rows of patch q sent to patches 0, 1,.
All inputs are finite; a program needn't handle non-finite values.
Results may differ from a plain program's by a relative error of at most 0.017.
Values may be sent and summed in bfloat16 or wider, within the bound.
No kernel may reach another device: no remote copies, remote signals or barrier semaphores. Data moves between devices by JAX's collectives and lax.ppermute only.
A program may use at most 64 MiB of HBM per device.

v0:
```python
import jax
import jax.numpy as jnp
from jax import lax
from jax.sharding import PartitionSpec as P


def norm_rows(values_in):
    average = jnp.mean(values_in, axis=-1, keepdims=True)
    centred = values_in - average
    spread = jnp.mean(centred * centred, axis=-1, keepdims=True)
    return centred * lax.rsqrt(spread + 1e-05)


def network_tail(preact, out_weight):
    hidden = jax.nn.silu(preact).astype(jnp.bfloat16)
    return norm_rows(jnp.dot(hidden, out_weight, preferred_element_type=jnp.float32))


def update_rows(node_rows, running, weights):
    preact = jnp.dot(node_rows, weights[0], preferred_element_type=jnp.float32) + jnp.dot(
        running.astype(jnp.bfloat16), weights[1], preferred_element_type=jnp.float32
    )
    return (node_rows.astype(jnp.float32) + network_tail(preact, weights[2])).astype(jnp.bfloat16)


def node_update(node_rows, partial_value, weights):
    share_rows = lax.psum_scatter(
        partial_value.astype(jnp.bfloat16), "band", scatter_dimension=0, tiled=True
    ).astype(jnp.float32)
    row_count = share_rows.shape[0]
    first_row = lax.axis_index("band") * row_count
    own_rows = lax.dynamic_slice_in_dim(node_rows, first_row, row_count, 0)
    updated = update_rows(own_rows, share_rows, weights)
    return lax.all_gather(updated, "band", axis=0, tiled=True)


def per_device(
    grid_feat,
    enc_sender,
    enc_patch,
    enc_node,
    enc_geo,
    mesh_nodes,
    mesh_edge,
    mesh_send,
    mesh_recv,
    halo_rows,
    grid_in,
    grid_out,
    geo_weight,
    enc_edge_w,
    enc_node_w,
    proc_edge_w,
    proc_node_w,
):
    peer_count = lax.axis_size("patch")
    latent_width = mesh_nodes.shape[1]
    mesh_count = mesh_nodes.shape[0]
    edge_count = enc_sender.shape[0]
    capacity = 4 * edge_count // (3 * peer_count)
    hidden = jax.nn.silu(jnp.dot(grid_feat, grid_in, preferred_element_type=jnp.float32)).astype(
        jnp.bfloat16
    )
    grid_lat = norm_rows(jnp.dot(hidden, grid_out, preferred_element_type=jnp.float32)).astype(
        jnp.bfloat16
    )
    sender_proj = jnp.dot(grid_lat, enc_edge_w[0], preferred_element_type=jnp.float32)
    geo_term = lax.dot_general(
        enc_geo, geo_weight, (((0,), (0,)), ((), ())), preferred_element_type=jnp.float32
    )
    send_term = (sender_proj[enc_sender] + geo_term).astype(jnp.bfloat16)
    target = enc_patch[:, 0]
    onehot = (target[:, None] == jnp.arange(peer_count, dtype=jnp.int32)[None, :]).astype(jnp.int32)
    slot_index = jnp.sum((jnp.cumsum(onehot, axis=0) - 1) * onehot, axis=1)
    outbox = (
        jnp.zeros((peer_count, capacity, latent_width), jnp.bfloat16)
        .at[target, slot_index]
        .set(send_term)
    )
    addresses = (
        jnp.full((peer_count, capacity), mesh_count, jnp.int32).at[target, slot_index].set(enc_node)
    )
    recv_proj = jnp.dot(mesh_nodes, enc_edge_w[1], preferred_element_type=jnp.float32)
    sender_terms = lax.all_to_all(outbox, "patch", split_axis=0, concat_axis=0, tiled=True)
    places = lax.all_to_all(addresses, "patch", split_axis=0, concat_axis=0, tiled=True)
    preact = sender_terms.astype(jnp.float32) + recv_proj[jnp.minimum(places, mesh_count - 1)]
    messages, places = (network_tail(preact, enc_edge_w[2]), places)
    partial_value = (
        jnp.zeros((mesh_count, latent_width), jnp.float32)
        .at[places.reshape(-1)]
        .add(messages.reshape(-1, latent_width), mode="drop")
    )
    mesh_one = node_update(mesh_nodes, partial_value, enc_node_w)
    sent_proj = jnp.dot(mesh_one, proc_edge_w[1], preferred_element_type=jnp.float32).astype(
        jnp.bfloat16
    )
    recv_two = jnp.dot(mesh_one, proc_edge_w[2], preferred_element_type=jnp.float32)
    outgoing = sent_proj[halo_rows[0]].reshape(peer_count, -1, latent_width)
    ghosts = lax.all_to_all(outgoing, "patch", split_axis=0, concat_axis=0, tiled=True)
    lookup = jnp.concatenate([sent_proj, ghosts.reshape(-1, latent_width)], axis=0)
    preact = (
        jnp.dot(mesh_edge, proc_edge_w[0], preferred_element_type=jnp.float32)
        + lookup[mesh_send].astype(jnp.float32)
        + recv_two[mesh_recv]
    )
    edge_new = mesh_edge.astype(jnp.float32) + network_tail(preact, proc_edge_w[3])
    partial_two = jnp.zeros((mesh_count, latent_width), jnp.float32).at[mesh_recv].add(edge_new)
    mesh_two = node_update(mesh_one, partial_two, proc_node_w)
    return (mesh_two, edge_new.astype(jnp.bfloat16))


def solution(mesh):
    in_specs = (
        P(("band", "patch"), None),
        P(("band", "patch")),
        P(("band", "patch"), None),
        P(("band", "patch")),
        P(None, ("band", "patch")),
        P("patch", None),
        P(("band", "patch"), None),
        P(("band", "patch")),
        P(("band", "patch")),
        P("patch", None),
        P(),
        P(),
        P(),
        P(),
        P(),
        P(),
        P(),
    )
    out_specs = (P("patch", None), P(("band", "patch"), None))
    return jax.shard_map(
        per_device, mesh=mesh, in_specs=in_specs, out_specs=out_specs, check_vma=False
    )
```

profile of v0, /device:TPU:0, one launch (start us, length us, event | category | flops | bytes accessed | tf_op | source)
XLA Modules:
  0.0 226.3 jit_solution(14767564303968868727)
XLA Ops:
  7.9 0.9 reduce-window.6
  10.5 54.0 %scatter_fusion = s32[16,32]{1,0:T(8,128)} fusion(s32[16,32]{1,0:T(8,128)} %broadcast.226, s32[384]{0:T(512)S(1)} %fusion.71, s32[384]{0:T(512)} %param.20), kind=kCustom, calls=%fused_computation.5 | custom fusion | bytes 7680 | tf_op jit(solution)/shard_map/scatter | solution.py:81
  64.5 7.1 %all-to-all-start = ((s32[16,1,32]{2,1,0:T(1,128)}), s32[16,1,32]{2,1,0:T(1,128)S(1)}, u32[]{:S(2)}, u32[]{:S(2)}) async-start(s32[16,1,32]{2,1,0:T(1,128)} %bitcast.3), calls=%async_computation | async-start | bytes 16384 | tf_op jit(solution)/shard_map/all_to_all | solution.py:85
  72.6 1.4 fusion.20
  74.0 1.6 gather_fusion
  76.0 0.8 broadcast_in_dim.8
  76.8 49.8 %scatter_fusion.1 = bf16[16,32,512]{2,1,0:T(8,128)(2,1)} fusion(bf16[16,32,512]{2,1,0:T(8,128)(2,1)} %broadcast_in_dim.8, s32[384]{0:T(512)S(1)} %fusion.71, bf16[384,512]{1,0:T(8,128)(2,1)S(1)} %fusion), kind=kCustom, calls=%fused_computation.6 | custom fusion | bytes 1182720 | tf_op jit(solution)/shard_map/scatter | solution.py:78
  126.7 6.0 %all-to-all-start.1 = ((bf16[16,32,512]{2,1,0:T(8,128)(2,1)}), bf16[16,32,512]{2,1,0:T(8,128)(2,1)S(1)}, u32[]{:S(2)}, u32[]{:S(2)}) async-start(bf16[16,32,512]{2,1,0:T(8,128)(2,1)} %scatter_fusion.1), calls=%async_computation.1 | async-start | bytes 1048576 | tf_op jit(solution)/shard_map/all_to_all | solution.py:84
  132.7 1.4 fusion.18
  135.5 1.6 gather_fusion.1
  137.1 10.0 %all-to-all-done.1 = bf16[16,32,512]{2,1,0:T(8,128)(2,1)S(1)} async-done(((bf16[16,32,512]{2,1,0:T(8,128)(2,1)}), bf16[16,32,512]{2,1,0:T(8,128)(2,1)S(1)}, u32[]{:S(2)}, u32[]{:S(2)}) %all-to-all-start.1) | async-done | bytes 524320 | tf_op jit(solution)/shard_map/all_to_all | solution.py:84
  147.2 1.6 fusion.80
  149.3 3.7 %scatter_custom_fusion.2 = f32[320,512]{1,0:T(8,128)S(1)} fusion(s32[512]{0:T(512)S(1)} %bitcast.115, f32[512,512]{1,0:T(8,128)S(1)} %bitcast.108, f32[]{:T(128)} %constant.26.clone.1), kind=kCustom, calls=%fused_computation.70 | custom fusion | flops 262144 | bytes 655364 | tf_op jit(solution)/shard_map/scatter-add | solution.py:91
  153.0 0.8 convert_element_type.70
  153.9 1.3 fusion.22
  155.2 10.9 %reduce-scatter.3.cloned.1.call-done = bf16[160,512]{1,0:T(8,128)(2,1)} async-done(((bf16[320,512]{1,0:T(8,128)(2,1)}), bf16[160,512]{1,0:T(8,128)(2,1)}) %reduce-scatter.3.cloned.1.call-update) | async-done | bytes 163856 | tf_op jit(solution)/shard_map/reduce_scatter | solution.py:27
  166.1 1.8 fusion.81
  168.3 6.6 %all_gather.6 = bf16[320,512]{1,0:T(8,128)(2,1)S(1)} all-gather(bf16[160,512]{1,0:T(8,128)(2,1)S(1)} %add_convert_fusion.1), channel_id=1, replica_groups=mesh['band'=2,'patch'=16] {'band'}, dimensions={0}, use_global_device_ids=true | all-gather | bytes 491520 | tf_op jit(solution)/shard_map/all_gather | solution.py:34
  174.9 1.4 convolution_convert_fusion
  176.3 1.9 gather_fusion.2
  178.1 5.6 %all-to-all-start.2 = ((bf16[16,16,512]{2,1,0:T(8,128)(2,1)}), bf16[16,16,512]{2,1,0:T(8,128)(2,1)S(1)}, u32[]{:S(2)}, u32[]{:S(2)}) async-start(bf16[16,16,512]{2,1,0:T(8,128)(2,1)} %bitcast.19), calls=%async_computation.3 | async-start | bytes 524288 | tf_op jit(solution)/shard_map/all_to_all | solution.py:99
  184.1 1.4 fusion.7
  185.4 1.0 gather_fusion.4
  186.4 7.4 %all-to-all-done.2 = bf16[16,16,512]{2,1,0:T(8,128)(2,1)S(1)} async-done(((bf16[16,16,512]{2,1,0:T(8,128)(2,1)}), bf16[16,16,512]{2,1,0:T(8,128)(2,1)S(1)}, u32[]{:S(2)}, u32[]{:S(2)}) %all-to-all-start.2) | async-done | bytes 262176 | tf_op jit(solution)/shard_map/all_to_all | solution.py:99
  193.9 1.2 gather_fusion.3
  195.0 1.9 fusion.84
  197.1 2.4 %scatter_custom_fusion.3 = f32[320,512]{1,0:T(8,128)S(1)} fusion(s32[256]{0:T(256)S(1)} %compare_select_fusion.7, f32[]{:T(128)} %constant.26.clone.1, bf16[256,512]{1,0:T(8,128)(2,1)S(1)} %copy-done.2, f32[256,512]{1,0:T(8,128)S(1)} %get-tuple-element.11, f32[256]{0:T(256)S(1)} %add_rsqrt_fusion.2, f32[256]{0:T(256)S(1)} %broadcast_multiply_fusion.3), kind=kCustom, calls=%fused_computation.68 | custom fusion | flops 655360 | bytes 1443844 | tf_op jit(solution)/shard_map/scatter-add | solution.py:107
  200.3 1.4 fusion.11
  201.7 0.9 fusion.55
  202.6 7.6 %reduce-scatter.5.cloned.1.call-done = bf16[160,512]{1,0:T(8,128)(2,1)} async-done(((bf16[320,512]{1,0:T(8,128)(2,1)}), bf16[160,512]{1,0:T(8,128)(2,1)}) %reduce-scatter.5.cloned.1.call-update) | async-done | bytes 163856 | tf_op jit(solution)/shard_map/reduce_scatter | solution.py:27
  210.2 1.5 fusion.87
  212.1 6.6 %all_gather.7 = bf16[320,512]{1,0:T(8,128)(2,1)S(1)} all-gather(bf16[160,512]{1,0:T(8,128)(2,1)S(1)} %add_convert_fusion), channel_id=1, replica_groups=mesh['band'=2,'patch'=16] {'band'}, dimensions={0}, use_global_device_ids=true | all-gather | bytes 491520 | tf_op jit(solution)/shard_map/all_gather | solution.py:34
  (74 shorter events, 8.3 us)
Async XLA Ops:
  7.2 64.4 %copy-start = (bf16[512,512]{1,0:T(8,128)(2,1)S(1)}, bf16[512,512]{1,0:T(8,128)(2,1)}, u32[]{:S(2)}) copy-start(bf16[512,512]{1,0:T(8,128)(2,1)} %param.28) | copy-start | bytes 1572868
  10.5 61.1 %copy-start.10 = (bf16[474,512]{1,0:T(8,128)(2,1)S(1)}, bf16[474,512]{1,0:T(8,128)(2,1)}, u32[]{:S(2)}) copy-start(bf16[474,512]{1,0:T(8,128)(2,1)} %param.27) | copy-start | bytes 1456132
  10.5 61.1 %copy-start.11 = (bf16[256,474]{0,1:T(8,128)(2,1)S(1)}, bf16[256,474]{0,1:T(8,128)(2,1)}, u32[]{:S(2)}) copy-start(bf16[256,474]{0,1:T(8,128)(2,1)} %param.17) | copy-start | bytes 728068
  64.5 62.2 %all-to-all-start = ((s32[16,1,32]{2,1,0:T(1,128)}), s32[16,1,32]{2,1,0:T(1,128)S(1)}, u32[]{:S(2)}, u32[]{:S(2)}) async-start(s32[16,1,32]{2,1,0:T(1,128)} %bitcast.3), calls=%async_computation | async-start | bytes 16384 | tf_op jit(solution)/shard_map/all_to_all | solution.py:85
  71.6 0.9 copy-start.6
  74.0 1.7 copy-start.4
  74.0 1.7 copy-start.5
  76.8 55.9 %copy-start.1 = (bf16[320,512]{1,0:T(8,128)(2,1)S(1)}, bf16[320,512]{1,0:T(8,128)(2,1)}, u32[]{:S(2)}) copy-start(bf16[320,512]{1,0:T(8,128)(2,1)} %param.22) | copy-start | bytes 983044
  126.7 20.5 %all-to-all-start.1 = ((bf16[16,32,512]{2,1,0:T(8,128)(2,1)}), bf16[16,32,512]{2,1,0:T(8,128)(2,1)S(1)}, u32[]{:S(2)}, u32[]{:S(2)}) async-start(bf16[16,32,512]{2,1,0:T(8,128)(2,1)} %scatter_fusion.1), calls=%async_computation.1 | async-start | bytes 1048576 | tf_op jit(solution)/shard_map/all_to_all | solution.py:84
  132.7 33.4 %reduce-scatter.3.cloned.1.call-start = ((), (), s32[]{:S(2)}) async-start(), calls=%async_computation.5 | async-start | bytes 491520 | tf_op jit(solution)/shard_map/reduce_scatter | solution.py:27
  149.0 4.8 %copy-start.7 = (s32[1,256]{1,0:T(1,128)S(1)}, s32[1,256]{1,0:T(1,128)}, u32[]{:S(2)}) copy-start(s32[1,256]{1,0:T(1,128)} %param.26) | copy-start | bytes 3076
  149.0 4.8 %copy-start.8 = (s32[256]{0:T(256)S(1)}, s32[256]{0:T(256)}, u32[]{:S(2)}) copy-start(s32[256]{0:T(256)} %param.24) | copy-start | bytes 3076
  176.3 7.7 %copy-start.9 = (s32[256]{0:T(256)S(1)}, s32[256]{0:T(256)}, u32[]{:S(2)}) copy-start(s32[256]{0:T(256)} %param.25) | copy-start | bytes 3076
  178.1 15.7 %all-to-all-start.2 = ((bf16[16,16,512]{2,1,0:T(8,128)(2,1)}), bf16[16,16,512]{2,1,0:T(8,128)(2,1)S(1)}, u32[]{:S(2)}, u32[]{:S(2)}) async-start(bf16[16,16,512]{2,1,0:T(8,128)(2,1)} %bitcast.19), calls=%async_computation.3 | async-start | bytes 524288 | tf_op jit(solution)/shard_map/all_to_all | solution.py:99
  183.8 26.5 %reduce-scatter.5.cloned.1.call-start = ((), (), s32[]{:S(2)}) async-start(), calls=%async_computation.6 | async-start | bytes 491520 | tf_op jit(solution)/shard_map/reduce_scatter | solution.py:27
  193.8 1.2 copy-start.2
  200.3 9.9 %copy-start.3 = (bf16[3,512,512]{2,1,0:T(8,128)(2,1)S(1)}, bf16[3,512,512]{2,1,0:T(8,128)(2,1)}, u32[]{:S(2)}) copy-start(bf16[3,512,512]{2,1,0:T(8,128)(2,1)} %param.33) | copy-start | bytes 4718596
Sparse Core Ops, SparseCore 0:
  153.9 12.1 reduce-scatter.2
  200.4 9.7 reduce-scatter.4
where the time goes:
time: 230 us; the launch traced here: 226 us
  local copies, waits for them, and re-layouts  114 us (50%)
  waiting for transfers between devices  36 us (16%)
  starting transfers between devices  19 us (8%)
  matrix products  16 us (7%)
  between operations  14.5 us (6%)
  other arithmetic  13.4 us (6%)
  blocking collectives  13.2 us (6%)
    scatter x1, local copies, waits for them, and re-layouts, per_device(): jnp.full((peer_count, capacity), mesh_count, jnp.int32)  54 us
    scatter x1, local copies, waits for them, and re-layouts, per_device(): outbox = jnp.zeros((peer_count, capacity, latent_width), jnp.bfloat16).at...  49.8 us
    reduce_scatter x2, waiting for transfers between devices, node_update(): lax.psum_scatter(partial_value.astype(jnp.bfloat16), 'band', scatter_dime...  18.5 us
    all_gather x2, blocking collectives, node_update(): return lax.all_gather(updated, 'band', axis=0, tiled=True)  13.2 us
    all_to_all x1, waiting for transfers between devices, per_device(): lax.all_to_all(outbox, 'patch', split_axis=0, concat_axis=0, tiled=True)  10 us
    all_to_all x1, waiting for transfers between devices, per_device(): lax.all_to_all(outgoing, 'patch', split_axis=0, concat_axis=0, tiled=True)  7.42 us
    all_to_all x1, starting transfers between devices, per_device(): lax.all_to_all(addresses, 'patch', split_axis=0, concat_axis=0, tiled=True)  7.08 us
    dot_general x4, matrix products, network_tail(): jnp.dot(hidden, out_weight, preferred_element_type=jnp.float32)  6.79 us
  transfers between devices with their start and end apart: 5, of which 4 were waited for; matrix products, arithmetic and copies ran while one was open for 29% of the time, Pallas kernels for 0%

commit v1 on v0

v1 whole, which is shorter than its diff:
```python
import functools

import jax
import jax.numpy as jnp
from jax import lax
from jax.experimental import pallas as pl
from jax.experimental.pallas import tpu as pltpu
from jax.sharding import PartitionSpec as P

F32 = jnp.float32
BF16 = jnp.bfloat16
LANES = 128
RADIX = 32


def dot_nn(left, right):
    return jnp.dot(left, right, preferred_element_type=F32)


def dot_nt(left, right):
    return lax.dot_general(left, right, (((1,), (1,)), ((), ())), preferred_element_type=F32)


def dot_tn(left, right):
    return lax.dot_general(left, right, (((0,), (0,)), ((), ())), preferred_element_type=F32)


def as_onehot(hits):
    return jnp.where(hits, 1.0, 0.0).astype(BF16)


def rows_equal(row_count, names):
    rows = lax.broadcasted_iota(jnp.int32, (row_count, names.shape[1]), 0)
    return as_onehot(rows == names)


def norm_rows(values_in):
    average = jnp.mean(values_in, axis=-1, keepdims=True)
    centred = values_in - average
    spread = jnp.mean(centred * centred, axis=-1, keepdims=True)
    return centred * lax.rsqrt(spread + 1e-05)


def silu(values_in):
    return values_in * jax.nn.sigmoid(values_in)


def tail(preact, out_weight):
    return norm_rows(dot_nn(silu(preact).astype(BF16), out_weight))


def embed_kernel(
    feat_ref, sender_ref, patch_ref, node_ref, geo_ref, in_ref, out_ref, geo_w_ref, edge_w_ref, box_ref
):
    peers, box_rows, _ = box_ref.shape
    edges = sender_ref.shape[1]
    grid_rows = feat_ref.shape[1]
    pieces = edge_w_ref.shape[2] // LANES
    capacity = 4 * edges // (3 * peers)
    slots = peers * capacity
    me = lax.axis_index("patch")
    patch = patch_ref[...]
    named = lax.broadcasted_iota(jnp.int32, (peers, edges), 0) == patch
    named_f = jnp.where(named, 1.0, 0.0)
    earlier = as_onehot(
        lax.broadcasted_iota(jnp.int32, (edges, edges), 0)
        < lax.broadcasted_iota(jnp.int32, (edges, edges), 1)
    )
    before = dot_nn(named_f.astype(BF16), earlier)
    rank = jnp.sum(named_f * before, axis=0, keepdims=True).astype(jnp.int32)
    place = rows_equal(slots, patch * capacity + rank)
    source = rows_equal(grid_rows, sender_ref[...])
    pick = dot_nt(place, source).astype(BF16)
    geo = dot_nt(place, geo_ref[...]).astype(BF16)

    hidden = silu(dot_tn(feat_ref[...], in_ref[...])).astype(BF16)
    latent = norm_rows(dot_nn(hidden, out_ref[...])).astype(BF16)
    rows = dot_nn(pick, latent).astype(BF16)
    term = dot_nn(rows, edge_w_ref[0]) + dot_nn(geo, geo_w_ref[...])
    for piece in range(pieces):
        box_ref[:, piece * capacity : (piece + 1) * capacity, :] = (
            term[:, piece * LANES : (piece + 1) * LANES].reshape(peers, capacity, LANES).astype(BF16)
        )

    address = node_ref[...] + 1
    first = me * capacity
    lane = rows_equal(LANES, rank + lax.rem(first, LANES))
    high = dot_nt((named_f * (address // RADIX).astype(F32)).astype(BF16), lane)
    low = dot_nt((named_f * lax.rem(address, RADIX).astype(F32)).astype(BF16), lane)
    extra = box_rows - pieces * capacity
    row = lax.broadcasted_iota(jnp.int32, (peers, extra, LANES), 1)
    mine = first // LANES
    words = jnp.where(
        row == mine,
        high[:, None, :],
        jnp.where(row == extra // 2 + mine, low[:, None, :], 0.0),
    )
    box_ref[:, pieces * capacity :, :] = words.astype(BF16)


def shadow_kernel(node_ref, halo_ref, edge_w_ref, node_w_ref, recv_ref, pre_ref, halo_hot_ref):
    nodes = node_ref[...]
    recv_ref[...] = dot_nn(nodes, edge_w_ref[0]).astype(BF16)
    pre_ref[...] = dot_nn(nodes, node_w_ref[0])
    halo_hot_ref[...] = rows_equal(nodes.shape[0], halo_ref[...]).T


def edge_shadow_kernel(*refs, count):
    edge_refs, send_refs, recv_refs = refs[:count], refs[count : 2 * count], refs[2 * count : 3 * count]
    edge_w_ref, edges_ref, pre_ref, ends_ref, far_ref, target_ref = refs[3 * count :]
    size = edge_refs[0].shape[0]
    mesh_rows = target_ref.shape[0]
    far_rows = far_ref.shape[1]
    for part in range(count):
        rows = slice(part * size, (part + 1) * size)
        if count == 2:
            keep = lax.axis_index("band") == part
            edges = jnp.where(keep, edge_refs[0][...], edge_refs[1][...])
            send = jnp.where(keep, send_refs[0][...], send_refs[1][...])
            recv = jnp.where(keep, recv_refs[0][...], recv_refs[1][...])
        else:
            edges, send, recv = edge_refs[0][...], send_refs[0][...], recv_refs[0][...]
        edges_ref[rows, :] = edges
        pre_ref[rows, :] = dot_nn(edges, edge_w_ref[0])
        receiver = rows_equal(mesh_rows, recv)
        target_ref[:, rows] = receiver
        near = rows_equal(mesh_rows, send)
        far = rows_equal(far_rows, send - mesh_rows)
        ends_ref[rows, :mesh_rows] = near.T
        ends_ref[rows, mesh_rows:] = receiver.T
        far_ref[rows, :] = far.T


def message_kernel(box_ref, recv_ref, out_w_ref, total_ref, *, capacity):
    peers = box_ref.shape[0]
    mesh_rows, width = recv_ref.shape
    pieces = width // LANES
    words = jnp.sum(box_ref[:, pieces * capacity :, :].astype(F32), axis=0)
    half = words.shape[0] // 2
    slots = peers * capacity
    hot = []
    for group in range(slots // LANES):
        name = words[group : group + 1] * float(RADIX) + words[half + group : half + group + 1] - 1.0
        hot.append(rows_equal(mesh_rows, name.astype(jnp.int32)))
    hot = jnp.concatenate(hot, axis=1)
    terms = jnp.concatenate(
        [
            box_ref[:, piece * capacity : (piece + 1) * capacity, :].astype(F32).reshape(slots, LANES)
            for piece in range(pieces)
        ],
        axis=1,
    )
    message = tail(terms + dot_tn(hot, recv_ref[...]), out_w_ref[0])
    total_ref[...] = dot_nn(hot, message.astype(BF16)).astype(BF16)


def add_up(refs):
    total = refs[0][...].astype(F32)
    for ref in refs[1:]:
        total = total + ref[...].astype(F32)
    return total.astype(BF16)


def mesh_kernel(*refs, count):
    total = add_up(refs[:count])
    node_ref, pre_ref, sum_w_ref, out_w_ref, sent_w_ref, halo_hot_ref, one_ref, box_ref = refs[count:]
    preact = pre_ref[...] + dot_nn(total, sum_w_ref[0])
    one = (node_ref[...].astype(F32) + tail(preact, out_w_ref[0])).astype(BF16)
    one_ref[...] = one
    rows = dot_nn(halo_hot_ref[...], one).astype(BF16)
    box_ref[...] = dot_nn(rows, sent_w_ref[0]).astype(BF16)


def local_kernel(one_ref, pre_ref, ends_ref, sent_w_ref, recv_w_ref, node_w_ref, out_ref, node_pre_ref):
    one = one_ref[...]
    sent = dot_nn(one, sent_w_ref[0]).astype(BF16)
    recv = dot_nn(one, recv_w_ref[0]).astype(BF16)
    out_ref[...] = pre_ref[...] + dot_nn(ends_ref[...], jnp.concatenate([sent, recv], axis=0))
    node_pre_ref[...] = dot_nn(one, node_w_ref[0])


def edge_values(ghost_ref, far_ref, pre_ref, edges_ref, out_w_ref):
    preact = pre_ref[...] + dot_nn(far_ref[...], ghost_ref[...])
    return edges_ref[...].astype(F32) + tail(preact, out_w_ref[0])


def node_values(total, one_ref, node_pre_ref, sum_w_ref, out_w_ref):
    preact = node_pre_ref[...] + dot_nn(total, sum_w_ref[0])
    return (one_ref[...].astype(F32) + tail(preact, out_w_ref[0])).astype(BF16)


def edge_node_kernel(
    ghost_ref, far_ref, pre_ref, edges_ref, edge_w_ref, target_ref,
    one_ref, node_pre_ref, sum_w_ref, out_w_ref, edge_out_ref, two_ref, held_ref,
):
    held_ref[...] = edge_values(ghost_ref, far_ref, pre_ref, edges_ref, edge_w_ref).astype(BF16)
    size = edge_out_ref.shape[0]
    first = pl.multiple_of(lax.axis_index("band") * size, size)
    edge_out_ref[...] = held_ref[pl.ds(first, size), :]
    total = dot_nn(target_ref[...], held_ref[...]).astype(BF16)
    two_ref[...] = node_values(total, one_ref, node_pre_ref, sum_w_ref, out_w_ref)


def edge_kernel(ghost_ref, far_ref, pre_ref, edges_ref, edge_w_ref, target_ref, edge_out_ref, total_ref):
    held = edge_values(ghost_ref, far_ref, pre_ref, edges_ref, edge_w_ref).astype(BF16)
    edge_out_ref[...] = held
    total_ref[...] = dot_nn(target_ref[...], held).astype(BF16)


def node_kernel(total_ref, one_ref, node_pre_ref, sum_w_ref, out_w_ref, two_ref):
    two_ref[...] = node_values(total_ref[...], one_ref, node_pre_ref, sum_w_ref, out_w_ref)


def call(kernel, outs, operands, flops, scratch=()):
    specs, arrays, moved = [], [], 0
    for operand in operands:
        if isinstance(operand, tuple):
            array, index = operand
            block = (1,) + array.shape[1:]
            specs.append(pl.BlockSpec(block, lambda i, index=index: (index, 0, 0)))
            moved += array.size // array.shape[0] * 2
        else:
            array = operand
            specs.append(pl.BlockSpec(array.shape, lambda i, rank=array.ndim: (0,) * rank))
            moved += array.size * array.dtype.itemsize
        arrays.append(array)
    return pl.pallas_call(
        kernel,
        grid=(1,),
        in_specs=specs,
        out_specs=[pl.BlockSpec(o.shape, lambda i, rank=len(o.shape): (0,) * rank) for o in outs],
        out_shape=outs,
        scratch_shapes=scratch,
        compiler_params=pltpu.CompilerParams(vmem_limit_bytes=32 * 1024 * 1024),
        cost_estimate=pl.CostEstimate(flops=flops, bytes_accessed=moved, transcendentals=0),
    )(*arrays)


def shape(dims, dtype=BF16):
    return jax.ShapeDtypeStruct(dims, dtype)


def per_device(
    grid_feat,
    enc_sender,
    enc_patch,
    enc_node,
    enc_geo,
    mesh_nodes,
    mesh_edge,
    mesh_send,
    mesh_recv,
    halo_rows,
    grid_in,
    grid_out,
    geo_weight,
    enc_edge_w,
    enc_node_w,
    proc_edge_w,
    proc_node_w,
):
    bands, peers = lax.axis_size("band"), lax.axis_size("patch")
    mesh_count, width = mesh_nodes.shape
    edge_count, medge_count = enc_sender.shape[0], mesh_edge.shape[0]
    halo_count = halo_rows.shape[1]
    capacity = 4 * edge_count // (3 * peers)
    slots = peers * capacity
    pieces = width // LANES
    address_rows = 2 * (slots // LANES)
    paired = bands == 2
    other = [(0, 1), (1, 0)]
    unit = 2 * width * width

    def band_sum(partial_value):
        share = lax.psum_scatter(partial_value, "band", scatter_dimension=0, tiled=True)
        return lax.all_gather(share, "band", axis=0, tiled=True)

    send_row, recv_row = mesh_send.reshape(1, -1), mesh_recv.reshape(1, -1)
    edge_parts, send_parts, recv_parts = [mesh_edge], [send_row], [recv_row]
    if paired:
        edge_parts.append(lax.ppermute(mesh_edge, "band", other))
        names = lax.ppermute(jnp.concatenate([send_row, recv_row], axis=0), "band", other)
        send_parts.append(names[0:1])
        recv_parts.append(names[1:2])
    count = len(edge_parts)
    edge_total = count * medge_count

    (outbox,) = call(
        embed_kernel,
        [shape((peers, pieces * capacity + address_rows, LANES))],
        [
            grid_feat.T,
            enc_sender.reshape(1, -1),
            enc_patch.reshape(1, -1),
            enc_node.reshape(1, -1),
            enc_geo,
            grid_in,
            grid_out,
            geo_weight,
            (enc_edge_w, 0),
        ],
        unit * 1500,
    )
    inbox = lax.all_to_all(outbox, "patch", split_axis=0, concat_axis=0, tiled=True)

    recv_proj, node_pre, halo_hot = call(
        shadow_kernel,
        [shape((mesh_count, width)), shape((mesh_count, width), F32), shape((halo_count, mesh_count))],
        [mesh_nodes, halo_rows, (enc_edge_w, 1), (enc_node_w, 0)],
        unit * 640,
    )
    edges, edge_pre, ends, far, target = call(
        functools.partial(edge_shadow_kernel, count=count),
        [
            shape((edge_total, width)),
            shape((edge_total, width), F32),
            shape((edge_total, 2 * mesh_count)),
            shape((edge_total, halo_count)),
            shape((mesh_count, edge_total)),
        ],
        edge_parts + send_parts + recv_parts + [(proc_edge_w, 0)],
        unit * edge_total,
    )

    (partial_value,) = call(
        functools.partial(message_kernel, capacity=capacity),
        [shape((mesh_count, width))],
        [inbox, recv_proj, (enc_edge_w, 2)],
        unit * 1200,
    )
    if paired:
        totals = [partial_value, lax.ppermute(partial_value, "band", other)]
    else:
        totals = [band_sum(partial_value)]
    mesh_one, halo_box = call(
        functools.partial(mesh_kernel, count=len(totals)),
        [shape((mesh_count, width)), shape((halo_count, width))],
        totals
        + [mesh_nodes, node_pre, (enc_node_w, 1), (enc_node_w, 2), (proc_edge_w, 1), halo_hot],
        unit * 1000,
    )
    ghosts = lax.all_to_all(
        halo_box.reshape(peers, -1, width), "patch", split_axis=0, concat_axis=0, tiled=True
    ).reshape(halo_count, width)
    edge_pre, node_pre = call(
        local_kernel,
        [shape((edge_total, width), F32), shape((mesh_count, width), F32)],
        [mesh_one, edge_pre, ends, (proc_edge_w, 1), (proc_edge_w, 2), (proc_node_w, 0)],
        unit * 1500,
    )
    edge_operands = [ghosts, far, edge_pre, edges, (proc_edge_w, 3), target]
    node_operands = [mesh_one, node_pre, (proc_node_w, 1), (proc_node_w, 2)]
    if paired:
        edge_out, mesh_two = call(
            edge_node_kernel,
            [shape((medge_count, width)), shape((mesh_count, width))],
            edge_operands + node_operands,
            unit * 1500,
            scratch=[pltpu.VMEM((edge_total, width), BF16)],
        )
    else:
        edge_out, partial_two = call(
            edge_kernel,
            [shape((medge_count, width)), shape((mesh_count, width))],
            edge_operands,
            unit * 800,
        )
        (mesh_two,) = call(
            node_kernel,
            [shape((mesh_count, width))],
            [band_sum(partial_two)] + node_operands,
            unit * 640,
        )
    return (mesh_two, edge_out)


def solution(mesh):
    both = ("band", "patch")
    in_specs = (
        P(both, None),
        P(both),
        P(both, None),
        P(both),
        P(None, both),
        P("patch", None),
        P(both, None),
        P(both),
        P(both),
        P("patch", None),
        P(),
        P(),
        P(),
        P(),
        P(),
        P(),
        P(),
    )
    out_specs = (P("patch", None), P(both, None))
    return jax.shard_map(
        per_device, mesh=mesh, in_specs=in_specs, out_specs=out_specs, check_vma=False
    )
```

time: 230 us -> 79.8 us (0.35); the launches traced: 226 us -> 78.8 us
  local copies, waits for them, and re-layouts: 114 us -> 25.1 us
  matrix products: 16 us -> 0 us
  between operations: 14.5 us -> 0.81 us
  other arithmetic: 13.4 us -> 0.01 us
  blocking collectives: 13.2 us -> 0 us
  Pallas kernels: 0 us -> 10.2 us
  waiting for transfers between devices: 36 us -> 27 us
  starting transfers between devices: 19 us -> 15.7 us
    scatter x2 -> x0, local copies, waits for them, and re-layouts: 104 us -> none  [the longest x1 54 us: per_device(): jnp.full((peer_count, capacity), mesh_count, jnp.int32)]
    unnamed x25 -> x70, local copies, waits for them, and re-layouts: 0.79 us -> 23.8 us
    reduce_scatter x2 -> x0, waiting for transfers between devices: 18.5 us -> none  [node_update(): lax.psum_scatter(partial_value.astype(jnp.bfloat16), 'band', scatter_dime...]
    dot_general x12 -> x0, matrix products: 16 us -> none  [the longest x4 6.79 us: network_tail(): jnp.dot(hidden, out_weight, preferred_element_type=jnp.float32)]
    ppermute x0 -> x3, waiting for transfers between devices: none -> 14.7 us  [the longest x1 8.13 us: per_device(): totals = [partial_value, lax.ppermute(partial_value, 'band', other)]]
    all_gather x2 -> x0, blocking collectives: 13.2 us -> none  [node_update(): return lax.all_gather(updated, 'band', axis=0, tiled=True)]
    pallas_call x0 -> x7, Pallas kernels: none -> 10.2 us  [call(): pl.pallas_call(kernel, grid=(1,), in_specs=specs, out_specs=[pl.BlockSpec...]
    all_to_all x2 -> x1, starting transfers between devices: 12.7 us -> 4.53 us  [per_device(): lax.all_to_all(halo_box.reshape(peers, -1, width), 'patch', split_axis=0,...]
  transfers between devices with their start and end apart: 5 -> 5, of which waited for: 4 -> 3; matrix products, arithmetic and copies ran while one was open for 29% -> 0% of each run, Pallas kernels for 0% -> 3%
where the time goes in v1:
time: 79.8 us; the launch traced here: 78.8 us
  waiting for transfers between devices  27 us (34%)
  local copies, waits for them, and re-layouts  25.1 us (31%)
  starting transfers between devices  15.7 us (20%)
  Pallas kernels  10.2 us (13%)
  between operations  0.81 us (1%)
    unnamed x70, local copies, waits for them, and re-layouts  23.8 us
    all_to_all x1, waiting for transfers between devices, per_device(): lax.all_to_all(outbox, 'patch', split_axis=0, concat_axis=0, tiled=True)  12.3 us
    pallas_call x7, Pallas kernels, call(): pl.pallas_call(kernel, grid=(1,), in_specs=specs, out_specs=[pl.BlockSpec...  10.2 us
    ppermute x1, waiting for transfers between devices, per_device(): totals = [partial_value, lax.ppermute(partial_value, 'band', other)]  8.13 us
    all_to_all x1, starting transfers between devices, per_device(): lax.all_to_all(outbox, 'patch', split_axis=0, concat_axis=0, tiled=True)  7.43 us
    ppermute x1, waiting for transfers between devices, per_device(): lax.ppermute(jnp.concatenate([send_row, recv_row], axis=0), 'band', other)  6.58 us
    all_to_all x1, starting transfers between devices, per_device(): lax.all_to_all(halo_box.reshape(peers, -1, width), 'patch', split_axis=0,...  4.53 us
  transfers between devices with their start and end apart: 5, of which 3 were waited for; matrix products, arithmetic and copies ran while one was open for 0% of the time, Pallas kernels for 3%

profile of v1, /device:TPU:0, one launch (start us, length us, event | category | flops | bytes accessed | tf_op | source)
XLA Modules:
  0.0 78.8 jit_solution(3612562866755715998)
XLA Ops:
  2.0 1.4 %copy-done.3 = bf16[3,512,512]{2,1,0:T(8,128)(2,1)S(1)} copy-done((bf16[3,512,512]{2,1,0:T(8,128)(2,1)S(1)}, bf16[3,512,512]{2,1,0:T(8,128)(2,1)}, u32[]{:S(2)}) %copy-start.3) | copy-done | bytes 1572888
  3.4 1.0 %copy-done.16 = bf16[512,512]{1,0:T(8,128)(2,1)S(1)} copy-done((bf16[512,512]{1,0:T(8,128)(2,1)S(1)}, bf16[512,512]{1,0:T(8,128)(2,1)}, u32[]{:S(2)}) %copy-start.16) | copy-done | bytes 524312
  4.4 1.0 %copy-done.17 = bf16[474,512]{1,0:T(8,128)(2,1)S(1)} copy-done((bf16[474,512]{1,0:T(8,128)(2,1)S(1)}, bf16[474,512]{1,0:T(8,128)(2,1)}, u32[]{:S(2)}) %copy-start.17) | copy-done | bytes 485400
  5.5 0.9 %copy-done.26 = bf16[256,474]{0,1:T(8,128)(2,1)S(1)} copy-done((bf16[256,474]{0,1:T(8,128)(2,1)S(1)}, bf16[256,474]{0,1:T(8,128)(2,1)}, u32[]{:S(2)}) %copy-start.26) | copy-done | bytes 242712
  8.5 1.8 %shard_map.176 = bf16[16,136,128]{2,1,0:T(8,128)(2,1)S(1)} custom-call(bf16[474,256]{1,0:T(8,128)(2,1)S(1)} %bitcast.8, s32[1,384]{1,0:T(1,128)S(1)} %reshape.25.sender_ref, s32[1,384]{1,0:T(1,128)S(1)} %bitcast.13, s32[1,384]{1,0:T(1,128)S(1)} %reshape.27.node_ref, bf16[4,384]{1,0:T(4,128)(2,1)S(1)} %copy-done.32, bf16[474,512]{1,0:T(8,128)(2,1)S(1)} %copy-done.17, ...), custom_call_target="tpu_custom_call" | custom-call | flops 786432000 | bytes 1788416 | tf_op jit(solution)/shard_map/pallas_call | solution.py:227
  10.3 0.8 %copy-done.8 = bf16[16,136,128]{2,1,0:T(8,128)(2,1)} copy-done((bf16[16,136,128]{2,1,0:T(8,128)(2,1)}, bf16[16,136,128]{2,1,0:T(8,128)(2,1)S(1)}, u32[]{:S(2)}) %copy-start.8) | copy-done | bytes 557080
  11.1 7.4 %all-to-all-start = ((bf16[16,136,128]{2,1,0:T(8,128)(2,1)}), bf16[16,136,128]{2,1,0:T(8,128)(2,1)}, u32[]{:S(2)}, u32[]{:S(2)}) async-start(bf16[16,136,128]{2,1,0:T(8,128)(2,1)} %copy-done.8), calls=%async_computation | async-start | bytes 1114112 | tf_op jit(solution)/shard_map/all_to_all | solution.py:304
  19.1 0.8 %copy-done.12 = f32[320,512]{1,0:T(8,128)} copy-done((f32[320,512]{1,0:T(8,128)}, f32[320,512]{1,0:T(8,128)S(1)}, u32[]{:S(2)}) %copy-start.12) | copy-done | bytes 655384
  19.9 0.7 copy-done.20
  21.3 12.3 %all-to-all-done.box_ref = bf16[16,136,128]{2,1,0:T(8,128)(2,1)} async-done(((bf16[16,136,128]{2,1,0:T(8,128)(2,1)}), bf16[16,136,128]{2,1,0:T(8,128)(2,1)}, u32[]{:S(2)}, u32[]{:S(2)}) %all-to-all-start) | async-done | bytes 557088 | tf_op jit(solution)/shard_map/all_to_all | solution.py:304
  33.6 1.4 %copy-done.5 = bf16[3,512,512]{2,1,0:T(8,128)(2,1)S(1)} copy-done((bf16[3,512,512]{2,1,0:T(8,128)(2,1)S(1)}, bf16[3,512,512]{2,1,0:T(8,128)(2,1)}, u32[]{:S(2)}) %copy-start.5) | copy-done | bytes 1572888
  35.0 1.0 %copy-done.21 = bf16[320,512]{1,0:T(8,128)(2,1)S(1)} copy-done((bf16[320,512]{1,0:T(8,128)(2,1)S(1)}, bf16[320,512]{1,0:T(8,128)(2,1)}, u32[]{:S(2)}) %copy-start.21) | copy-done | bytes 327704
  36.0 2.4 %shard_map.178.refs_0_ = bf16[320,512]{1,0:T(8,128)(2,1)S(1)} custom-call(bf16[16,136,128]{2,1,0:T(8,128)(2,1)} %all-to-all-done.box_ref, bf16[320,512]{1,0:T(8,128)(2,1)S(1)} %copy-done.21, bf16[3,512,512]{2,1,0:T(8,128)(2,1)S(1)} %copy-done.5), custom_call_target="tpu_custom_call" | custom-call | flops 629145600 | bytes 1409024 | tf_op jit(solution)/shard_map/pallas_call | solution.py:227
  38.5 1.6 %collective-permute-start = (bf16[320,512]{1,0:T(8,128)(2,1)S(1)}, bf16[320,512]{1,0:T(8,128)(2,1)S(1)}, u32[]{:S(2)}, u32[]{:S(2)}) collective-permute-start(bf16[320,512]{1,0:T(8,128)(2,1)S(1)} %shard_map.178.refs_0_), channel_id=1, source_target_pairs={{0,16},{16,0},{1,17},{17,1},{2,18},{18,2},{3,19},{19,3},{4,20},{20... | collective-permute-start | bytes 983048 | tf_op jit(solution)/shard_map/ppermute | solution.py:332
  40.0 8.1 %collective-permute-done.refs_1_ = bf16[320,512]{1,0:T(8,128)(2,1)S(1)} collective-permute-done((bf16[320,512]{1,0:T(8,128)(2,1)S(1)}, bf16[320,512]{1,0:T(8,128)(2,1)S(1)}, u32[]{:S(2)}, u32[]{:S(2)}) %collective-permute-start) | collective-permute-done | bytes 327712 | tf_op jit(solution)/shard_map/ppermute | solution.py:332
  48.2 1.4 %copy-done.2 = bf16[3,512,512]{2,1,0:T(8,128)(2,1)S(1)} copy-done((bf16[3,512,512]{2,1,0:T(8,128)(2,1)S(1)}, bf16[3,512,512]{2,1,0:T(8,128)(2,1)}, u32[]{:S(2)}) %copy-start.2) | copy-done | bytes 1572888
  49.6 0.9 %copy-done.28 = bf16[256,320]{1,0:T(8,128)(2,1)S(1)} copy-done((bf16[256,320]{1,0:T(8,128)(2,1)S(1)}, bf16[256,320]{1,0:T(8,128)(2,1)}, u32[]{:S(2)}) %copy-start.28) | copy-done | bytes 163864
  50.5 1.3 %shard_map.179 = (bf16[320,512]{1,0:T(8,128)(2,1)S(1)}, bf16[256,512]{1,0:T(8,128)(2,1)S(1)}) custom-call(bf16[320,512]{1,0:T(8,128)(2,1)S(1)} %shard_map.178.refs_0_, bf16[320,512]{1,0:T(8,128)(2,1)S(1)} %collective-permute-done.refs_1_, bf16[320,512]{1,0:T(8,128)(2,1)S(1)} %copy-done.9, f32[320,512]{1,0:T(8,128)S(1)} %copy-done.13, ...), custom_call_target="tpu_custom_call" | custom-call | flops 524288000 | bytes 3375104 | tf_op jit(solution)/shard_map/pallas_call | solution.py:227
  52.5 4.5 %all-to-all-start.1 = ((bf16[16,16,512]{2,1,0:T(8,128)(2,1)}), bf16[16,16,512]{2,1,0:T(8,128)(2,1)S(1)}, u32[]{:S(2)}, u32[]{:S(2)}) async-start(bf16[16,16,512]{2,1,0:T(8,128)(2,1)} %bitcast.7), calls=%async_computation.1 | async-start | bytes 524288 | tf_op jit(solution)/shard_map/all_to_all | solution.py:342
  57.0 1.6 %collective-permute-start.1 = (bf16[256,512]{1,0:T(8,128)(2,1)S(1)}, bf16[256,512]{1,0:T(8,128)(2,1)S(1)}, u32[]{:S(2)}, u32[]{:S(2)}) collective-permute-start(bf16[256,512]{1,0:T(8,128)(2,1)S(1)} %copy-done.22), channel_id=1, source_target_pairs={{0,16},{16,0},{1,17},{17,1},{2,18},{18,2},{3,19},{19,3},{4,20},{20... | collective-permute-start | bytes 786440 | tf_op jit(solution)/shard_map/ppermute | solution.py:281
  59.2 6.6 %collective-permute-done.2 = s32[2,256]{1,0:T(2,128)S(1)} collective-permute-done((s32[2,256]{1,0:T(2,128)S(1)}, s32[2,256]{1,0:T(2,128)S(1)}, u32[]{:S(2)}, u32[]{:S(2)}) %collective-permute-start.2) | collective-permute-done | bytes 2080 | tf_op jit(solution)/shard_map/ppermute | solution.py:282
  66.4 0.8 %copy-done.14 = bf16[512,512]{1,0:T(8,128)(2,1)} copy-done((bf16[512,512]{1,0:T(8,128)(2,1)}, bf16[512,512]{1,0:T(8,128)(2,1)S(1)}, u32[]{:S(2)}) %copy-start.14) | copy-done | bytes 524312
  67.2 0.7 copy-done.18
  67.9 0.7 copy-done.23
  68.6 1.1 %shard_map.181 = (f32[512,512]{1,0:T(8,128)S(1)}, f32[320,512]{1,0:T(8,128)S(1)}) custom-call(bf16[320,512]{1,0:T(8,128)(2,1)S(1)} %get-tuple-element.21.one_ref, f32[512,512]{1,0:T(8,128)S(1)} %get-tuple-element.22.pre_ref, bf16[512,640]{1,0:T(8,128)(2,1)S(1)} %get-tuple-element.23.ends_ref, bf16[4,512,512]{2,1,0:T(8,128)(2,1)S(1)} %copy-done, ...), custom_call_target="tpu_custom_call" | custom-call | flops 786432000 | bytes 3604480 | tf_op jit(solution)/shard_map/pallas_call | solution.py:227
  69.7 1.0 %copy-done.10 = f32[512,512]{1,0:T(8,128)} copy-done((f32[512,512]{1,0:T(8,128)}, f32[512,512]{1,0:T(8,128)S(1)}, u32[]{:S(2)}) %copy-start.10) | copy-done | bytes 1048600
  70.7 1.4 %copy-done.7 = bf16[3,512,512]{2,1,0:T(8,128)(2,1)S(1)} copy-done((bf16[3,512,512]{2,1,0:T(8,128)(2,1)S(1)}, bf16[3,512,512]{2,1,0:T(8,128)(2,1)}, u32[]{:S(2)}) %copy-start.7) | copy-done | bytes 1572888
  72.1 1.2 %copy-done.11 = f32[512,512]{1,0:T(8,128)S(1)} copy-done((f32[512,512]{1,0:T(8,128)S(1)}, f32[512,512]{1,0:T(8,128)}, u32[]{:S(2)}) %copy-start.11) | copy-done | bytes 1048600
  73.3 1.0 %copy-done.15 = bf16[512,512]{1,0:T(8,128)(2,1)S(1)} copy-done((bf16[512,512]{1,0:T(8,128)(2,1)S(1)}, bf16[512,512]{1,0:T(8,128)(2,1)}, u32[]{:S(2)}) %copy-start.15) | copy-done | bytes 524312
  74.4 1.0 %copy-done.19 = bf16[320,512]{1,0:T(8,128)(2,1)S(1)} copy-done((bf16[320,512]{1,0:T(8,128)(2,1)S(1)}, bf16[320,512]{1,0:T(8,128)(2,1)}, u32[]{:S(2)}) %copy-start.19) | copy-done | bytes 327704
  75.3 0.9 %copy-done.24 = bf16[512,256]{1,0:T(8,128)(2,1)S(1)} copy-done((bf16[512,256]{1,0:T(8,128)(2,1)S(1)}, bf16[512,256]{1,0:T(8,128)(2,1)}, u32[]{:S(2)}) %copy-start.24) | copy-done | bytes 262168
  76.3 2.6 %shard_map.182 = (bf16[256,512]{1,0:T(8,128)(2,1)}, bf16[320,512]{1,0:T(8,128)(2,1)}) custom-call(bf16[256,512]{1,0:T(8,128)(2,1)S(1)} %bitcast.6, bf16[512,256]{1,0:T(8,128)(2,1)S(1)} %copy-done.24, f32[512,512]{1,0:T(8,128)S(1)} %copy-done.11, bf16[512,512]{1,0:T(8,128)(2,1)S(1)} %copy-done.15, bf16[4,512,512]{2,1,0:T(8,128)(2,1)S(1)} %copy-done, ...), custom_call_target="tpu_custom_call" | custom-call | flops 786432000 | bytes 4980736 | tf_op jit(solution)/shard_map/pallas_call | solution.py:227
  (59 shorter events, 6.5 us)
Async XLA Ops:
  2.0 1.4 %copy-start.3 = (bf16[3,512,512]{2,1,0:T(8,128)(2,1)S(1)}, bf16[3,512,512]{2,1,0:T(8,128)(2,1)}, u32[]{:S(2)}) copy-start(bf16[3,512,512]{2,1,0:T(8,128)(2,1)} %out_w_ref.2) | copy-start | bytes 4718596
  3.4 1.0 %copy-start.16 = (bf16[512,512]{1,0:T(8,128)(2,1)S(1)}, bf16[512,512]{1,0:T(8,128)(2,1)}, u32[]{:S(2)}) copy-start(bf16[512,512]{1,0:T(8,128)(2,1)} %out_ref.1) | copy-start | bytes 1572868
  4.4 1.0 %copy-start.17 = (bf16[474,512]{1,0:T(8,128)(2,1)S(1)}, bf16[474,512]{1,0:T(8,128)(2,1)}, u32[]{:S(2)}) copy-start(bf16[474,512]{1,0:T(8,128)(2,1)} %in_ref.1) | copy-start | bytes 1456132
  5.5 0.9 %copy-start.26 = (bf16[256,474]{0,1:T(8,128)(2,1)S(1)}, bf16[256,474]{0,1:T(8,128)(2,1)}, u32[]{:S(2)}) copy-start(bf16[256,474]{0,1:T(8,128)(2,1)} %param.17) | copy-start | bytes 728068
  8.5 10.1 %copy-start.1 = (bf16[3,512,512]{2,1,0:T(8,128)(2,1)S(1)}, bf16[3,512,512]{2,1,0:T(8,128)(2,1)}, u32[]{:S(2)}) copy-start(bf16[3,512,512]{2,1,0:T(8,128)(2,1)} %refs_5_.1) | copy-start | bytes 4718596
  8.5 10.1 %copy-start.4 = (bf16[3,512,512]{2,1,0:T(8,128)(2,1)S(1)}, bf16[3,512,512]{2,1,0:T(8,128)(2,1)}, u32[]{:S(2)}) copy-start(bf16[3,512,512]{2,1,0:T(8,128)(2,1)} %out_w_ref.2) | copy-start | bytes 4718596
  8.5 10.1 %copy-start.9 = (bf16[320,512]{1,0:T(8,128)(2,1)S(1)}, bf16[320,512]{1,0:T(8,128)(2,1)}, u32[]{:S(2)}) copy-start(bf16[320,512]{1,0:T(8,128)(2,1)} %refs_2_.1) | copy-start | bytes 983044
  8.5 10.1 %copy-start.34 = (s32[1,256]{1,0:T(1,128)S(1)}, s32[1,256]{1,0:T(1,128)}, u32[]{:S(2)}) copy-start(s32[1,256]{1,0:T(1,128)} %halo_ref.1) | copy-start | bytes 3076
  10.3 0.8 %copy-start.8 = (bf16[16,136,128]{2,1,0:T(8,128)(2,1)}, bf16[16,136,128]{2,1,0:T(8,128)(2,1)S(1)}, u32[]{:S(2)}) copy-start(bf16[16,136,128]{2,1,0:T(8,128)(2,1)S(1)} %shard_map.176) | copy-start | bytes 1671172
  11.1 22.5 %all-to-all-start = ((bf16[16,136,128]{2,1,0:T(8,128)(2,1)}), bf16[16,136,128]{2,1,0:T(8,128)(2,1)}, u32[]{:S(2)}, u32[]{:S(2)}) async-start(bf16[16,136,128]{2,1,0:T(8,128)(2,1)} %copy-done.8), calls=%async_computation | async-start | bytes 1114112 | tf_op jit(solution)/shard_map/all_to_all | solution.py:304
  19.1 0.8 %copy-start.12 = (f32[320,512]{1,0:T(8,128)}, f32[320,512]{1,0:T(8,128)S(1)}, u32[]{:S(2)}) copy-start(f32[320,512]{1,0:T(8,128)S(1)} %get-tuple-element.17.refs_3_) | copy-start | bytes 1966084
  21.3 26.8 %copy-start = (bf16[4,512,512]{2,1,0:T(8,128)(2,1)S(1)}, bf16[4,512,512]{2,1,0:T(8,128)(2,1)}, u32[]{:S(2)}) copy-start(bf16[4,512,512]{2,1,0:T(8,128)(2,1)} %edge_w_ref.5) | copy-start | bytes 6291460
  33.6 1.4 %copy-start.5 = (bf16[3,512,512]{2,1,0:T(8,128)(2,1)S(1)}, bf16[3,512,512]{2,1,0:T(8,128)(2,1)}, u32[]{:S(2)}) copy-start(bf16[3,512,512]{2,1,0:T(8,128)(2,1)} %out_w_ref.2) | copy-start | bytes 4718596
  35.0 1.0 %copy-start.21 = (bf16[320,512]{1,0:T(8,128)(2,1)S(1)}, bf16[320,512]{1,0:T(8,128)(2,1)}, u32[]{:S(2)}) copy-start(bf16[320,512]{1,0:T(8,128)(2,1)} %copy-done.20) | copy-start | bytes 983044
  36.0 12.1 %copy-start.13 = (f32[320,512]{1,0:T(8,128)S(1)}, f32[320,512]{1,0:T(8,128)}, u32[]{:S(2)}) copy-start(f32[320,512]{1,0:T(8,128)} %copy-done.12) | copy-start | bytes 1966084
  38.5 9.7 %collective-permute-start = (bf16[320,512]{1,0:T(8,128)(2,1)S(1)}, bf16[320,512]{1,0:T(8,128)(2,1)S(1)}, u32[]{:S(2)}, u32[]{:S(2)}) collective-permute-start(bf16[320,512]{1,0:T(8,128)(2,1)S(1)} %shard_map.178.refs_0_), channel_id=1, source_target_pairs={{0,16},{16,0},{1,17},{17,1},{2,18},{18,2},{3,19},{19,3},{4,20},{20... | collective-permute-start | bytes 983048 | tf_op jit(solution)/shard_map/ppermute | solution.py:332
  48.2 1.4 %copy-start.2 = (bf16[3,512,512]{2,1,0:T(8,128)(2,1)S(1)}, bf16[3,512,512]{2,1,0:T(8,128)(2,1)}, u32[]{:S(2)}) copy-start(bf16[3,512,512]{2,1,0:T(8,128)(2,1)} %refs_5_.1) | copy-start | bytes 4718596
  49.6 0.9 %copy-start.28 = (bf16[256,320]{1,0:T(8,128)(2,1)S(1)}, bf16[256,320]{1,0:T(8,128)(2,1)}, u32[]{:S(2)}) copy-start(bf16[256,320]{1,0:T(8,128)(2,1)} %copy-done.27) | copy-start | bytes 491524
  50.5 6.5 %copy-start.22 = (bf16[256,512]{1,0:T(8,128)(2,1)S(1)}, bf16[256,512]{1,0:T(8,128)(2,1)}, u32[]{:S(2)}) copy-start(bf16[256,512]{1,0:T(8,128)(2,1)} %refs_0_.1) | copy-start | bytes 786436
  50.5 8.1 %copy-start.29 = (s32[256]{0:T(256)S(1)}, s32[256]{0:T(256)}, u32[]{:S(2)}) copy-start(s32[256]{0:T(256)} %param.24) | copy-start | bytes 3076
  50.5 8.1 %copy-start.30 = (s32[256]{0:T(256)S(1)}, s32[256]{0:T(256)}, u32[]{:S(2)}) copy-start(s32[256]{0:T(256)} %param.25) | copy-start | bytes 3076
  52.5 18.2 %all-to-all-start.1 = ((bf16[16,16,512]{2,1,0:T(8,128)(2,1)}), bf16[16,16,512]{2,1,0:T(8,128)(2,1)S(1)}, u32[]{:S(2)}, u32[]{:S(2)}) async-start(bf16[16,16,512]{2,1,0:T(8,128)(2,1)} %bitcast.7), calls=%async_computation.1 | async-start | bytes 524288 | tf_op jit(solution)/shard_map/all_to_all | solution.py:342
  57.0 11.6 %copy-start.6 = (bf16[3,512,512]{2,1,0:T(8,128)(2,1)S(1)}, bf16[3,512,512]{2,1,0:T(8,128)(2,1)}, u32[]{:S(2)}) copy-start(bf16[3,512,512]{2,1,0:T(8,128)(2,1)} %out_w_ref.3) | copy-start | bytes 4718596
  57.0 8.8 %collective-permute-start.1 = (bf16[256,512]{1,0:T(8,128)(2,1)S(1)}, bf16[256,512]{1,0:T(8,128)(2,1)S(1)}, u32[]{:S(2)}, u32[]{:S(2)}) collective-permute-start(bf16[256,512]{1,0:T(8,128)(2,1)S(1)} %copy-done.22), channel_id=1, source_target_pairs={{0,16},{16,0},{1,17},{17,1},{2,18},{18,2},{3,19},{19,3},{4,20},{20... | collective-permute-start | bytes 786440 | tf_op jit(solution)/shard_map/ppermute | solution.py:281
  58.6 7.2 %collective-permute-start.2 = (s32[2,256]{1,0:T(2,128)S(1)}, s32[2,256]{1,0:T(2,128)S(1)}, u32[]{:S(2)}, u32[]{:S(2)}) collective-permute-start(s32[2,256]{1,0:T(2,128)S(1)} %pad_add_fusion), channel_id=1, source_target_pairs={{0,16},{16,0},{1,17},{17,1},{2,18},{18,2},{3,19},{19,3},{4,20},{20... | collective-permute-start | bytes 6152 | tf_op jit(solution)/shard_map/ppermute | solution.py:282
  66.4 0.8 %copy-start.14 = (bf16[512,512]{1,0:T(8,128)(2,1)}, bf16[512,512]{1,0:T(8,128)(2,1)S(1)}, u32[]{:S(2)}) copy-start(bf16[512,512]{1,0:T(8,128)(2,1)S(1)} %get-tuple-element.25.edges_ref) | copy-start | bytes 1572868
  69.7 1.0 %copy-start.10 = (f32[512,512]{1,0:T(8,128)}, f32[512,512]{1,0:T(8,128)S(1)}, u32[]{:S(2)}) copy-start(f32[512,512]{1,0:T(8,128)S(1)} %get-tuple-element.24.pre_ref) | copy-start | bytes 3145732
  70.7 1.4 %copy-start.7 = (bf16[3,512,512]{2,1,0:T(8,128)(2,1)S(1)}, bf16[3,512,512]{2,1,0:T(8,128)(2,1)}, u32[]{:S(2)}) copy-start(bf16[3,512,512]{2,1,0:T(8,128)(2,1)} %out_w_ref.3) | copy-start | bytes 4718596
  72.1 1.2 %copy-start.11 = (f32[512,512]{1,0:T(8,128)S(1)}, f32[512,512]{1,0:T(8,128)}, u32[]{:S(2)}) copy-start(f32[512,512]{1,0:T(8,128)} %copy-done.10) | copy-start | bytes 3145732
  73.3 1.0 %copy-start.15 = (bf16[512,512]{1,0:T(8,128)(2,1)S(1)}, bf16[512,512]{1,0:T(8,128)(2,1)}, u32[]{:S(2)}) copy-start(bf16[512,512]{1,0:T(8,128)(2,1)} %copy-done.14) | copy-start | bytes 1572868
  74.4 1.0 %copy-start.19 = (bf16[320,512]{1,0:T(8,128)(2,1)S(1)}, bf16[320,512]{1,0:T(8,128)(2,1)}, u32[]{:S(2)}) copy-start(bf16[320,512]{1,0:T(8,128)(2,1)} %copy-done.18) | copy-start | bytes 983044
  75.3 0.9 %copy-start.24 = (bf16[512,256]{1,0:T(8,128)(2,1)S(1)}, bf16[512,256]{1,0:T(8,128)(2,1)}, u32[]{:S(2)}) copy-start(bf16[512,256]{1,0:T(8,128)(2,1)} %copy-done.23) | copy-start | bytes 786436
  (8 other events, 5.6 us)

commit v2 on v1

v2 whole, which is shorter than its diff:
```python
import functools
import math

import jax
import jax.numpy as jnp
from jax import lax
from jax.experimental import pallas as pl
from jax.experimental.pallas import tpu as pltpu
from jax.sharding import PartitionSpec as P

F32 = jnp.float32
BF16 = jnp.bfloat16
LANES = 128
RADIX = 32


def dot_nn(left, right):
    return jnp.dot(left, right, preferred_element_type=F32)


def dot_nt(left, right):
    return lax.dot_general(left, right, (((1,), (1,)), ((), ())), preferred_element_type=F32)


def dot_tn(left, right):
    return lax.dot_general(left, right, (((0,), (0,)), ((), ())), preferred_element_type=F32)


def as_onehot(hits):
    return jnp.where(hits, 1.0, 0.0).astype(BF16)


def rows_equal(row_count, names):
    rows = lax.broadcasted_iota(jnp.int32, (row_count, names.shape[1]), 0)
    return as_onehot(rows == names)


def norm_rows(values_in):
    average = jnp.mean(values_in, axis=-1, keepdims=True)
    centred = values_in - average
    spread = jnp.mean(centred * centred, axis=-1, keepdims=True)
    return centred * lax.rsqrt(spread + 1e-05)


def silu(values_in):
    return values_in * jax.nn.sigmoid(values_in)


def tail(preact, out_weight):
    return norm_rows(dot_nn(silu(preact).astype(BF16), out_weight))


class Arriving:
    def __init__(self, source, held, sem):
        self.held, self.copy, self.waited = held, pltpu.make_async_copy(source, held, sem), False
        self.copy.start()

    def ref(self):
        if not self.waited:
            self.copy.wait()
            self.waited = True
        return self.held

    def __call__(self):
        return self.ref()[...]


class Present:
    def __init__(self, held):
        self.held = held

    def ref(self):
        return self.held

    def __call__(self):
        return self.held[...]


class Leaving:
    def __init__(self, held, target=None, sems=None):
        self.held, self.target, self.sems, self.copies = held, target, sems, []
        self.shape = held.shape

    def send(self, first, count):
        if self.target is not None:
            rows = pl.ds(first, count)
            copy = pltpu.make_async_copy(
                self.held.at[rows], self.target.at[rows], self.sems.at[len(self.copies)]
            )
            copy.start()
            self.copies.append(copy)

    def put(self, value, first=0):
        self.held[first : first + value.shape[0]] = value
        self.send(first, value.shape[0])


class Far:
    def __init__(self, array, index=None, count=None):
        self.array, self.index, self.count = array, index, count
        self.shape = array.shape
        if index is not None:
            self.shape = array.shape[1:] if count is None else (count,) + array.shape[1:]

    def source(self, ref):
        if self.index is None:
            return ref
        return ref.at[self.index if self.count is None else pl.ds(self.index, self.count)]


PARTS = 4
BIG, MID, SMALL = 60, 48, 12


def call(body, outs, operands, flops, far_outs=False, room=SMALL):
    n_in, n_out = len(operands), len(outs)
    far_in = [isinstance(operand, Far) for operand in operands]
    arrays = [operand.array if away else operand for operand, away in zip(operands, far_in)]
    moved = sum(math.prod(o.shape) * a.dtype.itemsize for o, a in zip(operands, arrays))

    def kernel(*refs):
        given, results, scratch = refs[:n_in], refs[n_in : n_in + n_out], list(refs[n_in + n_out : -2])
        in_sems, out_sems = refs[-2:]
        arriving = []
        for i, (ref, operand) in enumerate(zip(given, operands)):
            if far_in[i]:
                arriving.append(Arriving(operand.source(ref), scratch.pop(0), in_sems.at[i]))
            else:
                arriving.append(Present(ref))
        leaving = []
        for i, ref in enumerate(results):
            if far_outs:
                leaving.append(Leaving(scratch.pop(0), ref, out_sems.at[pl.ds(i * PARTS, PARTS)]))
            else:
                leaving.append(Leaving(ref))
        body(arriving, leaving)
        for one in leaving:
            for copy in one.copies:
                copy.wait()

    here, away = pl.BlockSpec(memory_space=pltpu.VMEM), pl.BlockSpec(memory_space=pltpu.HBM)
    held = [pltpu.VMEM(o.shape, a.dtype) for o, a, is_far in zip(operands, arrays, far_in) if is_far]
    if far_outs:
        held += [pltpu.VMEM(o.shape, o.dtype) for o in outs]
    return pl.pallas_call(
        kernel,
        in_specs=[away if is_far else here for is_far in far_in],
        out_specs=[away if far_outs else here] * n_out,
        out_shape=outs,
        scratch_shapes=held
        + [pltpu.SemaphoreType.DMA((n_in,)), pltpu.SemaphoreType.DMA((n_out * PARTS,))],
        compiler_params=pltpu.CompilerParams(vmem_limit_bytes=room * 1024 * 1024),
        cost_estimate=pl.CostEstimate(flops=flops, bytes_accessed=moved, transcendentals=0),
    )(*arrays)


def as_row(block):
    return jnp.concatenate([block[i : i + 1] for i in range(block.shape[0])], axis=1)


def embed_body(arriving, leaving):
    patch, sender, geo, node, feat, in_w, out_w, edge_w, geo_w = arriving
    (box,) = leaving
    peers, box_rows, _ = box.shape
    edges = patch.held.shape[1]
    grid_rows = feat.held.shape[1]
    pieces = edge_w.held.shape[1] // LANES
    capacity = 4 * edges // (3 * peers)
    slots = peers * capacity
    me = lax.axis_index("patch")
    earlier = as_onehot(
        lax.broadcasted_iota(jnp.int32, (edges, edges), 0)
        < lax.broadcasted_iota(jnp.int32, (edges, edges), 1)
    )
    patch = patch()
    named = lax.broadcasted_iota(jnp.int32, (peers, edges), 0) == patch
    named_f = jnp.where(named, 1.0, 0.0)
    before = dot_nn(named_f.astype(BF16), earlier)
    rank = jnp.sum(named_f * before, axis=0, keepdims=True).astype(jnp.int32)
    place = rows_equal(slots, patch * capacity + rank)
    source = rows_equal(grid_rows, as_row(sender()))
    pick = dot_nt(place, source).astype(BF16)
    geo = dot_nt(place, geo()).astype(BF16)

    address = as_row(node()) + 1
    first = me * capacity
    lane = rows_equal(LANES, rank + lax.rem(first, LANES))
    high = dot_nt((named_f * (address // RADIX).astype(F32)).astype(BF16), lane)
    low = dot_nt((named_f * lax.rem(address, RADIX).astype(F32)).astype(BF16), lane)
    extra = box_rows - pieces * capacity
    row = lax.broadcasted_iota(jnp.int32, (peers, extra, LANES), 1)
    mine = first // LANES
    words = jnp.where(
        row == mine,
        high[:, None, :],
        jnp.where(row == extra // 2 + mine, low[:, None, :], 0.0),
    )
    box.held[:, pieces * capacity :, :] = words.astype(BF16)

    hidden = silu(dot_tn(feat(), in_w())).astype(BF16)
    latent = norm_rows(dot_nn(hidden, out_w())).astype(BF16)
    rows = dot_nn(pick, latent).astype(BF16)
    term = dot_nn(rows, edge_w()) + dot_nn(geo, geo_w())
    for piece in range(pieces):
        box.held[:, piece * capacity : (piece + 1) * capacity, :] = (
            term[:, piece * LANES : (piece + 1) * LANES].reshape(peers, capacity, LANES).astype(BF16)
        )
    box.send(0, peers)


def edge_shadow_body(arriving, leaving, *, count):
    edge_parts, names, edge_w = arriving[:count], arriving[count:-1], arriving[-1]
    edges_out, pre_out, ends_out, far_out, recv_out = leaving
    size = edge_parts[0].held.shape[0]
    mesh_rows = ends_out.shape[1] // 2
    far_rows = far_out.shape[1]
    for part in range(count):
        rows = slice(part * size, (part + 1) * size)
        if count == 2:
            keep = lax.axis_index("band") == part
            send = jnp.where(keep, names[0](), names[2]()[0:1])
            recv = jnp.where(keep, names[1](), names[2]()[1:2])
            edges = jnp.where(keep, edge_parts[0](), edge_parts[1]())
        else:
            send, recv, edges = names[0](), names[1](), edge_parts[0]()
        recv_out.held[:, rows] = recv
        far_out.put(rows_equal(far_rows, send - mesh_rows).T, rows.start)
        ends = [rows_equal(mesh_rows, send).T, rows_equal(mesh_rows, recv).T]
        ends_out.put(jnp.concatenate(ends, axis=1), rows.start)
        edges_out.put(edges, rows.start)
        pre_out.put(dot_nn(edges, edge_w()).astype(BF16), rows.start)
    recv_out.send(0, 1)


def bring_body(arriving, leaving):
    halo, nodes, recv_w, node_w, out_w, pair_w, sent_w = arriving
    message_out, node_pre_out, halo_out, nodes_out, pair_w_out, sent_w_out = leaving
    halo_out.put(rows_equal(nodes.held.shape[0], halo()).T)
    nodes_out.put(nodes())
    message_out.put(dot_nn(nodes(), recv_w()).astype(BF16))
    message_out.put(out_w(), nodes.held.shape[0])
    node_pre_out.put(dot_nn(nodes(), node_w()).astype(BF16))
    pair_w_out.put(pair_w())
    sent_w_out.put(sent_w())


def message_body(arriving, leaving, *, capacity):
    box, both = arriving
    (total,) = leaving
    mesh_rows, width = total.shape
    peers = box.held.shape[0]
    pieces = width // LANES
    box = box.ref()
    words = jnp.sum(box[:, pieces * capacity :, :].astype(F32), axis=0)
    half = words.shape[0] // 2
    slots = peers * capacity
    hot = []
    for group in range(slots // LANES):
        name = words[group : group + 1] * float(RADIX) + words[half + group : half + group + 1] - 1.0
        hot.append(rows_equal(mesh_rows, name.astype(jnp.int32)))
    hot = jnp.concatenate(hot, axis=1)
    terms = jnp.concatenate(
        [
            box[:, piece * capacity : (piece + 1) * capacity, :].astype(F32).reshape(slots, LANES)
            for piece in range(pieces)
        ],
        axis=1,
    )
    message = tail(terms + dot_tn(hot, both.ref()[:mesh_rows]), both.ref()[mesh_rows:]).astype(BF16)
    total.put(dot_nn(hot, message).astype(BF16))


def mesh_body(arriving, leaving, *, count):
    totals, (nodes, node_pre, pair_w, halo_hot, sent_w) = arriving[:count], arriving[count:]
    one_out, box_out = leaving
    total = totals[0]().astype(F32)
    for other in totals[1:]:
        total = total + other().astype(F32)
    preact = node_pre().astype(F32) + dot_nn(total.astype(BF16), pair_w.ref()[0])
    one = (nodes().astype(F32) + tail(preact, pair_w.ref()[1])).astype(BF16)
    one_out.put(one)
    rows = dot_nn(halo_hot(), one).astype(BF16)
    box_out.put(dot_nn(rows, sent_w()).astype(BF16))


def local_body(arriving, leaving):
    one, sent_w, recv_w, ends, pre, node_w = arriving
    pre_out, node_pre_out = leaving
    sent = dot_nn(one(), sent_w()).astype(BF16)
    recv = dot_nn(one(), recv_w()).astype(BF16)
    own = dot_nn(ends(), jnp.concatenate([sent, recv], axis=0))
    pre_out.put((pre().astype(F32) + own).astype(BF16))
    node_pre_out.put(dot_nn(one(), node_w()).astype(BF16))


def edge_values(arriving):
    far, ghosts, pre, edge_w, edges = arriving
    preact = pre().astype(F32) + dot_nn(far(), ghosts())
    return (edges().astype(F32) + tail(preact, edge_w())).astype(BF16)


def node_values(total, arriving):
    pair_w, node_pre, one = arriving
    preact = node_pre().astype(F32) + dot_nn(total, pair_w.ref()[0])
    return (one().astype(F32) + tail(preact, pair_w.ref()[1])).astype(BF16)


def edge_node_body(arriving, leaving):
    edge_out, two_out = leaving
    made = edge_values(arriving[:5])
    size = edge_out.shape[0]
    edge_out.put(jnp.where(lax.axis_index("band") == 0, made[:size], made[size:]))
    target = rows_equal(two_out.shape[0], arriving[5]())
    two_out.put(node_values(dot_nn(target, made).astype(BF16), arriving[6:]))


def edge_body(arriving, leaving):
    edge_out, total_out = leaving
    made = edge_values(arriving[:5])
    edge_out.put(made)
    total_out.put(dot_nn(rows_equal(total_out.shape[0], arriving[5]()), made).astype(BF16))


def node_body(arriving, leaving):
    leaving[0].put(node_values(arriving[0](), arriving[1:]))


def shape(dims, dtype=BF16):
    return jax.ShapeDtypeStruct(dims, dtype)


def per_device(
    grid_feat,
    enc_sender,
    enc_patch,
    enc_node,
    enc_geo,
    mesh_nodes,
    mesh_edge,
    mesh_send,
    mesh_recv,
    halo_rows,
    grid_in,
    grid_out,
    geo_weight,
    enc_edge_w,
    enc_node_w,
    proc_edge_w,
    proc_node_w,
):
    bands, peers = lax.axis_size("band"), lax.axis_size("patch")
    mesh_count, width = mesh_nodes.shape
    edge_count, medge_count = enc_sender.shape[0], mesh_edge.shape[0]
    halo_count = halo_rows.shape[1]
    capacity = 4 * edge_count // (3 * peers)
    slots = peers * capacity
    pieces = width // LANES
    address_rows = 2 * (slots // LANES)
    paired = bands == 2
    other = [(0, 1), (1, 0)]
    unit = 2 * width * width

    def band_sum(partial_value):
        share = lax.psum_scatter(partial_value, "band", scatter_dimension=0, tiled=True)
        return lax.all_gather(share, "band", axis=0, tiled=True)

    matrix, pair = shape((width, width)), shape((2, width, width))
    node_like, edge_like = shape((mesh_count, width)), shape((medge_count, width))
    sources = [
        enc_patch.reshape(1, -1),
        enc_sender.reshape(-1, LANES),
        enc_geo,
        enc_node.reshape(-1, LANES),
        grid_feat.T,
        grid_in,
        grid_out,
    ]
    (outbox,) = call(
        embed_body,
        [shape((peers, pieces * capacity + address_rows, LANES))],
        [Far(source) for source in sources] + [Far(enc_edge_w, 0), Far(geo_weight)],
        unit * 1500,
        far_outs=True,
        room=BIG,
    )
    inbox = lax.all_to_all(outbox, "patch", split_axis=0, concat_axis=0, tiled=True)

    send_row, recv_row = mesh_send.reshape(1, -1), mesh_recv.reshape(1, -1)
    edge_parts, names = [mesh_edge], [send_row, recv_row]
    if paired:
        own_edge, own_names, _ = lax.optimization_barrier(
            (mesh_edge, jnp.concatenate(names, axis=0), outbox)
        )
        edge_parts.append(lax.ppermute(own_edge, "band", other))
        names.append(lax.ppermute(own_names, "band", other))
    count = len(edge_parts)
    edge_total = count * medge_count
    nodes, _ = lax.optimization_barrier((mesh_nodes, outbox))
    message_pair, node_pre, halo_hot, nodes, node_w, sent_w = call(
        bring_body,
        [
            shape((mesh_count + width, width)),
            node_like,
            shape((halo_count, mesh_count)),
            node_like,
            pair,
            matrix,
        ],
        [
            Far(halo_rows),
            Far(nodes),
            Far(enc_edge_w, 1),
            Far(enc_node_w, 0),
            Far(enc_edge_w, 2),
            Far(enc_node_w, 1, 2),
            Far(proc_edge_w, 1),
        ],
        unit * 640,
        room=MID,
    )
    message_pair, edge_parts[-1], names[-1] = lax.optimization_barrier(
        (message_pair, edge_parts[-1], names[-1])
    )
    (partial_value,) = call(
        functools.partial(message_body, capacity=capacity),
        [node_like],
        [inbox, message_pair],
        unit * 1200,
    )
    names[0], partial_value = lax.optimization_barrier((names[0], partial_value))
    edges, edge_pre, ends, far, edge_recv = call(
        functools.partial(edge_shadow_body, count=count),
        [
            shape((edge_total, width)),
            shape((edge_total, width)),
            shape((edge_total, 2 * mesh_count)),
            shape((edge_total, halo_count)),
            shape((1, edge_total), jnp.int32),
        ],
        [Far(one) for one in edge_parts + names] + [Far(proc_edge_w, 0)],
        unit * edge_total,
        far_outs=True,
        room=MID,
    )
    if paired:
        totals = [partial_value, lax.ppermute(partial_value, "band", other)]
    else:
        totals = [band_sum(partial_value)]
    node_pre, edge_pre = lax.optimization_barrier((node_pre, edge_pre))
    mesh_one, halo_box = call(
        functools.partial(mesh_body, count=len(totals)),
        [node_like, shape((halo_count, width))],
        totals + [nodes, node_pre, node_w, halo_hot, sent_w],
        unit * 1000,
    )
    ghosts = lax.all_to_all(
        halo_box.reshape(peers, -1, width), "patch", split_axis=0, concat_axis=0, tiled=True
    ).reshape(halo_count, width)
    edge_whole = shape((edge_total, width))
    edge_pre, node_pre = call(
        local_body,
        [edge_whole, node_like],
        [mesh_one, sent_w, Far(proc_edge_w, 2), Far(ends), Far(edge_pre), Far(proc_node_w, 0)],
        unit * 1500,
        far_outs=True,
        room=MID,
    )
    edge_operands = [Far(far), Far(ghosts), Far(edge_pre), Far(proc_edge_w, 3), Far(edges), Far(edge_recv)]
    node_operands = [Far(proc_node_w, 1, 2), Far(node_pre), Far(mesh_one)]
    if paired:
        edge_out, mesh_two = call(
            edge_node_body,
            [edge_like, node_like],
            edge_operands + node_operands,
            unit * 1500,
            far_outs=True,
            room=BIG,
        )
    else:
        edge_out, partial_two = call(
            edge_body, [edge_like, node_like], edge_operands, unit * 800, far_outs=True, room=BIG
        )
        (mesh_two,) = call(
            node_body,
            [node_like],
            [Far(band_sum(partial_two))] + node_operands,
            unit * 640,
            far_outs=True,
            room=BIG,
        )
    return (mesh_two, edge_out)


def solution(mesh):
    both = ("band", "patch")
    in_specs = (
        P(both, None),
        P(both),
        P(both, None),
        P(both),
        P(None, both),
        P("patch", None),
        P(both, None),
        P(both),
        P(both),
        P("patch", None),
        P(),
        P(),
        P(),
        P(),
        P(),
        P(),
        P(),
    )
    out_specs = (P("patch", None), P(both, None))
    return jax.shard_map(
        per_device, mesh=mesh, in_specs=in_specs, out_specs=out_specs, check_vma=False
    )
```

time: 79.8 us -> 62.7 us (0.79)
  local copies, waits for them, and re-layouts: 25.1 us -> 10.1 us
  waiting for transfers between devices: 27 us -> 15.8 us
  Pallas kernels: 10.2 us -> 19.7 us
    unnamed x70 -> x58, local copies, waits for them, and re-layouts: 23.8 us -> 10.1 us
    pallas_call x7, Pallas kernels: 10.2 us -> 19.7 us  [call(): pl.pallas_call(kernel, in_specs=[away if is_far else here for is_far in f...]
    all_to_all x1, waiting for transfers between devices: 12.3 us -> 5.52 us  [per_device(): lax.all_to_all(outbox, 'patch', split_axis=0, concat_axis=0, tiled=True)]
    ppermute x2, waiting for transfers between devices: 6.58 us -> 0.65 us  [the longest x1 0.65 us: per_device(): names.append(lax.ppermute(own_names, 'band', other))]
    all_to_all x1, waiting for transfers between devices: 0.01 us -> 4.81 us  [per_device(): lax.all_to_all(halo_box.reshape(peers, -1, width), 'patch', split_axis=0,...]
    ppermute x1, waiting for transfers between devices: 8.13 us -> 4.81 us  [per_device(): totals = [partial_value, lax.ppermute(partial_value, 'band', other)]]
    reshape x2 -> x0, local copies, waits for them, and re-layouts: 1.37 us -> none  [the longest x1 0.68 us: per_device(): enc_sender.reshape(1, -1)]
  transfers between devices with their start and end apart: 5 -> 5, of which waited for: 3 -> 4; matrix products, arithmetic and copies ran while one was open for 0% -> 0% of each run, Pallas kernels for 3% -> 11%
where the time goes in v2:
time: 62.7 us; the launch traced here: 62.1 us
  Pallas kernels  19.7 us (31%)
  waiting for transfers between devices  15.8 us (25%)
  starting transfers between devices  15.6 us (25%)
  local copies, waits for them, and re-layouts  10.1 us (16%)
  between operations  0.95 us (2%)
    pallas_call x7, Pallas kernels, call(): pl.pallas_call(kernel, in_specs=[away if is_far else here for is_far in f...  19.7 us
    unnamed x58, local copies, waits for them, and re-layouts  10.1 us
    all_to_all x1, starting transfers between devices, per_device(): lax.all_to_all(outbox, 'patch', split_axis=0, concat_axis=0, tiled=True)  7.4 us
    all_to_all x1, waiting for transfers between devices, per_device(): lax.all_to_all(outbox, 'patch', split_axis=0, concat_axis=0, tiled=True)  5.52 us
    ppermute x1, waiting for transfers between devices, per_device(): totals = [partial_value, lax.ppermute(partial_value, 'band', other)]  4.81 us
    all_to_all x1, waiting for transfers between devices, per_device(): lax.all_to_all(halo_box.reshape(peers, -1, width), 'patch', split_axis=0,...  4.81 us
    all_to_all x1, starting transfers between devices, per_device(): lax.all_to_all(halo_box.reshape(peers, -1, width), 'patch', split_axis=0,...  4.55 us
    ppermute x1, starting transfers between devices, per_device(): totals = [partial_value, lax.ppermute(partial_value, 'band', other)]  1.55 us
  transfers between devices with their start and end apart: 5, of which 4 were waited for; matrix products, arithmetic and copies ran while one was open for 0% of the time, Pallas kernels for 11%

profile of v2, /device:TPU:0, one launch (start us, length us, event | category | flops | bytes accessed | tf_op | source)
XLA Modules:
  0.0 62.1 jit_solution(14788811527673913742)
XLA Ops:
  0.6 0.0 copy-start.22
  0.7 4.8 %shard_map.176 = bf16[16,136,128]{2,1,0:T(8,128)(2,1)} custom-call(s32[1,384]{1,0:T(1,128)} %bitcast.16, s32[3,128]{1,0:T(4,128)} %bitcast.14, bf16[4,384]{1,0:T(4,128)(2,1)} %refs_2_.3, s32[3,128]{1,0:T(4,128)} %bitcast.15, bf16[474,256]{1,0:T(8,128)(2,1)} %bitcast.13, bf16[474,512]{1,0:T(8,128)(2,1)} %refs_5_.4, bf16[512,512]{1,0:T(8,128)(2,1)} %refs_6_.3, ...), custom_call_target="tpu_custom_call" | custom-call | flops 786432000 | bytes 1788416 | tf_op jit(solution)/shard_map/pallas_call | solution.py:145
  5.5 7.4 %all-to-all-start = ((bf16[16,136,128]{2,1,0:T(8,128)(2,1)}), bf16[16,136,128]{2,1,0:T(8,128)(2,1)S(1)}, u32[]{:S(2)}, u32[]{:S(2)}) async-start(bf16[16,136,128]{2,1,0:T(8,128)(2,1)} %shard_map.176), calls=%async_computation | async-start | bytes 1114112 | tf_op jit(solution)/shard_map/all_to_all | solution.py:386
  12.9 1.5 %collective-permute-start = (bf16[256,512]{1,0:T(8,128)(2,1)S(1)}, bf16[256,512]{1,0:T(8,128)(2,1)S(1)}, u32[]{:S(2)}, u32[]{:S(2)}) collective-permute-start(bf16[256,512]{1,0:T(8,128)(2,1)S(1)} %copy-done.16), channel_id=1, source_target_pairs={{0,16},{16,0},{1,17},{17,1},{2,18},{18,2},{3,19},{19,3},{4,20},{20... | collective-permute-start | bytes 786440 | tf_op jit(solution)/shard_map/ppermute | solution.py:394
  14.5 0.5 collective-permute-start.1
  15.0 2.0 %shard_map.177 = (bf16[832,512]{1,0:T(8,128)(2,1)S(1)}, bf16[320,512]{1,0:T(8,128)(2,1)S(1)}, bf16[256,320]{1,0:T(8,128)(2,1)S(1)}, bf16[320,512]{1,0:T(8,128)(2...) custom-call(s32[1,256]{1,0:T(1,128)S(1)} %copy-done.25, bf16[320,512]{1,0:T(8,128)(2,1)S(1)} %copy-done.10, ...), custom_call_target="tpu_custom_call" | custom-call | flops 335544320 | bytes 3474432 | tf_op jit(solution)/shard_map/pallas_call | solution.py:145
  17.0 1.0 %copy-done.4 = bf16[2,512,512]{2,1,0:T(8,128)(2,1)} copy-done((bf16[2,512,512]{2,1,0:T(8,128)(2,1)}, bf16[2,512,512]{2,1,0:T(8,128)(2,1)S(1)}, u32[]{:S(2)}) %copy-start.4) | copy-done | bytes 1048600
  18.0 0.7 %copy-done.11 = bf16[320,512]{1,0:T(8,128)(2,1)} copy-done((bf16[320,512]{1,0:T(8,128)(2,1)}, bf16[320,512]{1,0:T(8,128)(2,1)S(1)}, u32[]{:S(2)}) %copy-start.11) | copy-done | bytes 327704
  18.7 0.7 %copy-done.13 = bf16[320,512]{1,0:T(8,128)(2,1)} copy-done((bf16[320,512]{1,0:T(8,128)(2,1)}, bf16[320,512]{1,0:T(8,128)(2,1)S(1)}, u32[]{:S(2)}) %copy-start.13) | copy-done | bytes 327704
  19.4 0.7 %copy-done.20 = bf16[256,320]{1,0:T(8,128)(2,1)} copy-done((bf16[256,320]{1,0:T(8,128)(2,1)}, bf16[256,320]{1,0:T(8,128)(2,1)S(1)}, u32[]{:S(2)}) %copy-start.20) | copy-done | bytes 163864
  20.1 0.9 %copy-done.26 = bf16[832,512]{1,0:T(8,128)(2,1)} copy-done((bf16[832,512]{1,0:T(8,128)(2,1)}, bf16[832,512]{1,0:T(8,128)(2,1)S(1)}, u32[]{:S(2)}) %copy-start.26) | copy-done | bytes 851992
  21.0 0.6 %collective-permute-done.1.refs_4_ = s32[2,256]{1,0:T(2,128)S(1)} collective-permute-done((s32[2,256]{1,0:T(2,128)S(1)}, s32[2,256]{1,0:T(2,128)S(1)}, u32[]{:S(2)}, u32[]{:S(2)}) %collective-permute-start.1) | collective-permute-done | bytes 2080 | tf_op jit(solution)/shard_map/ppermute | solution.py:395
  21.7 0.0 collective-permute-done.refs_1_
  21.7 0.7 %copy-done.17 = bf16[256,512]{1,0:T(8,128)(2,1)} copy-done((bf16[256,512]{1,0:T(8,128)(2,1)}, bf16[256,512]{1,0:T(8,128)(2,1)S(1)}, u32[]{:S(2)}) %copy-start.17) | copy-done | bytes 262168
  22.4 5.5 %all-to-all-done.refs_0_ = bf16[16,136,128]{2,1,0:T(8,128)(2,1)S(1)} async-done(((bf16[16,136,128]{2,1,0:T(8,128)(2,1)}), bf16[16,136,128]{2,1,0:T(8,128)(2,1)S(1)}, u32[]{:S(2)}, u32[]{:S(2)}) %all-to-all-start) | async-done | bytes 557088 | tf_op jit(solution)/shard_map/all_to_all | solution.py:386
  27.9 1.2 %copy-done.27 = bf16[832,512]{1,0:T(8,128)(2,1)S(1)} copy-done((bf16[832,512]{1,0:T(8,128)(2,1)S(1)}, bf16[832,512]{1,0:T(8,128)(2,1)}, u32[]{:S(2)}) %copy-start.27) | copy-done | bytes 851992
  29.0 1.4 %shard_map.178.refs_0_ = bf16[320,512]{1,0:T(8,128)(2,1)S(1)} custom-call(bf16[16,136,128]{2,1,0:T(8,128)(2,1)S(1)} %all-to-all-done.refs_0_, bf16[832,512]{1,0:T(8,128)(2,1)S(1)} %copy-done.27), custom_call_target="tpu_custom_call" | custom-call | flops 629145600 | bytes 1409024 | tf_op jit(solution)/shard_map/pallas_call | solution.py:145
  30.5 0.0 copy-start.14
  30.5 1.5 %collective-permute-start.2 = (bf16[320,512]{1,0:T(8,128)(2,1)S(1)}, bf16[320,512]{1,0:T(8,128)(2,1)S(1)}, u32[]{:S(2)}, u32[]{:S(2)}) collective-permute-start(bf16[320,512]{1,0:T(8,128)(2,1)S(1)} %shard_map.178.refs_0_), channel_id=1, source_target_pairs={{0,16},{16,0},{1,17},{17,1},{2,18},{18,2},{3,19},{19,3},{4,20},{20... | collective-permute-start | bytes 983048 | tf_op jit(solution)/shard_map/ppermute | solution.py:446
  32.0 0.9 %copy-done.18 = bf16[256,512]{1,0:T(8,128)(2,1)S(1)} copy-done((bf16[256,512]{1,0:T(8,128)(2,1)S(1)}, bf16[256,512]{1,0:T(8,128)(2,1)}, u32[]{:S(2)}) %copy-start.18) | copy-done | bytes 262168
  33.0 2.3 %shard_map.179 = (bf16[512,512]{1,0:T(8,128)(2,1)S(1)}, bf16[512,512]{1,0:T(8,128)(2,1)S(1)}, bf16[512,640]{1,0:T(8,128)(2,1)S(1)}, bf16[512,256]{1,0:T(8,128)(2,1)S(1)}, s32[1,512]{1,0:T(1,128)S(1)}) custom-call(bf16[256,512]{1,0:T(8,128)(2,1)S(1)} %copy-done.16, bf16[256,512]{1,0:T(8,128)(2,1)S(1)} %copy-done.18, s32[1,256]{1,0:T(1,128)S(1)} %bitcast.9, ...), custom_call_target="tpu_custom_call" | custom-call | flops 268435456 | bytes 1052672 | tf_op jit(solution)/shard_map/pallas_call | solution.py:145
  35.3 4.8 %collective-permute-done.2.refs_1_ = bf16[320,512]{1,0:T(8,128)(2,1)S(1)} collective-permute-done((bf16[320,512]{1,0:T(8,128)(2,1)S(1)}, bf16[320,512]{1,0:T(8,128)(2,1)S(1)}, u32[]{:S(2)}, u32[]{:S(2)}) %collective-permute-start.2) | collective-permute-done | bytes 327712 | tf_op jit(solution)/shard_map/ppermute | solution.py:446
  40.2 0.0 copy-start.2
  40.2 2.1 %shard_map.180 = (bf16[320,512]{1,0:T(8,128)(2,1)S(1)}, bf16[256,512]{1,0:T(8,128)(2,1)}) custom-call(bf16[320,512]{1,0:T(8,128)(2,1)S(1)} %shard_map.178.refs_0_, bf16[320,512]{1,0:T(8,128)(2,1)S(1)} %collective-permute-done.2.refs_1_, bf16[320,512]{1,0:T(8,128)(2,1)S(1)} %copy-done.14, bf16[320,512]{1,0:T(8,128)(2,1)S(1)} %copy-done.12, ...), custom_call_target="tpu_custom_call" | custom-call | flops 524288000 | bytes 3047424 | tf_op jit(solution)/shard_map/pallas_call | solution.py:145
  42.4 4.6 %all-to-all-start.1 = ((bf16[16,16,512]{2,1,0:T(8,128)(2,1)}), bf16[16,16,512]{2,1,0:T(8,128)(2,1)S(1)}, u32[]{:S(2)}, u32[]{:S(2)}) async-start(bf16[16,16,512]{2,1,0:T(8,128)(2,1)} %bitcast.6), calls=%async_computation.1 | async-start | bytes 524288 | tf_op jit(solution)/shard_map/all_to_all | solution.py:456
  47.0 1.0 %copy-done.8 = bf16[512,512]{1,0:T(8,128)(2,1)S(1)} copy-done((bf16[512,512]{1,0:T(8,128)(2,1)S(1)}, bf16[512,512]{1,0:T(8,128)(2,1)}, u32[]{:S(2)}) %copy-start.8) | copy-done | bytes 524312
  48.0 2.7 %shard_map.181 = (bf16[512,512]{1,0:T(8,128)(2,1)S(1)}, bf16[320,512]{1,0:T(8,128)(2,1)S(1)}) custom-call(bf16[320,512]{1,0:T(8,128)(2,1)S(1)} %get-tuple-element.47.refs_0_.refs_8_, bf16[512,512]{1,0:T(8,128)(2,1)S(1)} %get-tuple-element.45.refs_6_.refs_1_, bf16[4,512,512]{2,1,0:T(8,128)(2,1)} %refs_3_.3, bf16[512,640]{1,0:T(8,128)(2,1)S(1)} %get-tuple-element.48.refs_3_, ...), custom_call_target="tpu_custom_call" | custom-call | flops 786432000 | bytes 3080192 | tf_op jit(solution)/shard_map/pallas_call | solution.py:145
  50.7 0.8 %copy-done.9 = bf16[512,512]{1,0:T(8,128)(2,1)} copy-done((bf16[512,512]{1,0:T(8,128)(2,1)}, bf16[512,512]{1,0:T(8,128)(2,1)S(1)}, u32[]{:S(2)}) %copy-start.9) | copy-done | bytes 524312
  51.5 0.7 %copy-done.15 = bf16[320,512]{1,0:T(8,128)(2,1)} copy-done((bf16[320,512]{1,0:T(8,128)(2,1)}, bf16[320,512]{1,0:T(8,128)(2,1)S(1)}, u32[]{:S(2)}) %copy-start.15) | copy-done | bytes 327704
  52.2 4.8 %all-to-all-done.1 = bf16[16,16,512]{2,1,0:T(8,128)(2,1)S(1)} async-done(((bf16[16,16,512]{2,1,0:T(8,128)(2,1)}), bf16[16,16,512]{2,1,0:T(8,128)(2,1)S(1)}, u32[]{:S(2)}, u32[]{:S(2)}) %all-to-all-start.1) | async-done | bytes 262176 | tf_op jit(solution)/shard_map/all_to_all | solution.py:456
  57.0 0.7 %copy-done.28 = bf16[16,16,512]{2,1,0:T(8,128)(2,1)} copy-done((bf16[16,16,512]{2,1,0:T(8,128)(2,1)}, bf16[16,16,512]{2,1,0:T(8,128)(2,1)S(1)}, u32[]{:S(2)}) %copy-start.28) | copy-done | bytes 262168
  57.7 4.4 %shard_map.182 = (bf16[256,512]{1,0:T(8,128)(2,1)}, bf16[320,512]{1,0:T(8,128)(2,1)}) custom-call(bf16[512,256]{1,0:T(8,128)(2,1)} %copy-done.19, bf16[256,512]{1,0:T(8,128)(2,1)} %bitcast.12, bf16[512,512]{1,0:T(8,128)(2,1)} %copy-done.9, bf16[4,512,512]{2,1,0:T(8,128)(2,1)} %refs_3_.3, bf16[512,512]{1,0:T(8,128)(2,1)} %copy-done.6, s32[1,512]{1,0:T(1,128)} %copy-done.24, ...), custom_call_target="tpu_custom_call" | custom-call | flops 786432000 | bytes 3803136 | tf_op jit(solution)/shard_map/pallas_call | solution.py:145
  (44 shorter events, 0.1 us)
Async XLA Ops:
  0.6 12.2 %copy-start.22 = (s32[256]{0:T(256)S(1)}, s32[256]{0:T(256)}, u32[]{:S(2)}) copy-start(s32[256]{0:T(256)} %param.24) | copy-start | bytes 3076
  0.6 12.2 %copy-start.23 = (s32[256]{0:T(256)S(1)}, s32[256]{0:T(256)}, u32[]{:S(2)}) copy-start(s32[256]{0:T(256)} %param.25) | copy-start | bytes 3076
  0.7 12.2 %copy-start.16 = (bf16[256,512]{1,0:T(8,128)(2,1)S(1)}, bf16[256,512]{1,0:T(8,128)(2,1)}, u32[]{:S(2)}) copy-start(bf16[256,512]{1,0:T(8,128)(2,1)} %refs_0_.3) | copy-start | bytes 786436
  0.7 14.3 %copy-start.1 = (bf16[3,512,512]{2,1,0:T(8,128)(2,1)S(1)}, bf16[3,512,512]{2,1,0:T(8,128)(2,1)}, u32[]{:S(2)}) copy-start(bf16[3,512,512]{2,1,0:T(8,128)(2,1)} %refs_4_.1) | copy-start | bytes 4718596
  0.7 14.3 %copy-start.10 = (bf16[320,512]{1,0:T(8,128)(2,1)S(1)}, bf16[320,512]{1,0:T(8,128)(2,1)}, u32[]{:S(2)}) copy-start(bf16[320,512]{1,0:T(8,128)(2,1)} %refs_1_) | copy-start | bytes 983044
  0.7 14.3 %copy-start.25 = (s32[1,256]{1,0:T(1,128)S(1)}, s32[1,256]{1,0:T(1,128)}, u32[]{:S(2)}) copy-start(s32[1,256]{1,0:T(1,128)} %refs_0_.2) | copy-start | bytes 3076
  5.5 22.4 %all-to-all-start = ((bf16[16,136,128]{2,1,0:T(8,128)(2,1)}), bf16[16,136,128]{2,1,0:T(8,128)(2,1)S(1)}, u32[]{:S(2)}, u32[]{:S(2)}) async-start(bf16[16,136,128]{2,1,0:T(8,128)(2,1)} %shard_map.176), calls=%async_computation | async-start | bytes 1114112 | tf_op jit(solution)/shard_map/all_to_all | solution.py:386
  12.9 8.8 %collective-permute-start = (bf16[256,512]{1,0:T(8,128)(2,1)S(1)}, bf16[256,512]{1,0:T(8,128)(2,1)S(1)}, u32[]{:S(2)}, u32[]{:S(2)}) collective-permute-start(bf16[256,512]{1,0:T(8,128)(2,1)S(1)} %copy-done.16), channel_id=1, source_target_pairs={{0,16},{16,0},{1,17},{17,1},{2,18},{18,2},{3,19},{19,3},{4,20},{20... | collective-permute-start | bytes 786440 | tf_op jit(solution)/shard_map/ppermute | solution.py:394
  14.5 7.2 %collective-permute-start.1 = (s32[2,256]{1,0:T(2,128)S(1)}, s32[2,256]{1,0:T(2,128)S(1)}, u32[]{:S(2)}, u32[]{:S(2)}) collective-permute-start(s32[2,256]{1,0:T(2,128)S(1)} %pad_add_fusion), channel_id=1, source_target_pairs={{0,16},{16,0},{1,17},{17,1},{2,18},{18,2},{3,19},{19,3},{4,20},{20... | collective-permute-start | bytes 6152 | tf_op jit(solution)/shard_map/ppermute | solution.py:395
  17.0 1.0 %copy-start.4 = (bf16[2,512,512]{2,1,0:T(8,128)(2,1)}, bf16[2,512,512]{2,1,0:T(8,128)(2,1)S(1)}, u32[]{:S(2)}) copy-start(bf16[2,512,512]{2,1,0:T(8,128)(2,1)S(1)} %get-tuple-element.43.refs_4_) | copy-start | bytes 3145732
  18.0 0.7 %copy-start.11 = (bf16[320,512]{1,0:T(8,128)(2,1)}, bf16[320,512]{1,0:T(8,128)(2,1)S(1)}, u32[]{:S(2)}) copy-start(bf16[320,512]{1,0:T(8,128)(2,1)S(1)} %get-tuple-element.42.refs_3_) | copy-start | bytes 983044
  18.7 0.7 %copy-start.13 = (bf16[320,512]{1,0:T(8,128)(2,1)}, bf16[320,512]{1,0:T(8,128)(2,1)S(1)}, u32[]{:S(2)}) copy-start(bf16[320,512]{1,0:T(8,128)(2,1)S(1)} %get-tuple-element.39.refs_2_) | copy-start | bytes 983044
  20.1 0.9 %copy-start.26 = (bf16[832,512]{1,0:T(8,128)(2,1)}, bf16[832,512]{1,0:T(8,128)(2,1)S(1)}, u32[]{:S(2)}) copy-start(bf16[832,512]{1,0:T(8,128)(2,1)S(1)} %get-tuple-element.34.refs_1_) | copy-start | bytes 2555908
  21.0 11.0 %copy-start = (bf16[4,512,512]{2,1,0:T(8,128)(2,1)S(1)}, bf16[4,512,512]{2,1,0:T(8,128)(2,1)}, u32[]{:S(2)}) copy-start(bf16[4,512,512]{2,1,0:T(8,128)(2,1)} %refs_3_.3) | copy-start | bytes 6291460
  27.9 1.2 %copy-start.27 = (bf16[832,512]{1,0:T(8,128)(2,1)S(1)}, bf16[832,512]{1,0:T(8,128)(2,1)}, u32[]{:S(2)}) copy-start(bf16[832,512]{1,0:T(8,128)(2,1)} %copy-done.26) | copy-start | bytes 2555908
  30.4 9.7 %copy-start.5 = (bf16[2,512,512]{2,1,0:T(8,128)(2,1)S(1)}, bf16[2,512,512]{2,1,0:T(8,128)(2,1)}, u32[]{:S(2)}) copy-start(bf16[2,512,512]{2,1,0:T(8,128)(2,1)} %copy-done.4) | copy-start | bytes 3145732
  30.4 9.7 %copy-start.12 = (bf16[320,512]{1,0:T(8,128)(2,1)S(1)}, bf16[320,512]{1,0:T(8,128)(2,1)}, u32[]{:S(2)}) copy-start(bf16[320,512]{1,0:T(8,128)(2,1)} %copy-done.11) | copy-start | bytes 983044
  30.5 9.7 %copy-start.14 = (bf16[320,512]{1,0:T(8,128)(2,1)S(1)}, bf16[320,512]{1,0:T(8,128)(2,1)}, u32[]{:S(2)}) copy-start(bf16[320,512]{1,0:T(8,128)(2,1)} %copy-done.13) | copy-start | bytes 983044
  30.5 9.7 %collective-permute-start.2 = (bf16[320,512]{1,0:T(8,128)(2,1)S(1)}, bf16[320,512]{1,0:T(8,128)(2,1)S(1)}, u32[]{:S(2)}, u32[]{:S(2)}) collective-permute-start(bf16[320,512]{1,0:T(8,128)(2,1)S(1)} %shard_map.178.refs_0_), channel_id=1, source_target_pairs={{0,16},{16,0},{1,17},{17,1},{2,18},{18,2},{3,19},{19,3},{4,20},{20... | collective-permute-start | bytes 983048 | tf_op jit(solution)/shard_map/ppermute | solution.py:446
  32.0 1.0 %copy-start.18 = (bf16[256,512]{1,0:T(8,128)(2,1)S(1)}, bf16[256,512]{1,0:T(8,128)(2,1)}, u32[]{:S(2)}) copy-start(bf16[256,512]{1,0:T(8,128)(2,1)} %copy-done.17) | copy-start | bytes 786436
  33.0 7.2 %copy-start.21 = (bf16[256,320]{1,0:T(8,128)(2,1)S(1)}, bf16[256,320]{1,0:T(8,128)(2,1)}, u32[]{:S(2)}) copy-start(bf16[256,320]{1,0:T(8,128)(2,1)} %copy-done.20) | copy-start | bytes 491524
  35.3 7.0 %copy-start.6 = (bf16[512,512]{1,0:T(8,128)(2,1)}, bf16[512,512]{1,0:T(8,128)(2,1)S(1)}, u32[]{:S(2)}) copy-start(bf16[512,512]{1,0:T(8,128)(2,1)S(1)} %get-tuple-element.51.refs_4_) | copy-start | bytes 1572868
  35.3 7.0 %copy-start.7 = (bf16[512,512]{1,0:T(8,128)(2,1)}, bf16[512,512]{1,0:T(8,128)(2,1)S(1)}, u32[]{:S(2)}) copy-start(bf16[512,512]{1,0:T(8,128)(2,1)S(1)} %get-tuple-element.49.refs_4_) | copy-start | bytes 1572868
  35.3 7.0 %copy-start.19 = (bf16[512,256]{1,0:T(8,128)(2,1)}, bf16[512,256]{1,0:T(8,128)(2,1)S(1)}, u32[]{:S(2)}) copy-start(bf16[512,256]{1,0:T(8,128)(2,1)S(1)} %get-tuple-element.37.refs_0_) | copy-start | bytes 786436
  35.3 7.0 %copy-start.24 = (s32[1,512]{1,0:T(1,128)}, s32[1,512]{1,0:T(1,128)S(1)}, u32[]{:S(2)}) copy-start(s32[1,512]{1,0:T(1,128)S(1)} %get-tuple-element.52.refs_5_) | copy-start | bytes 6148
  40.2 6.8 %copy-start.2 = (bf16[3,512,512]{2,1,0:T(8,128)(2,1)S(1)}, bf16[3,512,512]{2,1,0:T(8,128)(2,1)}, u32[]{:S(2)}) copy-start(bf16[3,512,512]{2,1,0:T(8,128)(2,1)} %refs_6_.5) | copy-start | bytes 4718596
  42.3 8.3 %copy-start.3 = (bf16[320,512]{1,0:T(8,128)(2,1)}, bf16[320,512]{1,0:T(8,128)(2,1)S(1)}, u32[]{:S(2)}) copy-start(bf16[320,512]{1,0:T(8,128)(2,1)S(1)} %get-tuple-element.47.refs_0_.refs_8_) | copy-start | bytes 983044
  42.4 14.6 %all-to-all-start.1 = ((bf16[16,16,512]{2,1,0:T(8,128)(2,1)}), bf16[16,16,512]{2,1,0:T(8,128)(2,1)S(1)}, u32[]{:S(2)}, u32[]{:S(2)}) async-start(bf16[16,16,512]{2,1,0:T(8,128)(2,1)} %bitcast.6), calls=%async_computation.1 | async-start | bytes 524288 | tf_op jit(solution)/shard_map/all_to_all | solution.py:456
  47.0 1.0 %copy-start.8 = (bf16[512,512]{1,0:T(8,128)(2,1)S(1)}, bf16[512,512]{1,0:T(8,128)(2,1)}, u32[]{:S(2)}) copy-start(bf16[512,512]{1,0:T(8,128)(2,1)} %copy-done.7) | copy-start | bytes 1572868
  50.7 0.8 %copy-start.9 = (bf16[512,512]{1,0:T(8,128)(2,1)}, bf16[512,512]{1,0:T(8,128)(2,1)S(1)}, u32[]{:S(2)}) copy-start(bf16[512,512]{1,0:T(8,128)(2,1)S(1)} %get-tuple-element.50.refs_2_) | copy-start | bytes 1572868
  51.5 0.7 %copy-start.15 = (bf16[320,512]{1,0:T(8,128)(2,1)}, bf16[320,512]{1,0:T(8,128)(2,1)S(1)}, u32[]{:S(2)}) copy-start(bf16[320,512]{1,0:T(8,128)(2,1)S(1)} %get-tuple-element.53.refs_7_) | copy-start | bytes 983044
  57.0 0.7 %copy-start.28 = (bf16[16,16,512]{2,1,0:T(8,128)(2,1)}, bf16[16,16,512]{2,1,0:T(8,128)(2,1)S(1)}, u32[]{:S(2)}) copy-start(bf16[16,16,512]{2,1,0:T(8,128)(2,1)S(1)} %all-to-all-done.1) | copy-start | bytes 786436
  (2 other events, 1.4 us)

commit v3 on v2

--- a/solution.py
+++ b/solution.py
@@ -109,10 +109,10 @@
 
 
 PARTS = 4
-BIG, MID, SMALL = 60, 48, 12
-
-
-def call(body, outs, operands, flops, far_outs=False, room=SMALL):
+BIG, ROOM = 60, 48
+
+
+def call(body, outs, operands, flops, far_outs=False, room=ROOM):
     n_in, n_out = len(operands), len(outs)
     far_in = [isinstance(operand, Far) for operand in operands]
     arrays = [operand.array if away else operand for operand, away in zip(operands, far_in)]
@@ -172,6 +172,8 @@
         lax.broadcasted_iota(jnp.int32, (edges, edges), 0)
         < lax.broadcasted_iota(jnp.int32, (edges, edges), 1)
     )
+    for one in arriving:
+        one.ref()
     patch = patch()
     named = lax.broadcasted_iota(jnp.int32, (peers, edges), 0) == patch
     named_f = jnp.where(named, 1.0, 0.0)
@@ -232,13 +234,18 @@
     recv_out.send(0, 1)
 
 
-def bring_body(arriving, leaving):
-    halo, nodes, recv_w, node_w, out_w, pair_w, sent_w = arriving
-    message_out, node_pre_out, halo_out, nodes_out, pair_w_out, sent_w_out = leaving
+def message_bring_body(arriving, leaving):
+    nodes, recv_w, out_w = arriving
+    (both,) = leaving
+    both.put(dot_nn(nodes(), recv_w()).astype(BF16))
+    both.put(out_w(), nodes.held.shape[0])
+
+
+def mesh_bring_body(arriving, leaving):
+    halo, nodes, node_w, pair_w, sent_w = arriving
+    node_pre_out, halo_out, nodes_out, pair_w_out, sent_w_out = leaving
     halo_out.put(rows_equal(nodes.held.shape[0], halo()).T)
     nodes_out.put(nodes())
-    message_out.put(dot_nn(nodes(), recv_w()).astype(BF16))
-    message_out.put(out_w(), nodes.held.shape[0])
     node_pre_out.put(dot_nn(nodes(), node_w()).astype(BF16))
     pair_w_out.put(pair_w())
     sent_w_out.put(sent_w())
@@ -396,27 +403,12 @@
     count = len(edge_parts)
     edge_total = count * medge_count
     nodes, _ = lax.optimization_barrier((mesh_nodes, outbox))
-    message_pair, node_pre, halo_hot, nodes, node_w, sent_w = call(
-        bring_body,
-        [
-            shape((mesh_count + width, width)),
-            node_like,
-            shape((halo_count, mesh_count)),
-            node_like,
-            pair,
-            matrix,
-        ],
-        [
-            Far(halo_rows),
-            Far(nodes),
-            Far(enc_edge_w, 1),
-            Far(enc_node_w, 0),
-            Far(enc_edge_w, 2),
-            Far(enc_node_w, 1, 2),
-            Far(proc_edge_w, 1),
-        ],
-        unit * 640,
-        room=MID,
+    (message_pair,) = call(
+        message_bring_body,
+        [shape((mesh_count + width, width))],
+        [Far(nodes), Far(enc_edge_w, 1), Far(enc_edge_w, 2)],
+        unit * 320,
+        room=ROOM,
     )
     message_pair, edge_parts[-1], names[-1] = lax.optimization_barrier(
         (message_pair, edge_parts[-1], names[-1])
@@ -440,12 +432,20 @@
         [Far(one) for one in edge_parts + names] + [Far(proc_edge_w, 0)],
         unit * edge_total,
         far_outs=True,
-        room=MID,
+        room=ROOM,
     )
     if paired:
         totals = [partial_value, lax.ppermute(partial_value, "band", other)]
     else:
         totals = [band_sum(partial_value)]
+    nodes, halo_rows, _ = lax.optimization_barrier((mesh_nodes, halo_rows, partial_value))
+    node_pre, halo_hot, nodes, node_w, sent_w = call(
+        mesh_bring_body,
+        [node_like, shape((halo_count, mesh_count)), node_like, pair, matrix],
+        [Far(halo_rows), Far(nodes), Far(enc_node_w, 0), Far(enc_node_w, 1, 2), Far(proc_edge_w, 1)],
+        unit * 320,
+        room=ROOM,
+    )
     node_pre, edge_pre = lax.optimization_barrier((node_pre, edge_pre))
     mesh_one, halo_box = call(
         functools.partial(mesh_body, count=len(totals)),
@@ -463,7 +463,7 @@
         [mesh_one, sent_w, Far(proc_edge_w, 2), Far(ends), Far(edge_pre), Far(proc_node_w, 0)],
         unit * 1500,
         far_outs=True,
-        room=MID,
+        room=ROOM,
     )
     edge_operands = [Far(far), Far(ghosts), Far(edge_pre), Far(proc_edge_w, 3), Far(edges), Far(edge_recv)]
     node_operands = [Far(proc_node_w, 1, 2), Far(node_pre), Far(mesh_one)]

time: 62.7 us -> 61 us (0.973)
  local copies, waits for them, and re-layouts: 10.1 us -> 6.23 us
  waiting for transfers between devices: 15.8 us -> 17.5 us
    ppermute x1, waiting for transfers between devices: 0.65 us -> 6.22 us  [per_device(): names.append(lax.ppermute(own_names, 'band', other))]
    unnamed x58 -> x38, local copies, waits for them, and re-layouts: 10.1 us -> 6.23 us
    ppermute x1, waiting for transfers between devices: 4.81 us -> 1.18 us  [per_device(): totals = [partial_value, lax.ppermute(partial_value, 'band', other)]]
    pallas_call x7 -> x8, Pallas kernels: 19.7 us -> 20.3 us  [call(): pl.pallas_call(kernel, in_specs=[away if is_far else here for is_far in f...]
  transfers between devices with their start and end apart: 5 -> 5, of which waited for: 4 -> 4; matrix products, arithmetic and copies ran while one was open for 0% -> 0% of each run, Pallas kernels for 11% -> 13%
where the time goes in v3:
time: 61 us; the launch traced here: 60.5 us
  Pallas kernels  20.3 us (33%)
  waiting for transfers between devices  17.5 us (29%)
  starting transfers between devices  15.6 us (26%)
  local copies, waits for them, and re-layouts  6.23 us (10%)
  between operations  0.88 us (1%)
    pallas_call x8, Pallas kernels, call(): pl.pallas_call(kernel, in_specs=[away if is_far else here for is_far in f...  20.3 us
    all_to_all x1, starting transfers between devices, per_device(): lax.all_to_all(outbox, 'patch', split_axis=0, concat_axis=0, tiled=True)  7.39 us
    unnamed x38, local copies, waits for them, and re-layouts  6.23 us
    ppermute x1, waiting for transfers between devices, per_device(): names.append(lax.ppermute(own_names, 'band', other))  6.22 us
    all_to_all x1, waiting for transfers between devices, per_device(): lax.all_to_all(outbox, 'patch', split_axis=0, concat_axis=0, tiled=True)  5.32 us
    all_to_all x1, waiting for transfers between devices, per_device(): lax.all_to_all(halo_box.reshape(peers, -1, width), 'patch', split_axis=0,...  4.79 us
    all_to_all x1, starting transfers between devices, per_device(): lax.all_to_all(halo_box.reshape(peers, -1, width), 'patch', split_axis=0,...  4.54 us
    ppermute x1, starting transfers between devices, per_device(): edge_parts.append(lax.ppermute(own_edge, 'band', other))  1.56 us
  transfers between devices with their start and end apart: 5, of which 4 were waited for; matrix products, arithmetic and copies ran while one was open for 0% of the time, Pallas kernels for 13%

profile of v3, /device:TPU:0, one launch (start us, length us, event | category | flops | bytes accessed | tf_op | source)
XLA Modules:
  0.0 60.5 jit_solution(12015393198036120300)
XLA Ops:
  0.6 0.0 copy-start.14
  0.6 0.0 copy-start.15
  0.7 0.0 copy-start.1
  0.7 4.4 %shard_map.176 = bf16[16,136,128]{2,1,0:T(8,128)(2,1)} custom-call(s32[1,384]{1,0:T(1,128)} %bitcast.16, s32[3,128]{1,0:T(4,128)} %bitcast.14, bf16[4,384]{1,0:T(4,128)(2,1)} %refs_2_.4, s32[3,128]{1,0:T(4,128)} %bitcast.15, bf16[474,256]{1,0:T(8,128)(2,1)} %bitcast.13, bf16[474,512]{1,0:T(8,128)(2,1)} %refs_5_.3, bf16[512,512]{1,0:T(8,128)(2,1)} %refs_6_.2, ...), custom_call_target="tpu_custom_call" | custom-call | flops 786432000 | bytes 1788416 | tf_op jit(solution)/shard_map/pallas_call | solution.py:145
  5.1 7.4 %all-to-all-start = ((bf16[16,136,128]{2,1,0:T(8,128)(2,1)}), bf16[16,136,128]{2,1,0:T(8,128)(2,1)S(1)}, u32[]{:S(2)}, u32[]{:S(2)}) async-start(bf16[16,136,128]{2,1,0:T(8,128)(2,1)} %shard_map.176), calls=%async_computation | async-start | bytes 1114112 | tf_op jit(solution)/shard_map/all_to_all | solution.py:393
  12.5 1.6 %collective-permute-start = (bf16[256,512]{1,0:T(8,128)(2,1)}, bf16[256,512]{1,0:T(8,128)(2,1)S(1)}, u32[]{:S(2)}, u32[]{:S(2)}) collective-permute-start(bf16[256,512]{1,0:T(8,128)(2,1)} %refs_0_.2), channel_id=1, source_target_pairs={{0,16},{16,0},{1,17},{17,1},{2,18},{18,2},{3,19},{19,3},{4,20},{20... | collective-permute-start | bytes 786440 | tf_op jit(solution)/shard_map/ppermute | solution.py:401
  14.0 0.5 collective-permute-start.1
  14.6 0.6 %shard_map.177.refs_1_ = bf16[832,512]{1,0:T(8,128)(2,1)S(1)} custom-call(bf16[320,512]{1,0:T(8,128)(2,1)S(1)} %copy-done.4, bf16[3,512,512]{2,1,0:T(8,128)(2,1)S(1)} %copy-done.1, bf16[3,512,512]{2,1,0:T(8,128)(2,1)S(1)} %copy-done.1), custom_call_target="tpu_custom_call" | custom-call | flops 167772160 | bytes 1376256 | tf_op jit(solution)/shard_map/pallas_call | solution.py:145
  15.2 0.0 copy-start.17
  15.2 6.2 %collective-permute-done.1.refs_4_ = s32[2,256]{1,0:T(2,128)S(1)} collective-permute-done((s32[2,256]{1,0:T(2,128)S(1)}, s32[2,256]{1,0:T(2,128)S(1)}, u32[]{:S(2)}, u32[]{:S(2)}) %collective-permute-start.1) | collective-permute-done | bytes 2080 | tf_op jit(solution)/shard_map/ppermute | solution.py:402
  21.4 0.0 collective-permute-done.refs_1_
  21.4 0.7 %copy-done.11 = bf16[256,512]{1,0:T(8,128)(2,1)} copy-done((bf16[256,512]{1,0:T(8,128)(2,1)}, bf16[256,512]{1,0:T(8,128)(2,1)S(1)}, u32[]{:S(2)}) %copy-start.11) | copy-done | bytes 262168
  22.1 5.3 %all-to-all-done.refs_0_ = bf16[16,136,128]{2,1,0:T(8,128)(2,1)S(1)} async-done(((bf16[16,136,128]{2,1,0:T(8,128)(2,1)}), bf16[16,136,128]{2,1,0:T(8,128)(2,1)S(1)}, u32[]{:S(2)}, u32[]{:S(2)}) %all-to-all-start) | async-done | bytes 557088 | tf_op jit(solution)/shard_map/all_to_all | solution.py:393
  27.5 1.4 %shard_map.178.refs_0_ = bf16[320,512]{1,0:T(8,128)(2,1)S(1)} custom-call(bf16[16,136,128]{2,1,0:T(8,128)(2,1)S(1)} %all-to-all-done.refs_0_, bf16[832,512]{1,0:T(8,128)(2,1)S(1)} %shard_map.177.refs_1_), custom_call_target="tpu_custom_call" | custom-call | flops 629145600 | bytes 1409024 | tf_op jit(solution)/shard_map/pallas_call | solution.py:145
  28.8 0.0 copy-start
  28.8 1.6 %collective-permute-start.2 = (bf16[320,512]{1,0:T(8,128)(2,1)S(1)}, bf16[320,512]{1,0:T(8,128)(2,1)S(1)}, u32[]{:S(2)}, u32[]{:S(2)}) collective-permute-start(bf16[320,512]{1,0:T(8,128)(2,1)S(1)} %shard_map.178.refs_0_), channel_id=1, source_target_pairs={{0,16},{16,0},{1,17},{17,1},{2,18},{18,2},{3,19},{19,3},{4,20},{20... | collective-permute-start | bytes 983048 | tf_op jit(solution)/shard_map/ppermute | solution.py:438
  30.4 1.4 %copy-done.2 = bf16[3,512,512]{2,1,0:T(8,128)(2,1)S(1)} copy-done((bf16[3,512,512]{2,1,0:T(8,128)(2,1)S(1)}, bf16[3,512,512]{2,1,0:T(8,128)(2,1)}, u32[]{:S(2)}) %copy-start.2) | copy-done | bytes 1572888
  31.8 1.5 %shard_map.180 = (bf16[320,512]{1,0:T(8,128)(2,1)S(1)}, bf16[256,320]{1,0:T(8,128)(2,1)S(1)}, bf16[320,512]{1,0:T(8,128)(2,1)S(1)}, bf16[2,512,512]{2,1,0:T(8,128)(2,1)S(1)}, bf16[512,512]{1,0:T(8,128)(2,1)S(1)}) custom-call(s32[1,256]{1,0:T(1,128)S(1)} %copy-done.17, bf16[320,512]{1,0:T(8,128)(2,1)S(1)} %copy-done.4, bf16[3,512,512]{2,1,0:T(8,128)(2,1)S(1)} %copy-done.2, ...), custom_call_target="tpu_custom_call" | custom-call | flops 167772160 | bytes 2425856 | tf_op jit(solution)/shard_map/pallas_call | solution.py:145
  33.4 3.2 %shard_map.179 = (bf16[512,512]{1,0:T(8,128)(2,1)S(1)}, bf16[512,512]{1,0:T(8,128)(2,1)S(1)}, bf16[512,640]{1,0:T(8,128)(2,1)S(1)}, bf16[512,256]{1,0:T(8,128)(2,1)S(1)}, s32[1,512]{1,0:T(1,128)S(1)}) custom-call(bf16[256,512]{1,0:T(8,128)(2,1)} %refs_0_.2, bf16[256,512]{1,0:T(8,128)(2,1)S(1)} %copy-done.12, s32[1,256]{1,0:T(1,128)S(1)} %bitcast.9, ...), custom_call_target="tpu_custom_call" | custom-call | flops 268435456 | bytes 1052672 | tf_op jit(solution)/shard_map/pallas_call | solution.py:145
  36.6 0.8 %copy-done.7 = bf16[512,512]{1,0:T(8,128)(2,1)} copy-done((bf16[512,512]{1,0:T(8,128)(2,1)}, bf16[512,512]{1,0:T(8,128)(2,1)S(1)}, u32[]{:S(2)}) %copy-start.7) | copy-done | bytes 524312
  37.4 1.2 %collective-permute-done.2.refs_1_ = bf16[320,512]{1,0:T(8,128)(2,1)S(1)} collective-permute-done((bf16[320,512]{1,0:T(8,128)(2,1)S(1)}, bf16[320,512]{1,0:T(8,128)(2,1)S(1)}, u32[]{:S(2)}, u32[]{:S(2)}) %collective-permute-start.2) | collective-permute-done | bytes 327712 | tf_op jit(solution)/shard_map/ppermute | solution.py:438
  38.5 2.1 %shard_map.181 = (bf16[320,512]{1,0:T(8,128)(2,1)S(1)}, bf16[256,512]{1,0:T(8,128)(2,1)}) custom-call(bf16[320,512]{1,0:T(8,128)(2,1)S(1)} %shard_map.178.refs_0_, bf16[320,512]{1,0:T(8,128)(2,1)S(1)} %collective-permute-done.2.refs_1_, bf16[320,512]{1,0:T(8,128)(2,1)S(1)} %get-tuple-element.41.refs_2_, bf16[320,512]{1,0:T(8,128)(2,1)S(1)} %get-tuple-element.44.refs_3_, ...), custom_call_target="tpu_custom_call" | custom-call | flops 524288000 | bytes 3047424 | tf_op jit(solution)/shard_map/pallas_call | solution.py:145
  40.7 4.5 %all-to-all-start.1 = ((bf16[16,16,512]{2,1,0:T(8,128)(2,1)}), bf16[16,16,512]{2,1,0:T(8,128)(2,1)S(1)}, u32[]{:S(2)}, u32[]{:S(2)}) async-start(bf16[16,16,512]{2,1,0:T(8,128)(2,1)} %bitcast.6), calls=%async_computation.1 | async-start | bytes 524288 | tf_op jit(solution)/shard_map/all_to_all | solution.py:456
  45.3 1.0 %copy-done.8 = bf16[512,512]{1,0:T(8,128)(2,1)S(1)} copy-done((bf16[512,512]{1,0:T(8,128)(2,1)S(1)}, bf16[512,512]{1,0:T(8,128)(2,1)}, u32[]{:S(2)}) %copy-start.8) | copy-done | bytes 524312
  46.3 2.7 %shard_map.182 = (bf16[512,512]{1,0:T(8,128)(2,1)S(1)}, bf16[320,512]{1,0:T(8,128)(2,1)S(1)}) custom-call(bf16[320,512]{1,0:T(8,128)(2,1)S(1)} %get-tuple-element.49.refs_0_.refs_8_, bf16[512,512]{1,0:T(8,128)(2,1)S(1)} %get-tuple-element.47.refs_6_.refs_1_, bf16[4,512,512]{2,1,0:T(8,128)(2,1)} %refs_3_.3, bf16[512,640]{1,0:T(8,128)(2,1)S(1)} %get-tuple-element.50.refs_3_, ...), custom_call_target="tpu_custom_call" | custom-call | flops 786432000 | bytes 3080192 | tf_op jit(solution)/shard_map/pallas_call | solution.py:145
  49.0 0.0 copy-done.5
  49.0 0.0 copy-start.9
  49.0 0.8 %copy-done.9 = bf16[512,512]{1,0:T(8,128)(2,1)} copy-done((bf16[512,512]{1,0:T(8,128)(2,1)}, bf16[512,512]{1,0:T(8,128)(2,1)S(1)}, u32[]{:S(2)}) %copy-start.9) | copy-done | bytes 524312
  49.8 0.7 %copy-done.10 = bf16[320,512]{1,0:T(8,128)(2,1)} copy-done((bf16[320,512]{1,0:T(8,128)(2,1)}, bf16[320,512]{1,0:T(8,128)(2,1)S(1)}, u32[]{:S(2)}) %copy-start.10) | copy-done | bytes 327704
  50.5 4.8 %all-to-all-done.1 = bf16[16,16,512]{2,1,0:T(8,128)(2,1)S(1)} async-done(((bf16[16,16,512]{2,1,0:T(8,128)(2,1)}), bf16[16,16,512]{2,1,0:T(8,128)(2,1)S(1)}, u32[]{:S(2)}, u32[]{:S(2)}) %all-to-all-start.1) | async-done | bytes 262176 | tf_op jit(solution)/shard_map/all_to_all | solution.py:456
  55.3 0.7 %copy-done.18 = bf16[16,16,512]{2,1,0:T(8,128)(2,1)} copy-done((bf16[16,16,512]{2,1,0:T(8,128)(2,1)}, bf16[16,16,512]{2,1,0:T(8,128)(2,1)S(1)}, u32[]{:S(2)}) %copy-start.18) | copy-done | bytes 262168
  56.0 4.4 %shard_map.183 = (bf16[256,512]{1,0:T(8,128)(2,1)}, bf16[320,512]{1,0:T(8,128)(2,1)}) custom-call(bf16[512,256]{1,0:T(8,128)(2,1)} %copy-done.13, bf16[256,512]{1,0:T(8,128)(2,1)} %bitcast.12, bf16[512,512]{1,0:T(8,128)(2,1)} %copy-done.9, bf16[4,512,512]{2,1,0:T(8,128)(2,1)} %refs_3_.3, bf16[512,512]{1,0:T(8,128)(2,1)} %copy-done.6, s32[1,512]{1,0:T(1,128)} %copy-done.16, ...), custom_call_target="tpu_custom_call" | custom-call | flops 786432000 | bytes 3803136 | tf_op jit(solution)/shard_map/pallas_call | solution.py:145
  (25 shorter events, 0.1 us)
Async XLA Ops:
  0.6 11.8 %copy-start.14 = (s32[256]{0:T(256)S(1)}, s32[256]{0:T(256)}, u32[]{:S(2)}) copy-start(s32[256]{0:T(256)} %param.24) | copy-start | bytes 3076
  0.6 11.8 %copy-start.15 = (s32[256]{0:T(256)S(1)}, s32[256]{0:T(256)}, u32[]{:S(2)}) copy-start(s32[256]{0:T(256)} %param.25) | copy-start | bytes 3076
  0.7 13.9 %copy-start.1 = (bf16[3,512,512]{2,1,0:T(8,128)(2,1)S(1)}, bf16[3,512,512]{2,1,0:T(8,128)(2,1)}, u32[]{:S(2)}) copy-start(bf16[3,512,512]{2,1,0:T(8,128)(2,1)} %refs_2_.5) | copy-start | bytes 4718596
  0.7 13.9 %copy-start.4 = (bf16[320,512]{1,0:T(8,128)(2,1)S(1)}, bf16[320,512]{1,0:T(8,128)(2,1)}, u32[]{:S(2)}) copy-start(bf16[320,512]{1,0:T(8,128)(2,1)} %refs_1_.2) | copy-start | bytes 983044
  5.1 22.4 %all-to-all-start = ((bf16[16,136,128]{2,1,0:T(8,128)(2,1)}), bf16[16,136,128]{2,1,0:T(8,128)(2,1)S(1)}, u32[]{:S(2)}, u32[]{:S(2)}) async-start(bf16[16,136,128]{2,1,0:T(8,128)(2,1)} %shard_map.176), calls=%async_computation | async-start | bytes 1114112 | tf_op jit(solution)/shard_map/all_to_all | solution.py:393
  12.5 9.0 %collective-permute-start = (bf16[256,512]{1,0:T(8,128)(2,1)}, bf16[256,512]{1,0:T(8,128)(2,1)S(1)}, u32[]{:S(2)}, u32[]{:S(2)}) collective-permute-start(bf16[256,512]{1,0:T(8,128)(2,1)} %refs_0_.2), channel_id=1, source_target_pairs={{0,16},{16,0},{1,17},{17,1},{2,18},{18,2},{3,19},{19,3},{4,20},{20... | collective-permute-start | bytes 786440 | tf_op jit(solution)/shard_map/ppermute | solution.py:401
  14.0 7.4 %collective-permute-start.1 = (s32[2,256]{1,0:T(2,128)S(1)}, s32[2,256]{1,0:T(2,128)S(1)}, u32[]{:S(2)}, u32[]{:S(2)}) collective-permute-start(s32[2,256]{1,0:T(2,128)S(1)} %pad_add_fusion), channel_id=1, source_target_pairs={{0,16},{16,0},{1,17},{17,1},{2,18},{18,2},{3,19},{19,3},{4,20},{20... | collective-permute-start | bytes 6152 | tf_op jit(solution)/shard_map/ppermute | solution.py:402
  15.2 15.2 %copy-start.17 = (s32[1,256]{1,0:T(1,128)S(1)}, s32[1,256]{1,0:T(1,128)}, u32[]{:S(2)}) copy-start(s32[1,256]{1,0:T(1,128)} %refs_0_.3) | copy-start | bytes 3076
  21.4 0.7 %copy-start.11 = (bf16[256,512]{1,0:T(8,128)(2,1)}, bf16[256,512]{1,0:T(8,128)(2,1)S(1)}, u32[]{:S(2)}) copy-start(bf16[256,512]{1,0:T(8,128)(2,1)S(1)} %collective-permute-done.refs_1_) | copy-start | bytes 786436
  28.8 4.5 %copy-start = (bf16[4,512,512]{2,1,0:T(8,128)(2,1)S(1)}, bf16[4,512,512]{2,1,0:T(8,128)(2,1)}, u32[]{:S(2)}) copy-start(bf16[4,512,512]{2,1,0:T(8,128)(2,1)} %refs_3_.3) | copy-start | bytes 6291460
  28.8 9.7 %collective-permute-start.2 = (bf16[320,512]{1,0:T(8,128)(2,1)S(1)}, bf16[320,512]{1,0:T(8,128)(2,1)S(1)}, u32[]{:S(2)}, u32[]{:S(2)}) collective-permute-start(bf16[320,512]{1,0:T(8,128)(2,1)S(1)} %shard_map.178.refs_0_), channel_id=1, source_target_pairs={{0,16},{16,0},{1,17},{17,1},{2,18},{18,2},{3,19},{19,3},{4,20},{20... | collective-permute-start | bytes 983048 | tf_op jit(solution)/shard_map/ppermute | solution.py:438
  30.4 1.4 %copy-start.2 = (bf16[3,512,512]{2,1,0:T(8,128)(2,1)S(1)}, bf16[3,512,512]{2,1,0:T(8,128)(2,1)}, u32[]{:S(2)}) copy-start(bf16[3,512,512]{2,1,0:T(8,128)(2,1)} %refs_3_.2) | copy-start | bytes 4718596
  31.8 1.5 %copy-start.12 = (bf16[256,512]{1,0:T(8,128)(2,1)S(1)}, bf16[256,512]{1,0:T(8,128)(2,1)}, u32[]{:S(2)}) copy-start(bf16[256,512]{1,0:T(8,128)(2,1)} %copy-done.11) | copy-start | bytes 786436
  36.6 0.8 %copy-start.7 = (bf16[512,512]{1,0:T(8,128)(2,1)}, bf16[512,512]{1,0:T(8,128)(2,1)S(1)}, u32[]{:S(2)}) copy-start(bf16[512,512]{1,0:T(8,128)(2,1)S(1)} %get-tuple-element.51.refs_4_) | copy-start | bytes 1572868
  37.4 3.3 %copy-start.6 = (bf16[512,512]{1,0:T(8,128)(2,1)}, bf16[512,512]{1,0:T(8,128)(2,1)S(1)}, u32[]{:S(2)}) copy-start(bf16[512,512]{1,0:T(8,128)(2,1)S(1)} %get-tuple-element.53.refs_4_) | copy-start | bytes 1572868
  37.4 3.4 %copy-start.13 = (bf16[512,256]{1,0:T(8,128)(2,1)}, bf16[512,256]{1,0:T(8,128)(2,1)S(1)}, u32[]{:S(2)}) copy-start(bf16[512,256]{1,0:T(8,128)(2,1)S(1)} %get-tuple-element.37.refs_0_) | copy-start | bytes 786436
  37.4 3.4 %copy-start.16 = (s32[1,512]{1,0:T(1,128)}, s32[1,512]{1,0:T(1,128)S(1)}, u32[]{:S(2)}) copy-start(s32[1,512]{1,0:T(1,128)S(1)} %get-tuple-element.54.refs_5_) | copy-start | bytes 6148
  38.5 6.7 %copy-start.3 = (bf16[3,512,512]{2,1,0:T(8,128)(2,1)S(1)}, bf16[3,512,512]{2,1,0:T(8,128)(2,1)}, u32[]{:S(2)}) copy-start(bf16[3,512,512]{2,1,0:T(8,128)(2,1)} %refs_6_.3) | copy-start | bytes 4718596
  40.7 8.3 %copy-start.5 = (bf16[320,512]{1,0:T(8,128)(2,1)}, bf16[320,512]{1,0:T(8,128)(2,1)S(1)}, u32[]{:S(2)}) copy-start(bf16[320,512]{1,0:T(8,128)(2,1)S(1)} %get-tuple-element.49.refs_0_.refs_8_) | copy-start | bytes 983044
  40.7 14.6 %all-to-all-start.1 = ((bf16[16,16,512]{2,1,0:T(8,128)(2,1)}), bf16[16,16,512]{2,1,0:T(8,128)(2,1)S(1)}, u32[]{:S(2)}, u32[]{:S(2)}) async-start(bf16[16,16,512]{2,1,0:T(8,128)(2,1)} %bitcast.6), calls=%async_computation.1 | async-start | bytes 524288 | tf_op jit(solution)/shard_map/all_to_all | solution.py:456
  45.3 1.0 %copy-start.8 = (bf16[512,512]{1,0:T(8,128)(2,1)S(1)}, bf16[512,512]{1,0:T(8,128)(2,1)}, u32[]{:S(2)}) copy-start(bf16[512,512]{1,0:T(8,128)(2,1)} %copy-done.7) | copy-start | bytes 1572868
  49.0 0.8 %copy-start.9 = (bf16[512,512]{1,0:T(8,128)(2,1)}, bf16[512,512]{1,0:T(8,128)(2,1)S(1)}, u32[]{:S(2)}) copy-start(bf16[512,512]{1,0:T(8,128)(2,1)S(1)} %get-tuple-element.52.refs_2_) | copy-start | bytes 1572868
  49.8 0.7 %copy-start.10 = (bf16[320,512]{1,0:T(8,128)(2,1)}, bf16[320,512]{1,0:T(8,128)(2,1)S(1)}, u32[]{:S(2)}) copy-start(bf16[320,512]{1,0:T(8,128)(2,1)S(1)} %get-tuple-element.55.refs_7_) | copy-start | bytes 983044
  55.3 0.7 %copy-start.18 = (bf16[16,16,512]{2,1,0:T(8,128)(2,1)}, bf16[16,16,512]{2,1,0:T(8,128)(2,1)S(1)}, u32[]{:S(2)}) copy-start(bf16[16,16,512]{2,1,0:T(8,128)(2,1)S(1)} %all-to-all-done.1) | copy-start | bytes 786436

commit v4 on v3

--- a/solution.py
+++ b/solution.py
@@ -149,7 +149,7 @@
         out_shape=outs,
         scratch_shapes=held
         + [pltpu.SemaphoreType.DMA((n_in,)), pltpu.SemaphoreType.DMA((n_out * PARTS,))],
-        compiler_params=pltpu.CompilerParams(vmem_limit_bytes=room * 1024 * 1024),
+        compiler_params=pltpu.CompilerParams(vmem_limit_bytes=int(room * 1024) * 1024),
         cost_estimate=pl.CostEstimate(flops=flops, bytes_accessed=moved, transcendentals=0),
     )(*arrays)
 
@@ -172,13 +172,13 @@
         lax.broadcasted_iota(jnp.int32, (edges, edges), 0)
         < lax.broadcasted_iota(jnp.int32, (edges, edges), 1)
     )
-    for one in arriving:
-        one.ref()
     patch = patch()
     named = lax.broadcasted_iota(jnp.int32, (peers, edges), 0) == patch
     named_f = jnp.where(named, 1.0, 0.0)
     before = dot_nn(named_f.astype(BF16), earlier)
     rank = jnp.sum(named_f * before, axis=0, keepdims=True).astype(jnp.int32)
+    for one in arriving:
+        one.ref()
     place = rows_equal(slots, patch * capacity + rank)
     source = rows_equal(grid_rows, as_row(sender()))
     pick = dot_nt(place, source).astype(BF16)
@@ -202,12 +202,15 @@
     hidden = silu(dot_tn(feat(), in_w())).astype(BF16)
     latent = norm_rows(dot_nn(hidden, out_w())).astype(BF16)
     rows = dot_nn(pick, latent).astype(BF16)
-    term = dot_nn(rows, edge_w()) + dot_nn(geo, geo_w())
-    for piece in range(pieces):
-        box.held[:, piece * capacity : (piece + 1) * capacity, :] = (
-            term[:, piece * LANES : (piece + 1) * LANES].reshape(peers, capacity, LANES).astype(BF16)
-        )
-    box.send(0, peers)
+    some = peers // PARTS
+    for part in range(PARTS):
+        own = slice(part * some * capacity, (part + 1) * some * capacity)
+        term = dot_nn(rows[own], edge_w()) + dot_nn(geo[own], geo_w())
+        for piece in range(pieces):
+            box.held[part * some : (part + 1) * some, piece * capacity : (piece + 1) * capacity, :] = (
+                term[:, piece * LANES : (piece + 1) * LANES].reshape(some, capacity, LANES).astype(BF16)
+            )
+        box.send(part * some, some)
 
 
 def edge_shadow_body(arriving, leaving, *, count):
@@ -302,7 +305,7 @@
 
 def edge_values(arriving):
     far, ghosts, pre, edge_w, edges = arriving
-    preact = pre().astype(F32) + dot_nn(far(), ghosts())
+    preact = dot_nn(far(), ghosts()) + pre().astype(F32)
     return (edges().astype(F32) + tail(preact, edge_w())).astype(BF16)
 
 
@@ -474,7 +477,7 @@
             edge_operands + node_operands,
             unit * 1500,
             far_outs=True,
-            room=BIG,
+            room=53.5,
         )
     else:
         edge_out, partial_two = call(

time: 61 us -> 60 us (0.984)
  local copies, waits for them, and re-layouts: 6.23 us -> 5.52 us
    unnamed x38 -> x32, local copies, waits for them, and re-layouts: 6.23 us -> 5.52 us
where the time goes in v4:
time: 60 us; the launch traced here: 59.5 us
  Pallas kernels  19.9 us (33%)
  waiting for transfers between devices  17.6 us (29%)
  starting transfers between devices  15.6 us (26%)
  local copies, waits for them, and re-layouts  5.52 us (9%)
  between operations  0.86 us (1%)
    pallas_call x8, Pallas kernels, call(): pl.pallas_call(kernel, in_specs=[away if is_far else here for is_far in f...  19.9 us
    all_to_all x1, starting transfers between devices, per_device(): lax.all_to_all(outbox, 'patch', split_axis=0, concat_axis=0, tiled=True)  7.39 us
    ppermute x1, waiting for transfers between devices, per_device(): names.append(lax.ppermute(own_names, 'band', other))  6.22 us
    unnamed x32, local copies, waits for them, and re-layouts  5.52 us
    all_to_all x1, waiting for transfers between devices, per_device(): lax.all_to_all(outbox, 'patch', split_axis=0, concat_axis=0, tiled=True)  5.32 us
    all_to_all x1, waiting for transfers between devices, per_device(): lax.all_to_all(halo_box.reshape(peers, -1, width), 'patch', split_axis=0,...  4.84 us
    all_to_all x1, starting transfers between devices, per_device(): lax.all_to_all(halo_box.reshape(peers, -1, width), 'patch', split_axis=0,...  4.59 us
    ppermute x1, starting transfers between devices, per_device(): totals = [partial_value, lax.ppermute(partial_value, 'band', other)]  1.57 us
  transfers between devices with their start and end apart: 5, of which 4 were waited for; matrix products, arithmetic and copies ran while one was open for 0% of the time, Pallas kernels for 13%

profile of v4, /device:TPU:0, one launch (start us, length us, event | category | flops | bytes accessed | tf_op | source)
XLA Modules:
  0.0 59.5 jit_solution(7311867458316643168)
XLA Ops:
  0.6 0.0 copy-start.13
  0.6 0.0 copy-start.14
  0.7 0.0 copy-start.1
  0.7 0.0 copy-start.4
  0.7 4.1 %shard_map.176 = bf16[16,136,128]{2,1,0:T(8,128)(2,1)} custom-call(s32[1,384]{1,0:T(1,128)} %bitcast.15, s32[3,128]{1,0:T(4,128)} %bitcast.13, bf16[4,384]{1,0:T(4,128)(2,1)} %refs_2_.4, s32[3,128]{1,0:T(4,128)} %bitcast.14, bf16[474,256]{1,0:T(8,128)(2,1)} %bitcast.12, bf16[474,512]{1,0:T(8,128)(2,1)} %refs_5_.3, bf16[512,512]{1,0:T(8,128)(2,1)} %refs_6_.2, ...), custom_call_target="tpu_custom_call" | custom-call | flops 786432000 | bytes 1788416 | tf_op jit(solution)/shard_map/pallas_call | solution.py:145
  4.8 7.4 %all-to-all-start = ((bf16[16,136,128]{2,1,0:T(8,128)(2,1)}), bf16[16,136,128]{2,1,0:T(8,128)(2,1)S(1)}, u32[]{:S(2)}, u32[]{:S(2)}) async-start(bf16[16,136,128]{2,1,0:T(8,128)(2,1)} %shard_map.176), calls=%async_computation | async-start | bytes 1114112 | tf_op jit(solution)/shard_map/all_to_all | solution.py:396
  12.2 0.0 copy-done.13
  12.2 0.0 copy-done.14
  12.2 1.6 %collective-permute-start = (bf16[256,512]{1,0:T(8,128)(2,1)}, bf16[256,512]{1,0:T(8,128)(2,1)S(1)}, u32[]{:S(2)}, u32[]{:S(2)}) collective-permute-start(bf16[256,512]{1,0:T(8,128)(2,1)} %refs_0_.2), channel_id=1, source_target_pairs={{0,16},{16,0},{1,17},{17,1},{2,18},{18,2},{3,19},{19,3},{4,20},{20... | collective-permute-start | bytes 786440 | tf_op jit(solution)/shard_map/ppermute | solution.py:404
  13.8 0.5 collective-permute-start.1
  14.3 0.6 %shard_map.177.refs_1_ = bf16[832,512]{1,0:T(8,128)(2,1)S(1)} custom-call(bf16[320,512]{1,0:T(8,128)(2,1)S(1)} %copy-done.4, bf16[3,512,512]{2,1,0:T(8,128)(2,1)S(1)} %copy-done.1, bf16[3,512,512]{2,1,0:T(8,128)(2,1)S(1)} %copy-done.1), custom_call_target="tpu_custom_call" | custom-call | flops 167772160 | bytes 1376256 | tf_op jit(solution)/shard_map/pallas_call | solution.py:145
  15.0 0.0 copy-start.15
  15.0 6.2 %collective-permute-done.1.refs_4_ = s32[2,256]{1,0:T(2,128)S(1)} collective-permute-done((s32[2,256]{1,0:T(2,128)S(1)}, s32[2,256]{1,0:T(2,128)S(1)}, u32[]{:S(2)}, u32[]{:S(2)}) %collective-permute-start.1) | collective-permute-done | bytes 2080 | tf_op jit(solution)/shard_map/ppermute | solution.py:405
  21.2 0.0 collective-permute-done.refs_1_
  21.2 0.7 %copy-done.11 = bf16[256,512]{1,0:T(8,128)(2,1)} copy-done((bf16[256,512]{1,0:T(8,128)(2,1)}, bf16[256,512]{1,0:T(8,128)(2,1)S(1)}, u32[]{:S(2)}) %copy-start.11) | copy-done | bytes 262168
  21.9 5.3 %all-to-all-done.refs_0_ = bf16[16,136,128]{2,1,0:T(8,128)(2,1)S(1)} async-done(((bf16[16,136,128]{2,1,0:T(8,128)(2,1)}), bf16[16,136,128]{2,1,0:T(8,128)(2,1)S(1)}, u32[]{:S(2)}, u32[]{:S(2)}) %all-to-all-start) | async-done | bytes 557088 | tf_op jit(solution)/shard_map/all_to_all | solution.py:396
  27.2 1.4 %shard_map.178.refs_0_ = bf16[320,512]{1,0:T(8,128)(2,1)S(1)} custom-call(bf16[16,136,128]{2,1,0:T(8,128)(2,1)S(1)} %all-to-all-done.refs_0_, bf16[832,512]{1,0:T(8,128)(2,1)S(1)} %shard_map.177.refs_1_), custom_call_target="tpu_custom_call" | custom-call | flops 629145600 | bytes 1409024 | tf_op jit(solution)/shard_map/pallas_call | solution.py:145
  28.6 0.0 copy-start
  28.6 1.6 %collective-permute-start.2 = (bf16[320,512]{1,0:T(8,128)(2,1)S(1)}, bf16[320,512]{1,0:T(8,128)(2,1)S(1)}, u32[]{:S(2)}, u32[]{:S(2)}) collective-permute-start(bf16[320,512]{1,0:T(8,128)(2,1)S(1)} %shard_map.178.refs_0_), channel_id=1, source_target_pairs={{0,16},{16,0},{1,17},{17,1},{2,18},{18,2},{3,19},{19,3},{4,20},{20... | collective-permute-start | bytes 983048 | tf_op jit(solution)/shard_map/ppermute | solution.py:441
  30.2 1.4 %copy-done.2 = bf16[3,512,512]{2,1,0:T(8,128)(2,1)S(1)} copy-done((bf16[3,512,512]{2,1,0:T(8,128)(2,1)S(1)}, bf16[3,512,512]{2,1,0:T(8,128)(2,1)}, u32[]{:S(2)}) %copy-start.2) | copy-done | bytes 1572888
  31.6 1.5 %shard_map.180 = (bf16[320,512]{1,0:T(8,128)(2,1)S(1)}, bf16[256,320]{1,0:T(8,128)(2,1)S(1)}, bf16[320,512]{1,0:T(8,128)(2,1)S(1)}, bf16[2,512,512]{2,1,0:T(8,128)(2,1)S(1)}, bf16[512,512]{1,0:T(8,128)(2,1)S(1)}) custom-call(s32[1,256]{1,0:T(1,128)S(1)} %copy-done.15, bf16[320,512]{1,0:T(8,128)(2,1)S(1)} %copy-done.4, bf16[3,512,512]{2,1,0:T(8,128)(2,1)S(1)} %copy-done.2, ...), custom_call_target="tpu_custom_call" | custom-call | flops 167772160 | bytes 2425856 | tf_op jit(solution)/shard_map/pallas_call | solution.py:145
  33.1 3.2 %shard_map.179 = (bf16[512,512]{1,0:T(8,128)(2,1)S(1)}, bf16[512,512]{1,0:T(8,128)(2,1)S(1)}, bf16[512,640]{1,0:T(8,128)(2,1)S(1)}, bf16[512,256]{1,0:T(8,128)(2,1)S(1)}, s32[1,512]{1,0:T(1,128)S(1)}) custom-call(bf16[256,512]{1,0:T(8,128)(2,1)} %refs_0_.2, bf16[256,512]{1,0:T(8,128)(2,1)S(1)} %copy-done.12, s32[1,256]{1,0:T(1,128)S(1)} %bitcast.9, ...), custom_call_target="tpu_custom_call" | custom-call | flops 268435456 | bytes 1052672 | tf_op jit(solution)/shard_map/pallas_call | solution.py:145
  36.3 0.8 %copy-done.7 = bf16[512,512]{1,0:T(8,128)(2,1)} copy-done((bf16[512,512]{1,0:T(8,128)(2,1)}, bf16[512,512]{1,0:T(8,128)(2,1)S(1)}, u32[]{:S(2)}) %copy-start.7) | copy-done | bytes 524312
  37.1 1.2 %collective-permute-done.2.refs_1_ = bf16[320,512]{1,0:T(8,128)(2,1)S(1)} collective-permute-done((bf16[320,512]{1,0:T(8,128)(2,1)S(1)}, bf16[320,512]{1,0:T(8,128)(2,1)S(1)}, u32[]{:S(2)}, u32[]{:S(2)}) %collective-permute-start.2) | collective-permute-done | bytes 327712 | tf_op jit(solution)/shard_map/ppermute | solution.py:441
  38.3 2.1 %shard_map.181 = (bf16[320,512]{1,0:T(8,128)(2,1)S(1)}, bf16[256,512]{1,0:T(8,128)(2,1)}) custom-call(bf16[320,512]{1,0:T(8,128)(2,1)S(1)} %shard_map.178.refs_0_, bf16[320,512]{1,0:T(8,128)(2,1)S(1)} %collective-permute-done.2.refs_1_, bf16[320,512]{1,0:T(8,128)(2,1)S(1)} %get-tuple-element.41.refs_2_, bf16[320,512]{1,0:T(8,128)(2,1)S(1)} %get-tuple-element.44.refs_3_, ...), custom_call_target="tpu_custom_call" | custom-call | flops 524288000 | bytes 3047424 | tf_op jit(solution)/shard_map/pallas_call | solution.py:145
  40.5 4.6 %all-to-all-start.1 = ((bf16[16,16,512]{2,1,0:T(8,128)(2,1)}), bf16[16,16,512]{2,1,0:T(8,128)(2,1)}, u32[]{:S(2)}, u32[]{:S(2)}) async-start(bf16[16,16,512]{2,1,0:T(8,128)(2,1)} %bitcast.6), calls=%async_computation.1 | async-start | bytes 524288 | tf_op jit(solution)/shard_map/all_to_all | solution.py:459
  45.1 1.0 %copy-done.8 = bf16[512,512]{1,0:T(8,128)(2,1)S(1)} copy-done((bf16[512,512]{1,0:T(8,128)(2,1)S(1)}, bf16[512,512]{1,0:T(8,128)(2,1)}, u32[]{:S(2)}) %copy-start.8) | copy-done | bytes 524312
  46.1 2.7 %shard_map.182 = (bf16[512,512]{1,0:T(8,128)(2,1)S(1)}, bf16[320,512]{1,0:T(8,128)(2,1)S(1)}) custom-call(bf16[320,512]{1,0:T(8,128)(2,1)S(1)} %get-tuple-element.49.refs_0_.refs_8_, bf16[512,512]{1,0:T(8,128)(2,1)S(1)} %get-tuple-element.47.refs_6_.refs_1_, bf16[4,512,512]{2,1,0:T(8,128)(2,1)} %refs_3_.3, bf16[512,640]{1,0:T(8,128)(2,1)S(1)} %get-tuple-element.50.refs_3_, ...), custom_call_target="tpu_custom_call" | custom-call | flops 786432000 | bytes 3080192 | tf_op jit(solution)/shard_map/pallas_call | solution.py:145
  48.8 0.8 %copy-done.9 = bf16[512,512]{1,0:T(8,128)(2,1)} copy-done((bf16[512,512]{1,0:T(8,128)(2,1)}, bf16[512,512]{1,0:T(8,128)(2,1)S(1)}, u32[]{:S(2)}) %copy-start.9) | copy-done | bytes 524312
  49.6 0.7 %copy-done.10 = bf16[320,512]{1,0:T(8,128)(2,1)} copy-done((bf16[320,512]{1,0:T(8,128)(2,1)}, bf16[320,512]{1,0:T(8,128)(2,1)S(1)}, u32[]{:S(2)}) %copy-start.10) | copy-done | bytes 327704
  50.3 4.8 %all-to-all-done.1 = bf16[16,16,512]{2,1,0:T(8,128)(2,1)} async-done(((bf16[16,16,512]{2,1,0:T(8,128)(2,1)}), bf16[16,16,512]{2,1,0:T(8,128)(2,1)}, u32[]{:S(2)}, u32[]{:S(2)}) %all-to-all-start.1) | async-done | bytes 262176 | tf_op jit(solution)/shard_map/all_to_all | solution.py:459
  55.2 4.3 %shard_map.183 = (bf16[256,512]{1,0:T(8,128)(2,1)}, bf16[320,512]{1,0:T(8,128)(2,1)}) custom-call(bf16[512,256]{1,0:T(8,128)(2,1)S(1)} %get-tuple-element.37.refs_0_, bf16[256,512]{1,0:T(8,128)(2,1)} %bitcast.7.refs_1_, bf16[512,512]{1,0:T(8,128)(2,1)} %copy-done.9, bf16[4,512,512]{2,1,0:T(8,128)(2,1)} %refs_3_.3, bf16[512,512]{1,0:T(8,128)(2,1)} %copy-done.6, ...), custom_call_target="tpu_custom_call" | custom-call | flops 786432000 | bytes 3803136 | tf_op jit(solution)/shard_map/pallas_call | solution.py:145
  (19 shorter events, 0.0 us)
Async XLA Ops:
  0.6 11.6 %copy-start.13 = (s32[256]{0:T(256)S(1)}, s32[256]{0:T(256)}, u32[]{:S(2)}) copy-start(s32[256]{0:T(256)} %param.24) | copy-start | bytes 3076
  0.6 11.6 %copy-start.14 = (s32[256]{0:T(256)S(1)}, s32[256]{0:T(256)}, u32[]{:S(2)}) copy-start(s32[256]{0:T(256)} %param.25) | copy-start | bytes 3076
  0.7 13.7 %copy-start.1 = (bf16[3,512,512]{2,1,0:T(8,128)(2,1)S(1)}, bf16[3,512,512]{2,1,0:T(8,128)(2,1)}, u32[]{:S(2)}) copy-start(bf16[3,512,512]{2,1,0:T(8,128)(2,1)} %refs_2_.5) | copy-start | bytes 4718596
  0.7 13.7 %copy-start.4 = (bf16[320,512]{1,0:T(8,128)(2,1)S(1)}, bf16[320,512]{1,0:T(8,128)(2,1)}, u32[]{:S(2)}) copy-start(bf16[320,512]{1,0:T(8,128)(2,1)} %refs_1_.2) | copy-start | bytes 983044
  4.8 22.4 %all-to-all-start = ((bf16[16,136,128]{2,1,0:T(8,128)(2,1)}), bf16[16,136,128]{2,1,0:T(8,128)(2,1)S(1)}, u32[]{:S(2)}, u32[]{:S(2)}) async-start(bf16[16,136,128]{2,1,0:T(8,128)(2,1)} %shard_map.176), calls=%async_computation | async-start | bytes 1114112 | tf_op jit(solution)/shard_map/all_to_all | solution.py:396
  12.2 9.0 %collective-permute-start = (bf16[256,512]{1,0:T(8,128)(2,1)}, bf16[256,512]{1,0:T(8,128)(2,1)S(1)}, u32[]{:S(2)}, u32[]{:S(2)}) collective-permute-start(bf16[256,512]{1,0:T(8,128)(2,1)} %refs_0_.2), channel_id=1, source_target_pairs={{0,16},{16,0},{1,17},{17,1},{2,18},{18,2},{3,19},{19,3},{4,20},{20... | collective-permute-start | bytes 786440 | tf_op jit(solution)/shard_map/ppermute | solution.py:404
  13.8 7.4 %collective-permute-start.1 = (s32[2,256]{1,0:T(2,128)S(1)}, s32[2,256]{1,0:T(2,128)S(1)}, u32[]{:S(2)}, u32[]{:S(2)}) collective-permute-start(s32[2,256]{1,0:T(2,128)S(1)} %pad_add_fusion), channel_id=1, source_target_pairs={{0,16},{16,0},{1,17},{17,1},{2,18},{18,2},{3,19},{19,3},{4,20},{20... | collective-permute-start | bytes 6152 | tf_op jit(solution)/shard_map/ppermute | solution.py:405
  15.0 15.2 %copy-start.15 = (s32[1,256]{1,0:T(1,128)S(1)}, s32[1,256]{1,0:T(1,128)}, u32[]{:S(2)}) copy-start(s32[1,256]{1,0:T(1,128)} %refs_0_.3) | copy-start | bytes 3076
  21.2 0.7 %copy-start.11 = (bf16[256,512]{1,0:T(8,128)(2,1)}, bf16[256,512]{1,0:T(8,128)(2,1)S(1)}, u32[]{:S(2)}) copy-start(bf16[256,512]{1,0:T(8,128)(2,1)S(1)} %collective-permute-done.refs_1_) | copy-start | bytes 786436
  28.6 4.5 %copy-start = (bf16[4,512,512]{2,1,0:T(8,128)(2,1)S(1)}, bf16[4,512,512]{2,1,0:T(8,128)(2,1)}, u32[]{:S(2)}) copy-start(bf16[4,512,512]{2,1,0:T(8,128)(2,1)} %refs_3_.3) | copy-start | bytes 6291460
  28.6 9.7 %collective-permute-start.2 = (bf16[320,512]{1,0:T(8,128)(2,1)S(1)}, bf16[320,512]{1,0:T(8,128)(2,1)S(1)}, u32[]{:S(2)}, u32[]{:S(2)}) collective-permute-start(bf16[320,512]{1,0:T(8,128)(2,1)S(1)} %shard_map.178.refs_0_), channel_id=1, source_target_pairs={{0,16},{16,0},{1,17},{17,1},{2,18},{18,2},{3,19},{19,3},{4,20},{20... | collective-permute-start | bytes 983048 | tf_op jit(solution)/shard_map/ppermute | solution.py:441
  30.2 1.4 %copy-start.2 = (bf16[3,512,512]{2,1,0:T(8,128)(2,1)S(1)}, bf16[3,512,512]{2,1,0:T(8,128)(2,1)}, u32[]{:S(2)}) copy-start(bf16[3,512,512]{2,1,0:T(8,128)(2,1)} %refs_3_.2) | copy-start | bytes 4718596
  31.6 1.5 %copy-start.12 = (bf16[256,512]{1,0:T(8,128)(2,1)S(1)}, bf16[256,512]{1,0:T(8,128)(2,1)}, u32[]{:S(2)}) copy-start(bf16[256,512]{1,0:T(8,128)(2,1)} %copy-done.11) | copy-start | bytes 786436
  36.3 0.8 %copy-start.7 = (bf16[512,512]{1,0:T(8,128)(2,1)}, bf16[512,512]{1,0:T(8,128)(2,1)S(1)}, u32[]{:S(2)}) copy-start(bf16[512,512]{1,0:T(8,128)(2,1)S(1)} %get-tuple-element.51.refs_4_) | copy-start | bytes 1572868
  37.1 3.3 %copy-start.6 = (bf16[512,512]{1,0:T(8,128)(2,1)}, bf16[512,512]{1,0:T(8,128)(2,1)S(1)}, u32[]{:S(2)}) copy-start(bf16[512,512]{1,0:T(8,128)(2,1)S(1)} %get-tuple-element.53.refs_4_) | copy-start | bytes 1572868
  38.3 6.8 %copy-start.3 = (bf16[3,512,512]{2,1,0:T(8,128)(2,1)S(1)}, bf16[3,512,512]{2,1,0:T(8,128)(2,1)}, u32[]{:S(2)}) copy-start(bf16[3,512,512]{2,1,0:T(8,128)(2,1)} %refs_6_.3) | copy-start | bytes 4718596
  40.5 8.3 %copy-start.5 = (bf16[320,512]{1,0:T(8,128)(2,1)}, bf16[320,512]{1,0:T(8,128)(2,1)S(1)}, u32[]{:S(2)}) copy-start(bf16[320,512]{1,0:T(8,128)(2,1)S(1)} %get-tuple-element.49.refs_0_.refs_8_) | copy-start | bytes 983044
  40.5 14.7 %all-to-all-start.1 = ((bf16[16,16,512]{2,1,0:T(8,128)(2,1)}), bf16[16,16,512]{2,1,0:T(8,128)(2,1)}, u32[]{:S(2)}, u32[]{:S(2)}) async-start(bf16[16,16,512]{2,1,0:T(8,128)(2,1)} %bitcast.6), calls=%async_computation.1 | async-start | bytes 524288 | tf_op jit(solution)/shard_map/all_to_all | solution.py:459
  45.1 1.0 %copy-start.8 = (bf16[512,512]{1,0:T(8,128)(2,1)S(1)}, bf16[512,512]{1,0:T(8,128)(2,1)}, u32[]{:S(2)}) copy-start(bf16[512,512]{1,0:T(8,128)(2,1)} %copy-done.7) | copy-start | bytes 1572868
  48.8 0.8 %copy-start.9 = (bf16[512,512]{1,0:T(8,128)(2,1)}, bf16[512,512]{1,0:T(8,128)(2,1)S(1)}, u32[]{:S(2)}) copy-start(bf16[512,512]{1,0:T(8,128)(2,1)S(1)} %get-tuple-element.52.refs_2_) | copy-start | bytes 1572868
  49.6 0.7 %copy-start.10 = (bf16[320,512]{1,0:T(8,128)(2,1)}, bf16[320,512]{1,0:T(8,128)(2,1)S(1)}, u32[]{:S(2)}) copy-start(bf16[320,512]{1,0:T(8,128)(2,1)S(1)} %get-tuple-element.55.refs_7_) | copy-start | bytes 983044

commit v5 on v4

--- a/solution.py
+++ b/solution.py
@@ -159,7 +159,7 @@
 
 
 def embed_body(arriving, leaving):
-    patch, sender, geo, node, feat, in_w, out_w, edge_w, geo_w = arriving
+    in_w, out_w, edge_w, feat, patch, sender, geo, node, geo_w = arriving
     (box,) = leaving
     peers, box_rows, _ = box.shape
     edges = patch.held.shape[1]
@@ -377,18 +377,17 @@
     matrix, pair = shape((width, width)), shape((2, width, width))
     node_like, edge_like = shape((mesh_count, width)), shape((medge_count, width))
     sources = [
+        grid_feat.T,
         enc_patch.reshape(1, -1),
         enc_sender.reshape(-1, LANES),
         enc_geo,
         enc_node.reshape(-1, LANES),
-        grid_feat.T,
-        grid_in,
-        grid_out,
+        geo_weight,
     ]
     (outbox,) = call(
         embed_body,
         [shape((peers, pieces * capacity + address_rows, LANES))],
-        [Far(source) for source in sources] + [Far(enc_edge_w, 0), Far(geo_weight)],
+        [Far(grid_in), Far(grid_out), Far(enc_edge_w, 0)] + [Far(source) for source in sources],
         unit * 1500,
         far_outs=True,
         room=BIG,

time: 60 us -> 59.9 us (level)
  no operation moved by 1% of the time
where the time goes in v5:
time: 59.9 us; the launch traced here: 59.4 us
  Pallas kernels  19.8 us (33%)
  waiting for transfers between devices  17.6 us (29%)
  starting transfers between devices  15.6 us (26%)
  local copies, waits for them, and re-layouts  5.52 us (9%)
  between operations  0.86 us (1%)
    pallas_call x8, Pallas kernels, call(): pl.pallas_call(kernel, in_specs=[away if is_far else here for is_far in f...  19.8 us
    all_to_all x1, starting transfers between devices, per_device(): lax.all_to_all(outbox, 'patch', split_axis=0, concat_axis=0, tiled=True)  7.4 us
    ppermute x1, waiting for transfers between devices, per_device(): names.append(lax.ppermute(own_names, 'band', other))  6.22 us
    unnamed x32, local copies, waits for them, and re-layouts  5.52 us
    all_to_all x1, waiting for transfers between devices, per_device(): lax.all_to_all(outbox, 'patch', split_axis=0, concat_axis=0, tiled=True)  5.32 us
    all_to_all x1, waiting for transfers between devices, per_device(): lax.all_to_all(halo_box.reshape(peers, -1, width), 'patch', split_axis=0,...  4.84 us
    all_to_all x1, starting transfers between devices, per_device(): lax.all_to_all(halo_box.reshape(peers, -1, width), 'patch', split_axis=0,...  4.58 us
    ppermute x1, starting transfers between devices, per_device(): edge_parts.append(lax.ppermute(own_edge, 'band', other))  1.56 us
  transfers between devices with their start and end apart: 5, of which 4 were waited for; matrix products, arithmetic and copies ran while one was open for 0% of the time, Pallas kernels for 13%

profile of v5, /device:TPU:0, one launch (start us, length us, event | category | flops | bytes accessed | tf_op | source)
XLA Modules:
  0.0 59.4 jit_solution(13793719556559076580)
XLA Ops:
  0.7 4.0 %shard_map.176 = bf16[16,136,128]{2,1,0:T(8,128)(2,1)} custom-call(bf16[474,512]{1,0:T(8,128)(2,1)} %refs_0_.2, bf16[512,512]{1,0:T(8,128)(2,1)} %refs_1_.2, bf16[3,512,512]{2,1,0:T(8,128)(2,1)} %refs_2_.5, bf16[474,256]{1,0:T(8,128)(2,1)} %bitcast.12, s32[1,384]{1,0:T(1,128)} %bitcast.15, s32[3,128]{1,0:T(4,128)} %bitcast.13, bf16[4,384]{1,0:T(4,128)(2,1)} %refs_6_.2, ...), custom_call_target="tpu_custom_call" | custom-call | flops 786432000 | bytes 1788416 | tf_op jit(solution)/shard_map/pallas_call | solution.py:145
  4.7 7.4 %all-to-all-start = ((bf16[16,136,128]{2,1,0:T(8,128)(2,1)}), bf16[16,136,128]{2,1,0:T(8,128)(2,1)S(1)}, u32[]{:S(2)}, u32[]{:S(2)}) async-start(bf16[16,136,128]{2,1,0:T(8,128)(2,1)} %shard_map.176), calls=%async_computation | async-start | bytes 1114112 | tf_op jit(solution)/shard_map/all_to_all | solution.py:395
  12.1 1.6 %collective-permute-start = (bf16[256,512]{1,0:T(8,128)(2,1)}, bf16[256,512]{1,0:T(8,128)(2,1)S(1)}, u32[]{:S(2)}, u32[]{:S(2)}) collective-permute-start(bf16[256,512]{1,0:T(8,128)(2,1)} %refs_0_.4), channel_id=1, source_target_pairs={{0,16},{16,0},{1,17},{17,1},{2,18},{18,2},{3,19},{19,3},{4,20},{20... | collective-permute-start | bytes 786440 | tf_op jit(solution)/shard_map/ppermute | solution.py:403
  13.7 0.5 collective-permute-start.1
  14.2 0.6 %shard_map.177.refs_1_ = bf16[832,512]{1,0:T(8,128)(2,1)S(1)} custom-call(bf16[320,512]{1,0:T(8,128)(2,1)S(1)} %copy-done.4, bf16[3,512,512]{2,1,0:T(8,128)(2,1)S(1)} %copy-done.1, bf16[3,512,512]{2,1,0:T(8,128)(2,1)S(1)} %copy-done.1), custom_call_target="tpu_custom_call" | custom-call | flops 167772160 | bytes 1376256 | tf_op jit(solution)/shard_map/pallas_call | solution.py:145
  14.8 0.0 copy-start.15
  14.9 6.2 %collective-permute-done.1.refs_4_ = s32[2,256]{1,0:T(2,128)S(1)} collective-permute-done((s32[2,256]{1,0:T(2,128)S(1)}, s32[2,256]{1,0:T(2,128)S(1)}, u32[]{:S(2)}, u32[]{:S(2)}) %collective-permute-start.1) | collective-permute-done | bytes 2080 | tf_op jit(solution)/shard_map/ppermute | solution.py:404
  21.1 0.0 collective-permute-done.refs_1_
  21.1 0.7 %copy-done.11 = bf16[256,512]{1,0:T(8,128)(2,1)} copy-done((bf16[256,512]{1,0:T(8,128)(2,1)}, bf16[256,512]{1,0:T(8,128)(2,1)S(1)}, u32[]{:S(2)}) %copy-start.11) | copy-done | bytes 262168
  21.8 5.3 %all-to-all-done.refs_0_ = bf16[16,136,128]{2,1,0:T(8,128)(2,1)S(1)} async-done(((bf16[16,136,128]{2,1,0:T(8,128)(2,1)}), bf16[16,136,128]{2,1,0:T(8,128)(2,1)S(1)}, u32[]{:S(2)}, u32[]{:S(2)}) %all-to-all-start) | async-done | bytes 557088 | tf_op jit(solution)/shard_map/all_to_all | solution.py:395
  27.1 1.4 %shard_map.178.refs_0_ = bf16[320,512]{1,0:T(8,128)(2,1)S(1)} custom-call(bf16[16,136,128]{2,1,0:T(8,128)(2,1)S(1)} %all-to-all-done.refs_0_, bf16[832,512]{1,0:T(8,128)(2,1)S(1)} %shard_map.177.refs_1_), custom_call_target="tpu_custom_call" | custom-call | flops 629145600 | bytes 1409024 | tf_op jit(solution)/shard_map/pallas_call | solution.py:145
  28.5 0.0 copy-start
  28.5 1.6 %collective-permute-start.2 = (bf16[320,512]{1,0:T(8,128)(2,1)S(1)}, bf16[320,512]{1,0:T(8,128)(2,1)S(1)}, u32[]{:S(2)}, u32[]{:S(2)}) collective-permute-start(bf16[320,512]{1,0:T(8,128)(2,1)S(1)} %shard_map.178.refs_0_), channel_id=1, source_target_pairs={{0,16},{16,0},{1,17},{17,1},{2,18},{18,2},{3,19},{19,3},{4,20},{20... | collective-permute-start | bytes 983048 | tf_op jit(solution)/shard_map/ppermute | solution.py:440
  30.1 1.4 %copy-done.2 = bf16[3,512,512]{2,1,0:T(8,128)(2,1)S(1)} copy-done((bf16[3,512,512]{2,1,0:T(8,128)(2,1)S(1)}, bf16[3,512,512]{2,1,0:T(8,128)(2,1)}, u32[]{:S(2)}) %copy-start.2) | copy-done | bytes 1572888
  31.5 1.5 %shard_map.180 = (bf16[320,512]{1,0:T(8,128)(2,1)S(1)}, bf16[256,320]{1,0:T(8,128)(2,1)S(1)}, bf16[320,512]{1,0:T(8,128)(2,1)S(1)}, bf16[2,512,512]{2,1,0:T(8,128)(2,1)S(1)}, bf16[512,512]{1,0:T(8,128)(2,1)S(1)}) custom-call(s32[1,256]{1,0:T(1,128)S(1)} %copy-done.15, bf16[320,512]{1,0:T(8,128)(2,1)S(1)} %copy-done.4, bf16[3,512,512]{2,1,0:T(8,128)(2,1)S(1)} %copy-done.2, ...), custom_call_target="tpu_custom_call" | custom-call | flops 167772160 | bytes 2425856 | tf_op jit(solution)/shard_map/pallas_call | solution.py:145
  33.0 0.0 copy-done
  33.0 0.0 copy-done.12
  33.0 3.2 %shard_map.179 = (bf16[512,512]{1,0:T(8,128)(2,1)S(1)}, bf16[512,512]{1,0:T(8,128)(2,1)S(1)}, bf16[512,640]{1,0:T(8,128)(2,1)S(1)}, bf16[512,256]{1,0:T(8,128)(2,1)S(1)}, s32[1,512]{1,0:T(1,128)S(1)}) custom-call(bf16[256,512]{1,0:T(8,128)(2,1)} %refs_0_.4, bf16[256,512]{1,0:T(8,128)(2,1)S(1)} %copy-done.12, s32[1,256]{1,0:T(1,128)S(1)} %bitcast.9, ...), custom_call_target="tpu_custom_call" | custom-call | flops 268435456 | bytes 1052672 | tf_op jit(solution)/shard_map/pallas_call | solution.py:145
  36.2 0.0 copy-start.7
  36.2 0.8 %copy-done.7 = bf16[512,512]{1,0:T(8,128)(2,1)} copy-done((bf16[512,512]{1,0:T(8,128)(2,1)}, bf16[512,512]{1,0:T(8,128)(2,1)S(1)}, u32[]{:S(2)}) %copy-start.7) | copy-done | bytes 524312
  37.0 1.2 %collective-permute-done.2.refs_1_ = bf16[320,512]{1,0:T(8,128)(2,1)S(1)} collective-permute-done((bf16[320,512]{1,0:T(8,128)(2,1)S(1)}, bf16[320,512]{1,0:T(8,128)(2,1)S(1)}, u32[]{:S(2)}, u32[]{:S(2)}) %collective-permute-start.2) | collective-permute-done | bytes 327712 | tf_op jit(solution)/shard_map/ppermute | solution.py:440
  38.2 2.1 %shard_map.181 = (bf16[320,512]{1,0:T(8,128)(2,1)S(1)}, bf16[256,512]{1,0:T(8,128)(2,1)}) custom-call(bf16[320,512]{1,0:T(8,128)(2,1)S(1)} %shard_map.178.refs_0_, bf16[320,512]{1,0:T(8,128)(2,1)S(1)} %collective-permute-done.2.refs_1_, bf16[320,512]{1,0:T(8,128)(2,1)S(1)} %get-tuple-element.41.refs_2_, bf16[320,512]{1,0:T(8,128)(2,1)S(1)} %get-tuple-element.44.refs_3_, ...), custom_call_target="tpu_custom_call" | custom-call | flops 524288000 | bytes 3047424 | tf_op jit(solution)/shard_map/pallas_call | solution.py:145
  40.3 0.0 copy-done.6
  40.3 0.0 copy-start.5
  40.4 4.6 %all-to-all-start.1 = ((bf16[16,16,512]{2,1,0:T(8,128)(2,1)}), bf16[16,16,512]{2,1,0:T(8,128)(2,1)}, u32[]{:S(2)}, u32[]{:S(2)}) async-start(bf16[16,16,512]{2,1,0:T(8,128)(2,1)} %bitcast.6), calls=%async_computation.1 | async-start | bytes 524288 | tf_op jit(solution)/shard_map/all_to_all | solution.py:458
  45.0 1.0 %copy-done.8 = bf16[512,512]{1,0:T(8,128)(2,1)S(1)} copy-done((bf16[512,512]{1,0:T(8,128)(2,1)S(1)}, bf16[512,512]{1,0:T(8,128)(2,1)}, u32[]{:S(2)}) %copy-start.8) | copy-done | bytes 524312
  46.0 2.7 %shard_map.182 = (bf16[512,512]{1,0:T(8,128)(2,1)S(1)}, bf16[320,512]{1,0:T(8,128)(2,1)S(1)}) custom-call(bf16[320,512]{1,0:T(8,128)(2,1)S(1)} %get-tuple-element.49.refs_0_.refs_8_, bf16[512,512]{1,0:T(8,128)(2,1)S(1)} %get-tuple-element.47.refs_6_.refs_1_, bf16[4,512,512]{2,1,0:T(8,128)(2,1)} %refs_3_.3, bf16[512,640]{1,0:T(8,128)(2,1)S(1)} %get-tuple-element.50.refs_3_, ...), custom_call_target="tpu_custom_call" | custom-call | flops 786432000 | bytes 3080192 | tf_op jit(solution)/shard_map/pallas_call | solution.py:145
  48.7 0.0 copy-done.5
  48.7 0.8 %copy-done.9 = bf16[512,512]{1,0:T(8,128)(2,1)} copy-done((bf16[512,512]{1,0:T(8,128)(2,1)}, bf16[512,512]{1,0:T(8,128)(2,1)S(1)}, u32[]{:S(2)}) %copy-start.9) | copy-done | bytes 524312
  49.5 0.7 %copy-done.10 = bf16[320,512]{1,0:T(8,128)(2,1)} copy-done((bf16[320,512]{1,0:T(8,128)(2,1)}, bf16[320,512]{1,0:T(8,128)(2,1)S(1)}, u32[]{:S(2)}) %copy-start.10) | copy-done | bytes 327704
  50.2 4.8 %all-to-all-done.1 = bf16[16,16,512]{2,1,0:T(8,128)(2,1)} async-done(((bf16[16,16,512]{2,1,0:T(8,128)(2,1)}), bf16[16,16,512]{2,1,0:T(8,128)(2,1)}, u32[]{:S(2)}, u32[]{:S(2)}) %all-to-all-start.1) | async-done | bytes 262176 | tf_op jit(solution)/shard_map/all_to_all | solution.py:458
  55.0 4.3 %shard_map.183 = (bf16[256,512]{1,0:T(8,128)(2,1)}, bf16[320,512]{1,0:T(8,128)(2,1)}) custom-call(bf16[512,256]{1,0:T(8,128)(2,1)S(1)} %get-tuple-element.37.refs_0_, bf16[256,512]{1,0:T(8,128)(2,1)} %bitcast.7.refs_1_, bf16[512,512]{1,0:T(8,128)(2,1)} %copy-done.9, bf16[4,512,512]{2,1,0:T(8,128)(2,1)} %refs_3_.3, bf16[512,512]{1,0:T(8,128)(2,1)} %copy-done.6, ...), custom_call_target="tpu_custom_call" | custom-call | flops 786432000 | bytes 3803136 | tf_op jit(solution)/shard_map/pallas_call | solution.py:145
  (19 shorter events, 0.0 us)
Async XLA Ops:
  0.6 11.4 %copy-start.13 = (s32[256]{0:T(256)S(1)}, s32[256]{0:T(256)}, u32[]{:S(2)}) copy-start(s32[256]{0:T(256)} %param.24) | copy-start | bytes 3076
  0.6 11.4 %copy-start.14 = (s32[256]{0:T(256)S(1)}, s32[256]{0:T(256)}, u32[]{:S(2)}) copy-start(s32[256]{0:T(256)} %param.25) | copy-start | bytes 3076
  0.7 13.6 %copy-start.1 = (bf16[3,512,512]{2,1,0:T(8,128)(2,1)S(1)}, bf16[3,512,512]{2,1,0:T(8,128)(2,1)}, u32[]{:S(2)}) copy-start(bf16[3,512,512]{2,1,0:T(8,128)(2,1)} %refs_2_.5) | copy-start | bytes 4718596
  0.7 13.5 %copy-start.4 = (bf16[320,512]{1,0:T(8,128)(2,1)S(1)}, bf16[320,512]{1,0:T(8,128)(2,1)}, u32[]{:S(2)}) copy-start(bf16[320,512]{1,0:T(8,128)(2,1)} %refs_1_.4) | copy-start | bytes 983044
  4.7 22.4 %all-to-all-start = ((bf16[16,136,128]{2,1,0:T(8,128)(2,1)}), bf16[16,136,128]{2,1,0:T(8,128)(2,1)S(1)}, u32[]{:S(2)}, u32[]{:S(2)}) async-start(bf16[16,136,128]{2,1,0:T(8,128)(2,1)} %shard_map.176), calls=%async_computation | async-start | bytes 1114112 | tf_op jit(solution)/shard_map/all_to_all | solution.py:395
  12.1 9.0 %collective-permute-start = (bf16[256,512]{1,0:T(8,128)(2,1)}, bf16[256,512]{1,0:T(8,128)(2,1)S(1)}, u32[]{:S(2)}, u32[]{:S(2)}) collective-permute-start(bf16[256,512]{1,0:T(8,128)(2,1)} %refs_0_.4), channel_id=1, source_target_pairs={{0,16},{16,0},{1,17},{17,1},{2,18},{18,2},{3,19},{19,3},{4,20},{20... | collective-permute-start | bytes 786440 | tf_op jit(solution)/shard_map/ppermute | solution.py:403
  13.7 7.4 %collective-permute-start.1 = (s32[2,256]{1,0:T(2,128)S(1)}, s32[2,256]{1,0:T(2,128)S(1)}, u32[]{:S(2)}, u32[]{:S(2)}) collective-permute-start(s32[2,256]{1,0:T(2,128)S(1)} %pad_add_fusion), channel_id=1, source_target_pairs={{0,16},{16,0},{1,17},{17,1},{2,18},{18,2},{3,19},{19,3},{4,20},{20... | collective-permute-start | bytes 6152 | tf_op jit(solution)/shard_map/ppermute | solution.py:404
  14.8 15.2 %copy-start.15 = (s32[1,256]{1,0:T(1,128)S(1)}, s32[1,256]{1,0:T(1,128)}, u32[]{:S(2)}) copy-start(s32[1,256]{1,0:T(1,128)} %refs_0_.5) | copy-start | bytes 3076
  21.1 0.7 %copy-start.11 = (bf16[256,512]{1,0:T(8,128)(2,1)}, bf16[256,512]{1,0:T(8,128)(2,1)S(1)}, u32[]{:S(2)}) copy-start(bf16[256,512]{1,0:T(8,128)(2,1)S(1)} %collective-permute-done.refs_1_) | copy-start | bytes 786436
  28.5 4.5 %copy-start = (bf16[4,512,512]{2,1,0:T(8,128)(2,1)S(1)}, bf16[4,512,512]{2,1,0:T(8,128)(2,1)}, u32[]{:S(2)}) copy-start(bf16[4,512,512]{2,1,0:T(8,128)(2,1)} %refs_3_.3) | copy-start | bytes 6291460
  28.5 9.7 %collective-permute-start.2 = (bf16[320,512]{1,0:T(8,128)(2,1)S(1)}, bf16[320,512]{1,0:T(8,128)(2,1)S(1)}, u32[]{:S(2)}, u32[]{:S(2)}) collective-permute-start(bf16[320,512]{1,0:T(8,128)(2,1)S(1)} %shard_map.178.refs_0_), channel_id=1, source_target_pairs={{0,16},{16,0},{1,17},{17,1},{2,18},{18,2},{3,19},{19,3},{4,20},{20... | collective-permute-start | bytes 983048 | tf_op jit(solution)/shard_map/ppermute | solution.py:440
  30.0 1.4 %copy-start.2 = (bf16[3,512,512]{2,1,0:T(8,128)(2,1)S(1)}, bf16[3,512,512]{2,1,0:T(8,128)(2,1)}, u32[]{:S(2)}) copy-start(bf16[3,512,512]{2,1,0:T(8,128)(2,1)} %refs_3_.2) | copy-start | bytes 4718596
  31.5 1.5 %copy-start.12 = (bf16[256,512]{1,0:T(8,128)(2,1)S(1)}, bf16[256,512]{1,0:T(8,128)(2,1)}, u32[]{:S(2)}) copy-start(bf16[256,512]{1,0:T(8,128)(2,1)} %copy-done.11) | copy-start | bytes 786436
  36.2 0.8 %copy-start.7 = (bf16[512,512]{1,0:T(8,128)(2,1)}, bf16[512,512]{1,0:T(8,128)(2,1)S(1)}, u32[]{:S(2)}) copy-start(bf16[512,512]{1,0:T(8,128)(2,1)S(1)} %get-tuple-element.51.refs_4_) | copy-start | bytes 1572868
  37.0 3.3 %copy-start.6 = (bf16[512,512]{1,0:T(8,128)(2,1)}, bf16[512,512]{1,0:T(8,128)(2,1)S(1)}, u32[]{:S(2)}) copy-start(bf16[512,512]{1,0:T(8,128)(2,1)S(1)} %get-tuple-element.53.refs_4_) | copy-start | bytes 1572868
  38.2 6.8 %copy-start.3 = (bf16[3,512,512]{2,1,0:T(8,128)(2,1)S(1)}, bf16[3,512,512]{2,1,0:T(8,128)(2,1)}, u32[]{:S(2)}) copy-start(bf16[3,512,512]{2,1,0:T(8,128)(2,1)} %refs_6_.3) | copy-start | bytes 4718596
  40.3 8.3 %copy-start.5 = (bf16[320,512]{1,0:T(8,128)(2,1)}, bf16[320,512]{1,0:T(8,128)(2,1)S(1)}, u32[]{:S(2)}) copy-start(bf16[320,512]{1,0:T(8,128)(2,1)S(1)} %get-tuple-element.49.refs_0_.refs_8_) | copy-start | bytes 983044
  40.4 14.7 %all-to-all-start.1 = ((bf16[16,16,512]{2,1,0:T(8,128)(2,1)}), bf16[16,16,512]{2,1,0:T(8,128)(2,1)}, u32[]{:S(2)}, u32[]{:S(2)}) async-start(bf16[16,16,512]{2,1,0:T(8,128)(2,1)} %bitcast.6), calls=%async_computation.1 | async-start | bytes 524288 | tf_op jit(solution)/shard_map/all_to_all | solution.py:458
  45.0 1.0 %copy-start.8 = (bf16[512,512]{1,0:T(8,128)(2,1)S(1)}, bf16[512,512]{1,0:T(8,128)(2,1)}, u32[]{:S(2)}) copy-start(bf16[512,512]{1,0:T(8,128)(2,1)} %copy-done.7) | copy-start | bytes 1572868
  48.7 0.8 %copy-start.9 = (bf16[512,512]{1,0:T(8,128)(2,1)}, bf16[512,512]{1,0:T(8,128)(2,1)S(1)}, u32[]{:S(2)}) copy-start(bf16[512,512]{1,0:T(8,128)(2,1)S(1)} %get-tuple-element.52.refs_2_) | copy-start | bytes 1572868
  49.5 0.7 %copy-start.10 = (bf16[320,512]{1,0:T(8,128)(2,1)}, bf16[320,512]{1,0:T(8,128)(2,1)S(1)}, u32[]{:S(2)}) copy-start(bf16[320,512]{1,0:T(8,128)(2,1)S(1)} %get-tuple-element.55.refs_7_) | copy-start | bytes 983044

commit v6 on v5

--- a/solution.py
+++ b/solution.py
@@ -46,8 +46,15 @@
     return values_in * jax.nn.sigmoid(values_in)
 
 
-def tail(preact, out_weight):
-    return norm_rows(dot_nn(silu(preact).astype(BF16), out_weight))
+def centre(weight):
+    wide = weight.astype(F32)
+    return (wide - jnp.mean(wide, axis=-1, keepdims=True)).astype(BF16)
+
+
+def tail(preact, centred_weight):
+    centred = dot_nn(silu(preact).astype(BF16), centred_weight)
+    spread = jnp.mean(centred * centred, axis=-1, keepdims=True)
+    return centred * lax.rsqrt(spread + 1e-05)
 
 
 class Arriving:
@@ -241,7 +248,7 @@
     nodes, recv_w, out_w = arriving
     (both,) = leaving
     both.put(dot_nn(nodes(), recv_w()).astype(BF16))
-    both.put(out_w(), nodes.held.shape[0])
+    both.put(centre(out_w()), nodes.held.shape[0])
 
 
 def mesh_bring_body(arriving, leaving):
@@ -250,7 +257,8 @@
     halo_out.put(rows_equal(nodes.held.shape[0], halo()).T)
     nodes_out.put(nodes())
     node_pre_out.put(dot_nn(nodes(), node_w()).astype(BF16))
-    pair_w_out.put(pair_w())
+    pair_w_out.held[0] = pair_w.ref()[0]
+    pair_w_out.held[1] = centre(pair_w.ref()[1])
     sent_w_out.put(sent_w())
 
 
@@ -294,13 +302,15 @@
 
 
 def local_body(arriving, leaving):
-    one, sent_w, recv_w, ends, pre, node_w = arriving
-    pre_out, node_pre_out = leaving
+    one, sent_w, recv_w, ends, pre, node_w, edge_out_w, node_out_w = arriving
+    pre_out, node_pre_out, edge_centred, node_centred = leaving
     sent = dot_nn(one(), sent_w()).astype(BF16)
     recv = dot_nn(one(), recv_w()).astype(BF16)
     own = dot_nn(ends(), jnp.concatenate([sent, recv], axis=0))
     pre_out.put((pre().astype(F32) + own).astype(BF16))
     node_pre_out.put(dot_nn(one(), node_w()).astype(BF16))
+    edge_centred.put(centre(edge_out_w()))
+    node_centred.put(centre(node_out_w()))
 
 
 def edge_values(arriving):
@@ -310,9 +320,9 @@
 
 
 def node_values(total, arriving):
-    pair_w, node_pre, one = arriving
-    preact = node_pre().astype(F32) + dot_nn(total, pair_w.ref()[0])
-    return (one().astype(F32) + tail(preact, pair_w.ref()[1])).astype(BF16)
+    sum_w, node_pre, out_w, one = arriving
+    preact = node_pre().astype(F32) + dot_nn(total, sum_w())
+    return (one().astype(F32) + tail(preact, out_w())).astype(BF16)
 
 
 def edge_node_body(arriving, leaving):
@@ -459,16 +469,17 @@
         halo_box.reshape(peers, -1, width), "patch", split_axis=0, concat_axis=0, tiled=True
     ).reshape(halo_count, width)
     edge_whole = shape((edge_total, width))
-    edge_pre, node_pre = call(
+    edge_pre, node_pre, edge_centred, node_centred = call(
         local_body,
-        [edge_whole, node_like],
-        [mesh_one, sent_w, Far(proc_edge_w, 2), Far(ends), Far(edge_pre), Far(proc_node_w, 0)],
+        [edge_whole, node_like, matrix, matrix],
+        [mesh_one, sent_w, Far(proc_edge_w, 2), Far(ends), Far(edge_pre), Far(proc_node_w, 0)]
+        + [Far(proc_edge_w, 3), Far(proc_node_w, 2)],
         unit * 1500,
         far_outs=True,
         room=ROOM,
     )
-    edge_operands = [Far(far), Far(ghosts), Far(edge_pre), Far(proc_edge_w, 3), Far(edges), Far(edge_recv)]
-    node_operands = [Far(proc_node_w, 1, 2), Far(node_pre), Far(mesh_one)]
+    edge_operands = [Far(far), Far(ghosts), Far(edge_pre), Far(edge_centred), Far(edges), Far(edge_recv)]
+    node_operands = [Far(proc_node_w, 1), Far(node_pre), Far(node_centred), Far(mesh_one)]
     if paired:
         edge_out, mesh_two = call(
             edge_node_body,

time: 59.9 us -> 59.4 us (level)
  local copies, waits for them, and re-layouts: 5.52 us -> 7.84 us
  waiting for transfers between devices: 17.6 us -> 15.4 us
  Pallas kernels: 19.8 us -> 19.2 us
    unnamed x32 -> x38, local copies, waits for them, and re-layouts: 5.52 us -> 7.84 us
    all_to_all x1, waiting for transfers between devices: 4.84 us -> 2.75 us  [per_device(): lax.all_to_all(halo_box.reshape(peers, -1, width), 'patch', split_axis=0,...]
  transfers between devices with their start and end apart: 5 -> 5, of which waited for: 4 -> 4; matrix products, arithmetic and copies ran while one was open for 0% -> 0% of each run, Pallas kernels for 13% -> 15%
where the time goes in v6:
time: 59.4 us; the launch traced here: 58.9 us
  Pallas kernels  19.2 us (32%)
  starting transfers between devices  15.6 us (26%)
  waiting for transfers between devices  15.4 us (26%)
  local copies, waits for them, and re-layouts  7.84 us (13%)
  between operations  0.86 us (1%)
    pallas_call x8, Pallas kernels, call(): pl.pallas_call(kernel, in_specs=[away if is_far else here for is_far in f...  19.2 us
    unnamed x38, local copies, waits for them, and re-layouts  7.84 us
    all_to_all x1, starting transfers between devices, per_device(): lax.all_to_all(outbox, 'patch', split_axis=0, concat_axis=0, tiled=True)  7.4 us
    ppermute x1, waiting for transfers between devices, per_device(): names.append(lax.ppermute(own_names, 'band', other))  6.11 us
    all_to_all x1, waiting for transfers between devices, per_device(): lax.all_to_all(outbox, 'patch', split_axis=0, concat_axis=0, tiled=True)  5.32 us
    all_to_all x1, starting transfers between devices, per_device(): lax.all_to_all(halo_box.reshape(peers, -1, width), 'patch', split_axis=0,...  4.58 us
    all_to_all x1, waiting for transfers between devices, per_device(): lax.all_to_all(halo_box.reshape(peers, -1, width), 'patch', split_axis=0,...  2.75 us
    ppermute x1, starting transfers between devices, per_device(): edge_parts.append(lax.ppermute(own_edge, 'band', other))  1.56 us
  transfers between devices with their start and end apart: 5, of which 4 were waited for; matrix products, arithmetic and copies ran while one was open for 0% of the time, Pallas kernels for 15%

profile of v6, /device:TPU:0, one launch (start us, length us, event | category | flops | bytes accessed | tf_op | source)
XLA Modules:
  0.0 58.9 jit_solution(12327339663435106688)
XLA Ops:
  0.7 4.0 %shard_map.176 = bf16[16,136,128]{2,1,0:T(8,128)(2,1)} custom-call(bf16[474,512]{1,0:T(8,128)(2,1)} %refs_0_.2, bf16[512,512]{1,0:T(8,128)(2,1)} %refs_1_.2, bf16[3,512,512]{2,1,0:T(8,128)(2,1)} %refs_2_.5, bf16[474,256]{1,0:T(8,128)(2,1)} %bitcast.13, s32[1,384]{1,0:T(1,128)} %bitcast.16, s32[3,128]{1,0:T(4,128)} %bitcast.14, bf16[4,384]{1,0:T(4,128)(2,1)} %refs_6_.3, ...), custom_call_target="tpu_custom_call" | custom-call | flops 786432000 | bytes 1788416 | tf_op jit(solution)/shard_map/pallas_call | solution.py:152
  4.7 7.4 %all-to-all-start = ((bf16[16,136,128]{2,1,0:T(8,128)(2,1)}), bf16[16,136,128]{2,1,0:T(8,128)(2,1)S(1)}, u32[]{:S(2)}, u32[]{:S(2)}) async-start(bf16[16,136,128]{2,1,0:T(8,128)(2,1)} %shard_map.176), calls=%async_computation | async-start | bytes 1114112 | tf_op jit(solution)/shard_map/all_to_all | solution.py:405
  12.1 1.6 %collective-permute-start = (bf16[256,512]{1,0:T(8,128)(2,1)}, bf16[256,512]{1,0:T(8,128)(2,1)S(1)}, u32[]{:S(2)}, u32[]{:S(2)}) collective-permute-start(bf16[256,512]{1,0:T(8,128)(2,1)} %refs_0_.4), channel_id=1, source_target_pairs={{0,16},{16,0},{1,17},{17,1},{2,18},{18,2},{3,19},{19,3},{4,20},{20... | collective-permute-start | bytes 786440 | tf_op jit(solution)/shard_map/ppermute | solution.py:413
  13.7 0.5 collective-permute-start.1
  14.2 0.0 copy-done.4
  14.2 0.7 %shard_map.177.refs_1_ = bf16[832,512]{1,0:T(8,128)(2,1)S(1)} custom-call(bf16[320,512]{1,0:T(8,128)(2,1)S(1)} %copy-done.4, bf16[3,512,512]{2,1,0:T(8,128)(2,1)S(1)} %copy-done.2, bf16[3,512,512]{2,1,0:T(8,128)(2,1)S(1)} %copy-done.2), custom_call_target="tpu_custom_call" | custom-call | flops 167772160 | bytes 1376256 | tf_op jit(solution)/shard_map/pallas_call | solution.py:152
  15.0 0.0 copy-start.18
  15.0 6.1 %collective-permute-done.1.refs_4_ = s32[2,256]{1,0:T(2,128)S(1)} collective-permute-done((s32[2,256]{1,0:T(2,128)S(1)}, s32[2,256]{1,0:T(2,128)S(1)}, u32[]{:S(2)}, u32[]{:S(2)}) %collective-permute-start.1) | collective-permute-done | bytes 2080 | tf_op jit(solution)/shard_map/ppermute | solution.py:414
  21.1 0.0 collective-permute-done.refs_1_
  21.1 0.7 %copy-done.13 = bf16[256,512]{1,0:T(8,128)(2,1)} copy-done((bf16[256,512]{1,0:T(8,128)(2,1)}, bf16[256,512]{1,0:T(8,128)(2,1)S(1)}, u32[]{:S(2)}) %copy-start.13) | copy-done | bytes 262168
  21.8 5.3 %all-to-all-done.refs_0_ = bf16[16,136,128]{2,1,0:T(8,128)(2,1)S(1)} async-done(((bf16[16,136,128]{2,1,0:T(8,128)(2,1)}), bf16[16,136,128]{2,1,0:T(8,128)(2,1)S(1)}, u32[]{:S(2)}, u32[]{:S(2)}) %all-to-all-start) | async-done | bytes 557088 | tf_op jit(solution)/shard_map/all_to_all | solution.py:405
  27.1 1.2 %shard_map.178.refs_0_ = bf16[320,512]{1,0:T(8,128)(2,1)S(1)} custom-call(bf16[16,136,128]{2,1,0:T(8,128)(2,1)S(1)} %all-to-all-done.refs_0_, bf16[832,512]{1,0:T(8,128)(2,1)S(1)} %shard_map.177.refs_1_), custom_call_target="tpu_custom_call" | custom-call | flops 629145600 | bytes 1409024 | tf_op jit(solution)/shard_map/pallas_call | solution.py:152
  28.3 0.0 copy-start
  28.3 1.5 %collective-permute-start.2 = (bf16[320,512]{1,0:T(8,128)(2,1)S(1)}, bf16[320,512]{1,0:T(8,128)(2,1)S(1)}, u32[]{:S(2)}, u32[]{:S(2)}) collective-permute-start(bf16[320,512]{1,0:T(8,128)(2,1)S(1)} %shard_map.178.refs_0_), channel_id=1, source_target_pairs={{0,16},{16,0},{1,17},{17,1},{2,18},{18,2},{3,19},{19,3},{4,20},{20... | collective-permute-start | bytes 983048 | tf_op jit(solution)/shard_map/ppermute | solution.py:450
  29.9 1.4 %copy-done.3 = bf16[3,512,512]{2,1,0:T(8,128)(2,1)S(1)} copy-done((bf16[3,512,512]{2,1,0:T(8,128)(2,1)S(1)}, bf16[3,512,512]{2,1,0:T(8,128)(2,1)}, u32[]{:S(2)}) %copy-start.3) | copy-done | bytes 1572888
  31.3 1.5 %shard_map.180 = (bf16[320,512]{1,0:T(8,128)(2,1)S(1)}, bf16[256,320]{1,0:T(8,128)(2,1)S(1)}, bf16[320,512]{1,0:T(8,128)(2,1)S(1)}, bf16[2,512,512]{2,1,0:T(8,128)(2,1)S(1)}, bf16[512,512]{1,0:T(8,128)(2,1)S(1)}) custom-call(s32[1,256]{1,0:T(1,128)S(1)} %copy-done.18, bf16[320,512]{1,0:T(8,128)(2,1)S(1)} %copy-done.4, bf16[3,512,512]{2,1,0:T(8,128)(2,1)S(1)} %copy-done.3, ...), custom_call_target="tpu_custom_call" | custom-call | flops 167772160 | bytes 2425856 | tf_op jit(solution)/shard_map/pallas_call | solution.py:152
  32.8 3.2 %shard_map.179 = (bf16[512,512]{1,0:T(8,128)(2,1)S(1)}, bf16[512,512]{1,0:T(8,128)(2,1)S(1)}, bf16[512,640]{1,0:T(8,128)(2,1)S(1)}, bf16[512,256]{1,0:T(8,128)(2,1)S(1)}, s32[1,512]{1,0:T(1,128)S(1)}) custom-call(bf16[256,512]{1,0:T(8,128)(2,1)} %refs_0_.4, bf16[256,512]{1,0:T(8,128)(2,1)S(1)} %copy-done.14, s32[1,256]{1,0:T(1,128)S(1)} %bitcast.10, ...), custom_call_target="tpu_custom_call" | custom-call | flops 268435456 | bytes 1052672 | tf_op jit(solution)/shard_map/pallas_call | solution.py:152
  36.0 0.0 copy-start.7
  36.0 0.8 %copy-done.7 = bf16[512,512]{1,0:T(8,128)(2,1)} copy-done((bf16[512,512]{1,0:T(8,128)(2,1)}, bf16[512,512]{1,0:T(8,128)(2,1)S(1)}, u32[]{:S(2)}) %copy-start.7) | copy-done | bytes 524312
  36.8 1.2 %collective-permute-done.2.refs_1_ = bf16[320,512]{1,0:T(8,128)(2,1)S(1)} collective-permute-done((bf16[320,512]{1,0:T(8,128)(2,1)S(1)}, bf16[320,512]{1,0:T(8,128)(2,1)S(1)}, u32[]{:S(2)}, u32[]{:S(2)}) %collective-permute-start.2) | collective-permute-done | bytes 327712 | tf_op jit(solution)/shard_map/ppermute | solution.py:450
  38.0 1.3 %shard_map.181 = (bf16[320,512]{1,0:T(8,128)(2,1)S(1)}, bf16[256,512]{1,0:T(8,128)(2,1)S(1)}) custom-call(bf16[320,512]{1,0:T(8,128)(2,1)S(1)} %shard_map.178.refs_0_, bf16[320,512]{1,0:T(8,128)(2,1)S(1)} %collective-permute-done.2.refs_1_, bf16[320,512]{1,0:T(8,128)(2,1)S(1)} %get-tuple-element.43.refs_2_, bf16[320,512]{1,0:T(8,128)(2,1)S(1)} %get-tuple-element.46.refs_3_, ...), custom_call_target="tpu_custom_call" | custom-call | flops 524288000 | bytes 3047424 | tf_op jit(solution)/shard_map/pallas_call | solution.py:152
  39.4 0.0 copy-start.15
  39.4 0.7 %copy-done.15 = bf16[256,512]{1,0:T(8,128)(2,1)} copy-done((bf16[256,512]{1,0:T(8,128)(2,1)}, bf16[256,512]{1,0:T(8,128)(2,1)S(1)}, u32[]{:S(2)}) %copy-start.15) | copy-done | bytes 262168
  40.1 4.6 %all-to-all-start.1 = ((bf16[16,16,512]{2,1,0:T(8,128)(2,1)}), bf16[16,16,512]{2,1,0:T(8,128)(2,1)}, u32[]{:S(2)}, u32[]{:S(2)}) async-start(bf16[16,16,512]{2,1,0:T(8,128)(2,1)} %bitcast.8), calls=%async_computation.1 | async-start | bytes 524288 | tf_op jit(solution)/shard_map/all_to_all | solution.py:468
  44.7 1.0 %copy-done.8 = bf16[512,512]{1,0:T(8,128)(2,1)S(1)} copy-done((bf16[512,512]{1,0:T(8,128)(2,1)S(1)}, bf16[512,512]{1,0:T(8,128)(2,1)}, u32[]{:S(2)}) %copy-start.8) | copy-done | bytes 524312
  45.7 3.1 %shard_map.182 = (bf16[512,512]{1,0:T(8,128)(2,1)S(1)}, bf16[320,512]{1,0:T(8,128)(2,1)S(1)}, bf16[512,512]{1,0:T(8,128)(2,1)S(1)}, bf16[512,512]{1,0:T(8,128)(2,1)S(1)}) custom-call(bf16[320,512]{1,0:T(8,128)(2,1)S(1)} %get-tuple-element.51.refs_0_.refs_9_, bf16[512,512]{1,0:T(8,128)(2,1)S(1)} %get-tuple-element.49.refs_6_.refs_1_, ...), custom_call_target="tpu_custom_call" | custom-call | flops 786432000 | bytes 4128768 | tf_op jit(solution)/shard_map/pallas_call | solution.py:152
  48.8 0.8 %copy-done.9 = bf16[512,512]{1,0:T(8,128)(2,1)} copy-done((bf16[512,512]{1,0:T(8,128)(2,1)}, bf16[512,512]{1,0:T(8,128)(2,1)S(1)}, u32[]{:S(2)}) %copy-start.9) | copy-done | bytes 524312
  49.6 0.8 %copy-done.10 = bf16[512,512]{1,0:T(8,128)(2,1)} copy-done((bf16[512,512]{1,0:T(8,128)(2,1)}, bf16[512,512]{1,0:T(8,128)(2,1)S(1)}, u32[]{:S(2)}) %copy-start.10) | copy-done | bytes 524312
  50.5 0.8 %copy-done.11 = bf16[512,512]{1,0:T(8,128)(2,1)} copy-done((bf16[512,512]{1,0:T(8,128)(2,1)}, bf16[512,512]{1,0:T(8,128)(2,1)S(1)}, u32[]{:S(2)}) %copy-start.11) | copy-done | bytes 524312
  51.3 0.7 %copy-done.12 = bf16[320,512]{1,0:T(8,128)(2,1)} copy-done((bf16[320,512]{1,0:T(8,128)(2,1)}, bf16[320,512]{1,0:T(8,128)(2,1)S(1)}, u32[]{:S(2)}) %copy-start.12) | copy-done | bytes 327704
  52.0 2.7 %all-to-all-done.1 = bf16[16,16,512]{2,1,0:T(8,128)(2,1)} async-done(((bf16[16,16,512]{2,1,0:T(8,128)(2,1)}), bf16[16,16,512]{2,1,0:T(8,128)(2,1)}, u32[]{:S(2)}, u32[]{:S(2)}) %all-to-all-start.1) | async-done | bytes 262176 | tf_op jit(solution)/shard_map/all_to_all | solution.py:468
  54.7 4.2 %shard_map.183 = (bf16[256,512]{1,0:T(8,128)(2,1)}, bf16[320,512]{1,0:T(8,128)(2,1)}) custom-call(bf16[512,256]{1,0:T(8,128)(2,1)S(1)} %get-tuple-element.39.refs_0_, bf16[256,512]{1,0:T(8,128)(2,1)} %bitcast.7.refs_1_, bf16[512,512]{1,0:T(8,128)(2,1)} %copy-done.9, bf16[512,512]{1,0:T(8,128)(2,1)} %copy-done.10, bf16[512,512]{1,0:T(8,128)(2,1)} %copy-done.6, ...), custom_call_target="tpu_custom_call" | custom-call | flops 786432000 | bytes 3803136 | tf_op jit(solution)/shard_map/pallas_call | solution.py:152
  (25 shorter events, 0.1 us)
Async XLA Ops:
  0.6 11.5 %copy-start.16 = (s32[256]{0:T(256)S(1)}, s32[256]{0:T(256)}, u32[]{:S(2)}) copy-start(s32[256]{0:T(256)} %param.24) | copy-start | bytes 3076
  0.6 11.5 %copy-start.17 = (s32[256]{0:T(256)S(1)}, s32[256]{0:T(256)}, u32[]{:S(2)}) copy-start(s32[256]{0:T(256)} %param.25) | copy-start | bytes 3076
  0.7 13.6 %copy-start.2 = (bf16[3,512,512]{2,1,0:T(8,128)(2,1)S(1)}, bf16[3,512,512]{2,1,0:T(8,128)(2,1)}, u32[]{:S(2)}) copy-start(bf16[3,512,512]{2,1,0:T(8,128)(2,1)} %refs_2_.5) | copy-start | bytes 4718596
  0.7 13.6 %copy-start.4 = (bf16[320,512]{1,0:T(8,128)(2,1)S(1)}, bf16[320,512]{1,0:T(8,128)(2,1)}, u32[]{:S(2)}) copy-start(bf16[320,512]{1,0:T(8,128)(2,1)} %refs_1_.4) | copy-start | bytes 983044
  4.7 22.4 %all-to-all-start = ((bf16[16,136,128]{2,1,0:T(8,128)(2,1)}), bf16[16,136,128]{2,1,0:T(8,128)(2,1)S(1)}, u32[]{:S(2)}, u32[]{:S(2)}) async-start(bf16[16,136,128]{2,1,0:T(8,128)(2,1)} %shard_map.176), calls=%async_computation | async-start | bytes 1114112 | tf_op jit(solution)/shard_map/all_to_all | solution.py:405
  12.1 9.0 %collective-permute-start = (bf16[256,512]{1,0:T(8,128)(2,1)}, bf16[256,512]{1,0:T(8,128)(2,1)S(1)}, u32[]{:S(2)}, u32[]{:S(2)}) collective-permute-start(bf16[256,512]{1,0:T(8,128)(2,1)} %refs_0_.4), channel_id=1, source_target_pairs={{0,16},{16,0},{1,17},{17,1},{2,18},{18,2},{3,19},{19,3},{4,20},{20... | collective-permute-start | bytes 786440 | tf_op jit(solution)/shard_map/ppermute | solution.py:413
  13.7 7.4 %collective-permute-start.1 = (s32[2,256]{1,0:T(2,128)S(1)}, s32[2,256]{1,0:T(2,128)S(1)}, u32[]{:S(2)}, u32[]{:S(2)}) collective-permute-start(s32[2,256]{1,0:T(2,128)S(1)} %pad_add_fusion), channel_id=1, source_target_pairs={{0,16},{16,0},{1,17},{17,1},{2,18},{18,2},{3,19},{19,3},{4,20},{20... | collective-permute-start | bytes 6152 | tf_op jit(solution)/shard_map/ppermute | solution.py:414
  15.0 14.9 %copy-start.18 = (s32[1,256]{1,0:T(1,128)S(1)}, s32[1,256]{1,0:T(1,128)}, u32[]{:S(2)}) copy-start(s32[1,256]{1,0:T(1,128)} %refs_0_.5) | copy-start | bytes 3076
  21.1 0.7 %copy-start.13 = (bf16[256,512]{1,0:T(8,128)(2,1)}, bf16[256,512]{1,0:T(8,128)(2,1)S(1)}, u32[]{:S(2)}) copy-start(bf16[256,512]{1,0:T(8,128)(2,1)S(1)} %collective-permute-done.refs_1_) | copy-start | bytes 786436
  28.3 4.5 %copy-start = (bf16[4,512,512]{2,1,0:T(8,128)(2,1)S(1)}, bf16[4,512,512]{2,1,0:T(8,128)(2,1)}, u32[]{:S(2)}) copy-start(bf16[4,512,512]{2,1,0:T(8,128)(2,1)} %refs_6_.4) | copy-start | bytes 6291460
  28.3 9.7 %collective-permute-start.2 = (bf16[320,512]{1,0:T(8,128)(2,1)S(1)}, bf16[320,512]{1,0:T(8,128)(2,1)S(1)}, u32[]{:S(2)}, u32[]{:S(2)}) collective-permute-start(bf16[320,512]{1,0:T(8,128)(2,1)S(1)} %shard_map.178.refs_0_), channel_id=1, source_target_pairs={{0,16},{16,0},{1,17},{17,1},{2,18},{18,2},{3,19},{19,3},{4,20},{20... | collective-permute-start | bytes 983048 | tf_op jit(solution)/shard_map/ppermute | solution.py:450
  29.9 1.4 %copy-start.3 = (bf16[3,512,512]{2,1,0:T(8,128)(2,1)S(1)}, bf16[3,512,512]{2,1,0:T(8,128)(2,1)}, u32[]{:S(2)}) copy-start(bf16[3,512,512]{2,1,0:T(8,128)(2,1)} %refs_3_.1) | copy-start | bytes 4718596
  31.3 1.5 %copy-start.14 = (bf16[256,512]{1,0:T(8,128)(2,1)S(1)}, bf16[256,512]{1,0:T(8,128)(2,1)}, u32[]{:S(2)}) copy-start(bf16[256,512]{1,0:T(8,128)(2,1)} %copy-done.13) | copy-start | bytes 786436
  36.0 0.8 %copy-start.7 = (bf16[512,512]{1,0:T(8,128)(2,1)}, bf16[512,512]{1,0:T(8,128)(2,1)S(1)}, u32[]{:S(2)}) copy-start(bf16[512,512]{1,0:T(8,128)(2,1)S(1)} %get-tuple-element.53.refs_4_) | copy-start | bytes 1572868
  36.8 2.5 %copy-start.6 = (bf16[512,512]{1,0:T(8,128)(2,1)}, bf16[512,512]{1,0:T(8,128)(2,1)S(1)}, u32[]{:S(2)}) copy-start(bf16[512,512]{1,0:T(8,128)(2,1)S(1)} %get-tuple-element.56.refs_4_) | copy-start | bytes 1572868
  38.0 6.6 %copy-start.1 = (bf16[3,512,512]{2,1,0:T(8,128)(2,1)S(1)}, bf16[3,512,512]{2,1,0:T(8,128)(2,1)}, u32[]{:S(2)}) copy-start(bf16[3,512,512]{2,1,0:T(8,128)(2,1)} %refs_6_.5) | copy-start | bytes 4718596
  39.4 0.7 %copy-start.15 = (bf16[256,512]{1,0:T(8,128)(2,1)}, bf16[256,512]{1,0:T(8,128)(2,1)S(1)}, u32[]{:S(2)}) copy-start(bf16[256,512]{1,0:T(8,128)(2,1)S(1)} %get-tuple-element.50) | copy-start | bytes 786436
  40.1 8.8 %copy-start.5 = (bf16[320,512]{1,0:T(8,128)(2,1)}, bf16[320,512]{1,0:T(8,128)(2,1)S(1)}, u32[]{:S(2)}) copy-start(bf16[320,512]{1,0:T(8,128)(2,1)S(1)} %get-tuple-element.51.refs_0_.refs_9_) | copy-start | bytes 983044
  40.1 14.7 %all-to-all-start.1 = ((bf16[16,16,512]{2,1,0:T(8,128)(2,1)}), bf16[16,16,512]{2,1,0:T(8,128)(2,1)}, u32[]{:S(2)}, u32[]{:S(2)}) async-start(bf16[16,16,512]{2,1,0:T(8,128)(2,1)} %bitcast.8), calls=%async_computation.1 | async-start | bytes 524288 | tf_op jit(solution)/shard_map/all_to_all | solution.py:468
  44.7 1.0 %copy-start.8 = (bf16[512,512]{1,0:T(8,128)(2,1)S(1)}, bf16[512,512]{1,0:T(8,128)(2,1)}, u32[]{:S(2)}) copy-start(bf16[512,512]{1,0:T(8,128)(2,1)} %copy-done.7) | copy-start | bytes 1572868
  48.8 0.8 %copy-start.9 = (bf16[512,512]{1,0:T(8,128)(2,1)}, bf16[512,512]{1,0:T(8,128)(2,1)S(1)}, u32[]{:S(2)}) copy-start(bf16[512,512]{1,0:T(8,128)(2,1)S(1)} %get-tuple-element.54.refs_2_) | copy-start | bytes 1572868
  49.6 0.8 %copy-start.10 = (bf16[512,512]{1,0:T(8,128)(2,1)}, bf16[512,512]{1,0:T(8,128)(2,1)S(1)}, u32[]{:S(2)}) copy-start(bf16[512,512]{1,0:T(8,128)(2,1)S(1)} %get-tuple-element.55.refs_3_) | copy-start | bytes 1572868
  50.5 0.8 %copy-start.11 = (bf16[512,512]{1,0:T(8,128)(2,1)}, bf16[512,512]{1,0:T(8,128)(2,1)S(1)}, u32[]{:S(2)}) copy-start(bf16[512,512]{1,0:T(8,128)(2,1)S(1)} %get-tuple-element.59.refs_8_) | copy-start | bytes 1572868
  51.3 0.7 %copy-start.12 = (bf16[320,512]{1,0:T(8,128)(2,1)}, bf16[320,512]{1,0:T(8,128)(2,1)S(1)}, u32[]{:S(2)}) copy-start(bf16[320,512]{1,0:T(8,128)(2,1)S(1)} %get-tuple-element.58.refs_7_) | copy-start | bytes 983044
